TPU v7x, 32 devices: a whole 2x2x4 slice. The times are simulated.
32 devices in a mesh: mem: 4 (over x, core), slab: 8 (over z, y).
Axes of the slice: x: 2, y: 2, z: 4, core: 2. Of those that a mesh axis runs over, the one named last changes fastest.
Arguments:
- prior_sample_group: bfloat16 [64, 32, 16, 1024], P('mem', None, 'slab'), may hold values from -6 to 6
- coefficients: float32 [3, 32, 16, 1024], P(None, None, 'slab'), may hold values from -0.3 to 0.3, as said below
- measured_quantity: float32 [32768], P('slab'), may hold values from -6 to 6
- measurement_precision: float32 [32768], P('slab'), may hold values from 0.5 to 4
- measurement_location: int32 [32768], P('slab'), may hold values from 0 to 65535
- obs_lists: int32 [16, 512, 128], P('slab', 'mem'), may hold values from 0 to 12287
- obs_counts: int32 [16, 512], P('slab', 'mem'), may hold values from 16 to 128, as said below
- loc_weight: float32 [16, 512, 128], P('slab', 'mem'), may hold values from 0.05 to 1
Outputs:
- analysis: bfloat16 [64, 32, 16, 1024], P(None, None, 'slab', 'mem')
Inputs may be any that keep to these rules, and one draw needn't show every extreme that they name: `coefficients`: the third dimension's component 0 and 1 lie in [-0.3, 0.3], component 2 in [0.03, 0.15]. `measurement_location`: flattened index, level first, into the 32 x 2 x 1024 cells of the slab that holds the observation (observation o lies in slab o // 4096). `obs_lists`: an entry of a patch in row r indexes the observations of slabs r // 2 - 1, r // 2, r // 2 + 1 laid end to end, 4096 each; slots from obs_counts on are unused. `obs_counts`: in every block of patches held by one device some patch uses all 128 slots.
All inputs are finite; a program needn't handle non-finite values. Where the computation divides by a largest or mean magnitude, that divisor is 1e-20 or more.
Results may differ from a plain program's by a relative error of at most 0.0051.
Values may be sent and summed in bfloat16 or wider, within the bound.
No kernel may reach another device: no remote copies, remote signals or barrier semaphores. Data moves between devices by JAX's collectives and lax.ppermute only.
A program may use at most 128 MiB of HBM per device.

v0:
```python
import math

import jax
import jax.numpy as jnp
from jax import lax
from jax.sharding import PartitionSpec as P

NS_ITERS = 4


INFL = 1.1
HIGH = lax.Precision.HIGHEST


def with_halo(cells, sides, width):
    for axis, dim in sides:
        count = lax.axis_size(axis)
        ends = count - 1
        head = lax.slice_in_dim(cells, 0, width, axis=dim)
        tail = lax.slice_in_dim(cells, cells.shape[dim] - width, cells.shape[dim], axis=dim)
        cells = jnp.concatenate(
            [
                lax.ppermute(tail, axis, [(i, (i + 1) % count) for i in range(ends)]),
                cells,
                lax.ppermute(head, axis, [((i + 1) % count, i) for i in range(ends)]),
            ],
            axis=dim,
        )
    return cells


def stencil(padded, coeffs):
    center = padded[..., 1:-1, :]
    upper_row = padded[..., 2:, :]
    lower_row = padded[..., :-2, :]
    toward_east = jnp.roll(center, -1, axis=-1)
    toward_west = jnp.roll(center, 1, axis=-1)
    advect = coeffs[0] * (upper_row - lower_row) + coeffs[1] * (toward_east - toward_west)
    laplace = upper_row + lower_row + toward_east + toward_west - 4.0 * center
    return center - 0.5 * advect + coeffs[2] * laplace


def analyse(fields_row, picked, counts_row, weights_row):
    members = fields_row.shape[0]
    ensemble = picked[..., :members]
    observed = picked[..., members]
    inverse_var = picked[..., members + 1]
    position = lax.broadcasted_iota(jnp.int32, weights_row.shape, 1)
    weight = jnp.where(position < counts_row[:, None], weights_row * inverse_var, 0.0)
    obs_mean = jnp.mean(ensemble, axis=-1)
    anomaly = ensemble - obs_mean[..., None]
    innovation = observed - obs_mean
    weighted = anomaly * weight[..., None]
    gram = jnp.einsum("plk,plm->pkm", weighted, anomaly, precision=HIGH)
    forcing = jnp.einsum("plk,pl->pk", weighted, innovation, precision=HIGH)
    inflated = (members - 1) / INFL
    ident = jnp.eye(members, dtype=jnp.float32)
    gershgorin = inflated + jnp.max(jnp.sum(jnp.abs(gram), axis=-1), axis=-1)
    square = (inflated * ident + gram) / gershgorin[:, None, None]
    inverse = jnp.broadcast_to(ident, gram.shape)
    for sweep in range(NS_ITERS):
        factor = 1.5 * ident - 0.5 * jnp.einsum("pij,pjk->pik", inverse, square, precision=HIGH)
        square = jnp.einsum("pij,pjk->pik", square, factor, precision=HIGH)
        inverse = jnp.einsum("pij,pjk->pik", factor, inverse, precision=HIGH)
    inv_root = inverse / jnp.sqrt(gershgorin)[:, None, None]
    posterior = jnp.einsum("pij,pjk->pik", inv_root, inv_root, precision=HIGH)
    mean_shift = jnp.einsum("pjk,pk->pj", posterior, forcing, precision=HIGH)
    transform = math.sqrt(members - 1.0) * inv_root + mean_shift[:, :, None]
    state_row = fields_row.astype(jnp.float32)
    center = jnp.mean(state_row, axis=0)
    deviation = state_row - center
    patches = transform.shape[0]
    levels = state_row.shape[1]
    blocks = deviation.reshape(members, levels, patches, -1)
    update = jnp.einsum("kzpc,pkm->mzpc", blocks, transform, precision=HIGH)
    return (center + update.reshape(members, levels, -1)).astype(jnp.bfloat16)


def on_device(
    prior_sample_group,
    coefficients,
    measured_quantity,
    measurement_precision,
    measurement_location,
    obs_lists,
    obs_counts,
    loc_weight,
):
    padded = with_halo(prior_sample_group, (("slab", 2),), 1).astype(jnp.float32)
    field = stencil(padded, coefficients)
    padded = with_halo(field, (("slab", 2),), 1)
    field = stencil(padded, coefficients)
    local_count = field.shape[0]
    raveled_model_vector = field.reshape(local_count, -1)
    predicted_measurements = jnp.take(raveled_model_vector, measurement_location, axis=1)
    shipped = field.astype(jnp.bfloat16)
    patches = lax.all_to_all(shipped, "mem", split_axis=3, concat_axis=0, tiled=True)
    obs_count = measured_quantity.shape[0]
    extras = jnp.stack([measured_quantity, measurement_precision], 0)
    piled_realizations = lax.all_gather(
        predicted_measurements.astype(jnp.bfloat16), "mem", axis=0, tiled=True
    ).astype(predicted_measurements.dtype)
    window = with_halo(jnp.concatenate([piled_realizations, extras], 0), (("slab", 1),), obs_count)
    measurement_catalog = window.T
    row_total = patches.shape[2]

    def analyse_row(row_index):
        fields_row = lax.dynamic_index_in_dim(patches, row_index, 2, keepdims=False)
        lists_row = lax.dynamic_index_in_dim(obs_lists, row_index, 0, keepdims=False)
        counts_row = lax.dynamic_index_in_dim(obs_counts, row_index, 0, keepdims=False)
        weights_row = lax.dynamic_index_in_dim(loc_weight, row_index, 0, keepdims=False)
        picked = jnp.take(measurement_catalog, lists_row, axis=0)
        return analyse(fields_row, picked, counts_row, weights_row)

    result = lax.map(analyse_row, jnp.arange(row_total, dtype=jnp.int32))
    return jnp.transpose(result, (1, 2, 0, 3))


def solution(mesh):
    return jax.shard_map(
        on_device,
        mesh=mesh,
        in_specs=(
            P("mem", None, "slab", None),
            P(None, None, "slab", None),
            P("slab"),
            P("slab"),
            P("slab"),
            P("slab", "mem", None),
            P("slab", "mem"),
            P("slab", "mem", None),
        ),
        out_specs=P(None, None, "slab", "mem"),
        check_vma=False,
    )
```

profile of v0, /device:TPU:9, one launch (start us, length us, event | category | flops | bytes accessed | tf_op | source)
XLA Modules:
  0.0 741.4 jit_solution(11417089235269392964)
XLA Ops:
  9.2 40.9 %collective-permute-done = bf16[16,32,1,1024]{3,1,2,0:T(8,128)(2,1)S(1)} collective-permute-done((bf16[16,32,1,1024]{3,1,2,0:T(8,128)(2,1)S(1)}, bf16[16,32,1,1024]{3,1,2,0:T(8,128)(2,1)S(1)}, u32[]{:S(2)}, u32[]{:S(2)}) %collective-permute-start) | collective-permute-done | bytes 1048608 | tf_op jit(solution)/shard_map/ppermute | solution.py:23
  68.1 86.3 %collective-permute-done.2 = f32[16,32,1,1024]{3,1,2,0:T(8,128)S(1)} collective-permute-done((f32[16,32,1,1024]{3,1,2,0:T(8,128)}, f32[16,32,1,1024]{3,1,2,0:T(8,128)S(1)}, u32[]{:S(2)}, u32[]{:S(2)}) %collective-permute-start.2) | collective-permute-done | bytes 2097184 | tf_op jit(solution)/shard_map/ppermute | solution.py:25
  157.9 11.5 %copy.111 = bf16[16,32,2,1024]{0,3,2,1:T(8,128)(2,1)} copy(bf16[16,32,2,1024]{3,1,2,0:T(8,128)(2,1)S(1)} %multiply_add_fusion) | data formatting | bytes 4194304 | tf_op jit(solution)/shard_map/add | solution.py:40
  169.3 22.3 %gather_fusion.1 = bf16[4096,16]{1,0:T(8,128)(2,1)} fusion(bf16[16,65536]{0,1:T(8,128)(2,1)} %bitcast.149, s32[4096]{0:T(1024)S(1)} %fusion.65), kind=kCustom, calls=%fused_computation.1 | custom fusion | bytes 278528 | tf_op jit(solution)/shard_map/jit(_take)/gather | solution.py:95
  195.3 8.3 %all_gather.3 = bf16[64,4096]{1,0:T(8,128)(2,1)S(1)} all-gather(bf16[16,4096]{1,0:T(8,128)(2,1)S(1)} %copy.112), channel_id=1, replica_groups=mesh['mem'=4,'slab'=8] {'mem'}, dimensions={0}, use_global_device_ids=true | all-gather | bytes 655360 | tf_op jit(solution)/shard_map/all_gather | solution.py:100
  211.0 12.2 %copy.108 = bf16[16,32,2,1024]{1,0,2,3:T(8,128)(2,1)} copy(bf16[16,32,2,1024]{3,1,2,0:T(8,128)(2,1)S(1)} %multiply_add_fusion) | data formatting | bytes 4194304 | tf_op jit(solution)/shard_map/convert_element_type | solution.py:96
  223.1 10.6 %reshape.153 = bf16[4,2,131072]{2,1,0:T(2,128)(2,1)} reshape(bf16[1024,2,16,32]{3,2,1,0:T(8,128)(2,1)} %bitcast.145) | data formatting | bytes 4194304
  238.8 19.4 %collective-permute-done.4 = f32[66,4096]{1,0:T(8,128)} collective-permute-done((f32[66,4096]{1,0:T(8,128)S(1)}, f32[66,4096]{1,0:T(8,128)}, u32[]{:S(2)}, u32[]{:S(2)}) %collective-permute-start.4) | collective-permute-done | bytes 1081376 | tf_op jit(solution)/shard_map/ppermute | solution.py:23
  267.3 7.4 reshape.154
  274.6 9.4 %copy.123 = bf16[16,32,2,4,256]{4,3,1,2,0:T(4,128)(2,1)S(1)} copy(bf16[16,32,2,4,256]{1,0,2,4,3:T(8,128)(2,1)} %bitcast.146) | data formatting | bytes 4194304 | tf_op jit(solution)/shard_map/all_to_all | solution.py:97
  285.8 454.2 %while.10 = (s32[]{:T(128)}, bf16[2,64,32,256]{3,0,2,1:T(2,128)(2,1)}, s32[2]{0:T(128)S(1)}, bf16[64,32,2,256]{3,1,2,0:T(8,128)(2,1)}, s32[2,128,128]{2,1,0:T(8,...) while((s32[]{:T(128)}, ...), condition=%wide.region_5.6_spmd, body=%wide.region_0.5_spmd.sunk | while | flops 6081503232 | bytes 161256720 | solution.py:115
  288.8 57.2 %gather_fusion = f32[16384,66]{1,0:T(8,128)} fusion(f32[12288,66]{1,0:T(8,128)} %get-tuple-element.229, s32[16384]{0:T(1024)S(1)} %fusion.160), kind=kCustom, calls=%fused_computation.clone.1 | custom fusion | bytes 8716288 | tf_op jit(solution)/shard_map/while/body/eval_jaxpr/jit(_take)/gather | solution.py:112
  346.0 8.2 %copy.134 = f32[128,128,66]{1,2,0:T(8,128)} copy(f32[128,128,66]{2,1,0:T(8,128)} %bitcast.142) | data formatting | bytes 8650752 | tf_op jit(solution)/shard_map/while/body/eval_jaxpr/jit(_take)/gather | solution.py:112
  364.6 8.3 %abs_reduce_fusion.2 = (f32[128,64]{1,0:T(8,128)S(1)}, f32[128,64,64]{1,2,0:T(8,128)}) fusion(f32[128,128,66]{1,2,0:T(8,128)S(1)} %broadcast_select_fusion.2, f32[128,128]{1,0:T(8,128)S(1)} %get-tuple-element.193, f32[128,128]{1,0:T(8,128)S(1)} %bitcast.151), kind=kOutput, calls=%fused_computation.19.clone.1 | convolution fusion | flops 809492480 | bytes 10715136 | tf_op jit(solution)/shard_map/while/body/eval_jaxpr/plk,plm->pkm/dot_general | solution.py:54
  373.2 10.1 %fusion.166 = f32[128,64,64]{2,1,0:T(8,128)} fusion(f32[64,64]{1,0:T(8,128)S(1)} %copy.135, f32[128,64,64]{1,2,0:T(8,128)} %get-tuple-element.197, f32[128]{0:T(128)S(1)} %get-tuple-element.198, f32[64,64]{0,1:T(8,128)S(1)} %fusion.165), kind=kOutput, calls=%fused_computation.46.clone.1 | convolution fusion | flops 403701760 | bytes 4227584 | tf_op jit(solution)/shard_map/while/body/eval_jaxpr/pij,pjk->pik/dot_general | solution.py:62
  383.4 10.4 %fusion.169 = f32[128,64,64]{2,1,0:T(8,128)S(1)} fusion(f32[128,64,64]{2,1,0:T(8,128)} %fusion.166, f32[64,64]{1,0:T(8,128)S(1)} %copy.136, f32[128,64,64]{1,2,0:T(8,128)} %get-tuple-element.197, f32[128]{0:T(128)S(1)} %get-tuple-element.198, f32[64,64]{0,1:T(8,128)S(1)} %fusion.165), kind=kOutput, calls=%fused_computation.23.clone.1 | convolution fusion | flops 404750336 | bytes 6324736 | tf_op jit(solution)/shard_map/while/body/eval_jaxpr/pij,pjk->pik/dot_general | solution.py:63
  460.7 6.9 fusion.180
  474.1 38.5 %dynamic_update_slice.5 = bf16[2,64,32,256]{3,0,2,1:T(2,128)(2,1)} dynamic-update-slice(bf16[2,64,32,256]{3,0,2,1:T(2,128)(2,1)} %get-tuple-element.213, bf16[1,64,32,256]{3,0,2,1:T(2,128)(2,1)} %copy.137, s32[]{:T(128)} %get-tuple-element.212, s32[]{:T(128)} %constant.75.clone.1..sunk, s32[]{:T(128)} %constant.75.clone.1..sunk, s32[]{:T(128)} %constant.75.clone.1..sunk) | dynamic-update-slice | bytes 2097156 | tf_op jit(solution)/shard_map/while/body/jit(dynamic_update_index_in_dim)/dynamic_update_slice | solution.py:115
  515.4 57.2 %gather_fusion = f32[16384,66]{1,0:T(8,128)} fusion(f32[12288,66]{1,0:T(8,128)} %get-tuple-element.229, s32[16384]{0:T(1024)S(1)} %fusion.160), kind=kCustom, calls=%fused_computation.clone.1 | custom fusion | bytes 8716288 | tf_op jit(solution)/shard_map/while/body/eval_jaxpr/jit(_take)/gather | solution.py:112
  572.5 8.2 %copy.134 = f32[128,128,66]{1,2,0:T(8,128)} copy(f32[128,128,66]{2,1,0:T(8,128)} %bitcast.142) | data formatting | bytes 8650752 | tf_op jit(solution)/shard_map/while/body/eval_jaxpr/jit(_take)/gather | solution.py:112
  591.2 8.3 %abs_reduce_fusion.2 = (f32[128,64]{1,0:T(8,128)S(1)}, f32[128,64,64]{1,2,0:T(8,128)}) fusion(f32[128,128,66]{1,2,0:T(8,128)S(1)} %broadcast_select_fusion.2, f32[128,128]{1,0:T(8,128)S(1)} %get-tuple-element.193, f32[128,128]{1,0:T(8,128)S(1)} %bitcast.151), kind=kOutput, calls=%fused_computation.19.clone.1 | convolution fusion | flops 809492480 | bytes 10715136 | tf_op jit(solution)/shard_map/while/body/eval_jaxpr/plk,plm->pkm/dot_general | solution.py:54
  599.8 10.3 %fusion.166 = f32[128,64,64]{2,1,0:T(8,128)} fusion(f32[64,64]{1,0:T(8,128)S(1)} %copy.135, f32[128,64,64]{1,2,0:T(8,128)} %get-tuple-element.197, f32[128]{0:T(128)S(1)} %get-tuple-element.198, f32[64,64]{0,1:T(8,128)S(1)} %fusion.165), kind=kOutput, calls=%fused_computation.46.clone.1 | convolution fusion | flops 403701760 | bytes 4227584 | tf_op jit(solution)/shard_map/while/body/eval_jaxpr/pij,pjk->pik/dot_general | solution.py:62
  610.2 10.4 %fusion.169 = f32[128,64,64]{2,1,0:T(8,128)S(1)} fusion(f32[128,64,64]{2,1,0:T(8,128)} %fusion.166, f32[64,64]{1,0:T(8,128)S(1)} %copy.136, f32[128,64,64]{1,2,0:T(8,128)} %get-tuple-element.197, f32[128]{0:T(128)S(1)} %get-tuple-element.198, f32[64,64]{0,1:T(8,128)S(1)} %fusion.165), kind=kOutput, calls=%fused_computation.23.clone.1 | convolution fusion | flops 404750336 | bytes 6324736 | tf_op jit(solution)/shard_map/while/body/eval_jaxpr/pij,pjk->pik/dot_general | solution.py:63
  700.7 38.5 %dynamic_update_slice.5 = bf16[2,64,32,256]{3,0,2,1:T(2,128)(2,1)} dynamic-update-slice(bf16[2,64,32,256]{3,0,2,1:T(2,128)(2,1)} %get-tuple-element.213, bf16[1,64,32,256]{3,0,2,1:T(2,128)(2,1)} %copy.137, s32[]{:T(128)} %get-tuple-element.212, s32[]{:T(128)} %constant.75.clone.1..sunk, s32[]{:T(128)} %constant.75.clone.1..sunk, s32[]{:T(128)} %constant.75.clone.1..sunk) | dynamic-update-slice | bytes 2097156 | tf_op jit(solution)/shard_map/while/body/jit(dynamic_update_index_in_dim)/dynamic_update_slice | solution.py:115
  (133 shorter events, 233.3 us)
Async XLA Ops:
  0.0 8.8 %copy-start.6 = (f32[3,32,2,1024]{3,2,1,0:T(2,128)S(1)}, f32[3,32,2,1024]{3,2,1,0:T(2,128)}, u32[]{:S(2)}) copy-start(f32[3,32,2,1024]{3,2,1,0:T(2,128)} %param.11) | copy-start | bytes 2359300
  2.6 47.4 %collective-permute-start = (bf16[16,32,1,1024]{3,1,2,0:T(8,128)(2,1)S(1)}, bf16[16,32,1,1024]{3,1,2,0:T(8,128)(2,1)S(1)}, u32[]{:S(2)}, u32[]{:S(2)}) collective-permute-start(bf16[16,32,1,1024]{3,1,2,0:T(8,128)(2,1)S(1)} %get-tuple-element.130), channel_id=1, source_target_pairs={{0,1},{1,2},{2,3},{3,4},{4,5},{5,6},{6,7},{8,9},{9,10},{10,11},{11... | collective-permute-start | bytes 3145736 | tf_op jit(solution)/shard_map/ppermute | solution.py:23
  5.8 47.2 %collective-permute-start.1 = (bf16[16,32,1,1024]{3,1,2,0:T(8,128)(2,1)S(1)}, bf16[16,32,1,1024]{3,1,2,0:T(8,128)(2,1)S(1)}, u32[]{:S(2)}, u32[]{:S(2)}) collective-permute-start(bf16[16,32,1,1024]{3,1,2,0:T(8,128)(2,1)S(1)} %get-tuple-element.131), channel_id=1, source_target_pairs={{1,0},{2,1},{3,2},{4,3},{5,4},{6,5},{7,6},{9,8},{10,9},{11,10},{12... | collective-permute-start | bytes 3145736 | tf_op jit(solution)/shard_map/ppermute | solution.py:25
  58.9 7.3 copy-start.9
  60.7 93.7 %collective-permute-start.2 = (f32[16,32,1,1024]{3,1,2,0:T(8,128)}, f32[16,32,1,1024]{3,1,2,0:T(8,128)S(1)}, u32[]{:S(2)}, u32[]{:S(2)}) collective-permute-start(f32[16,32,1,1024]{3,1,2,0:T(8,128)} %get-tuple-element.123), channel_id=1, source_target_pairs={{1,0},{2,1},{3,2},{4,3},{5,4},{6,5},{7,6},{9,8},{10,9},{11,10},{12... | collective-permute-start | bytes 6291464 | tf_op jit(solution)/shard_map/ppermute | solution.py:25
  62.6 91.8 %collective-permute-start.3 = (f32[16,32,1,1024]{3,1,2,0:T(8,128)S(1)}, f32[16,32,1,1024]{3,1,2,0:T(8,128)S(1)}, u32[]{:S(2)}, u32[]{:S(2)}) collective-permute-start(f32[16,32,1,1024]{3,1,2,0:T(8,128)S(1)} %get-tuple-element.122), channel_id=1, source_target_pairs={{0,1},{1,2},{2,3},{3,4},{4,5},{5,6},{6,7},{8,9},{9,10},{10,11},{11... | collective-permute-start | bytes 6291464 | tf_op jit(solution)/shard_map/ppermute | solution.py:23
  169.3 35.4 %copy-start.7 = (f32[4096]{0:T(1024)S(1)}, f32[4096]{0:T(1024)}, u32[]{:S(2)}) copy-start(f32[4096]{0:T(1024)} %param.13) | copy-start | bytes 49156
  169.3 35.4 %copy-start.8 = (f32[4096]{0:T(1024)S(1)}, f32[4096]{0:T(1024)}, u32[]{:S(2)}) copy-start(f32[4096]{0:T(1024)} %param.12) | copy-start | bytes 49156
  203.7 1.0 copy-start.3
  204.8 53.4 %collective-permute-start.4 = (f32[66,4096]{1,0:T(8,128)S(1)}, f32[66,4096]{1,0:T(8,128)}, u32[]{:S(2)}, u32[]{:S(2)}) collective-permute-start(f32[66,4096]{1,0:T(8,128)S(1)} %pad_maximum_fusion.6), channel_id=1, source_target_pairs={{0,1},{1,2},{2,3},{3,4},{4,5},{5,6},{6,7},{8,9},{9,10},{10,11},{11... | collective-permute-start | bytes 3244040 | tf_op jit(solution)/shard_map/ppermute | solution.py:23
  207.7 53.1 %collective-permute-start.5 = (f32[66,4096]{1,0:T(8,128)S(1)}, f32[66,4096]{1,0:T(8,128)}, u32[]{:S(2)}, u32[]{:S(2)}) collective-permute-start(f32[66,4096]{1,0:T(8,128)S(1)} %pad_maximum_fusion.6), channel_id=1, source_target_pairs={{1,0},{2,1},{3,2},{4,3},{5,4},{6,5},{7,6},{9,8},{10,9},{11,10},{12... | collective-permute-start | bytes 3244040 | tf_op jit(solution)/shard_map/ppermute | solution.py:25
  233.7 33.6 %all-to-all-start = ((bf16[4,2,131072]{2,1,0:T(2,128)(2,1)}), bf16[4,2,131072]{2,1,0:T(2,128)(2,1)}, u32[]{:S(2)}, u32[]{:S(2)}) async-start(bf16[4,2,131072]{2,1,0:T(2,128)(2,1)} %reshape.153), calls=%async_computation | async-start | bytes 4194304 | tf_op jit(solution)/shard_map/all_to_all | solution.py:97
  284.0 1.8 copy-start.4
  284.1 1.8 copy-start.5
  284.1 1.8 copy-start.10
  383.4 10.4 %copy-start.1 = (f32[128,64,64]{2,1,0:T(8,128)S(1)}, f32[128,64,64]{2,1,0:T(8,128)}, u32[]{:S(2)}) copy-start(f32[128,64,64]{2,1,0:T(8,128)} %fusion.166) | copy-start | bytes 6291460 | tf_op jit(solution)/shard_map/while
  443.7 5.5 copy-start
  449.3 6.6 copy-start.2
  610.2 10.4 %copy-start.1 = (f32[128,64,64]{2,1,0:T(8,128)S(1)}, f32[128,64,64]{2,1,0:T(8,128)}, u32[]{:S(2)}) copy-start(f32[128,64,64]{2,1,0:T(8,128)} %fusion.166) | copy-start | bytes 6291460 | tf_op jit(solution)/shard_map/while
  670.3 5.6 copy-start
  675.9 6.6 copy-start.2
where the time goes:
time: 756 us; the launch traced here: 741 us
  local copies, waits for them, and re-layouts  315 us (42%)
  matrix products  209 us (28%)
  waiting for transfers between devices  152 us (20%)
  other arithmetic  27.1 us (4%)
  starting transfers between devices  23 us (3%)
  blocking collectives  8.34 us (1%)
    gather x4, local copies, waits for them, and re-layouts, analyse_row(): picked = jnp.take(measurement_catalog, lists_row, axis=0)  131 us
    ppermute x3, waiting for transfers between devices, with_halo(): lax.ppermute(head, axis, [((i + 1) % count, i) for i in range(ends)])  91.9 us
    dynamic_update_slice x4, local copies, waits for them, and re-layouts, on_device(): result = lax.map(analyse_row, jnp.arange(row_total, dtype=jnp.int32))  86.4 us
    ppermute x3, waiting for transfers between devices, with_halo(): lax.ppermute(tail, axis, [(i, (i + 1) % count) for i in range(ends)])  60.3 us
    dot_general x8, matrix products, analyse(): jnp.einsum('pij,pjk->pik', inverse, square, precision=HIGH)  54.3 us
    dot_general x6, matrix products, analyse(): square = jnp.einsum('pij,pjk->pik', square, factor, precision=HIGH)  43.5 us
    dot_general x8, matrix products, analyse(): inverse = jnp.einsum('pij,pjk->pik', factor, inverse, precision=HIGH)  43 us
    gather x1, local copies, waits for them, and re-layouts, on_device(): jnp.take(raveled_model_vector, measurement_location, axis=1)  22.3 us
  transfers between devices with their start and end apart: 7, of which 5 were waited for; matrix products, arithmetic and copies ran while one was open for 4% of the time, Pallas kernels for 0%

commit v1 on v0

v1 whole, which is shorter than its diff:
```python
import functools
import math

import jax
import jax.numpy as jnp
from jax import lax
from jax.experimental import pallas as pl
from jax.experimental.pallas import tpu as pltpu
from jax.sharding import PartitionSpec as P

NS_ITERS = 4
INFL = 1.1
SHIFT = 1.25
LANES = 128
F32 = jnp.float32
BF16 = jnp.bfloat16
VMEM = pl.BlockSpec(memory_space=pltpu.VMEM)
SMEM = pl.BlockSpec(memory_space=pltpu.SMEM)


def params(mib):
    return pltpu.CompilerParams(vmem_limit_bytes=mib * 1024 * 1024)


def advance(upper, lower, center, c):
    width = center.shape[1]
    east = pltpu.roll(center, width - 1, 1)
    west = pltpu.roll(center, 1, 1)
    advect = c[0] * (upper - lower) + c[1] * (east - west)
    laplace = upper + lower + east + west - 4.0 * center
    return center - 0.5 * advect + c[2] * laplace


def forecast_kernel(groups, own_ref, prev_ref, next_ref, coef_ref, cprev_ref, cnext_ref, ship_ref, field_ref):
    levels, _, _, width = own_ref.shape
    part = width // groups

    def level(z, carry):
        rows = [prev_ref[z, 0], prev_ref[z, 1], own_ref[z, 0], own_ref[z, 1], next_ref[z, 0], next_ref[z, 1]]
        rows = [r.astype(F32) for r in rows]
        coeffs = [
            [cprev_ref[k, pl.ds(z, 1), :].astype(F32) for k in range(3)],
            [coef_ref[k, 0, pl.ds(z, 1), :] for k in range(3)],
            [coef_ref[k, 1, pl.ds(z, 1), :] for k in range(3)],
            [cnext_ref[k, pl.ds(z, 1), :].astype(F32) for k in range(3)],
        ]
        once = [advance(rows[i + 2], rows[i], rows[i + 1], coeffs[i]) for i in range(4)]
        for r in range(2):
            twice = advance(once[r + 2], once[r], once[r + 1], coeffs[r + 1]).astype(BF16)
            for g in range(groups):
                ship_ref[g, z, r] = twice[:, g * part : (g + 1) * part]
            for t in range(width // LANES):
                field_ref[(z * 2 + r) * (width // LANES) + t] = twice[:, t * LANES : (t + 1) * LANES]
        return carry

    lax.fori_loop(0, levels, level, 0)


def forecast(own, prev, following, coef, cprev, cnext, groups):
    levels, rows, members, width = own.shape
    return pl.pallas_call(
        functools.partial(forecast_kernel, groups),
        out_shape=[
            jax.ShapeDtypeStruct((groups, levels, rows, members, width // groups), BF16),
            jax.ShapeDtypeStruct((levels * rows * (width // LANES), members, LANES), BF16),
        ],
        in_specs=[VMEM] * 6,
        out_specs=[VMEM] * 2,
        compiler_params=params(48),
        name="forecast",
    )(own, prev, following, coef, cprev, cnext)


def observe_kernel(block_ref, shift_ref, field_ref, out_ref):
    count = out_ref.shape[0]
    members = out_ref.shape[1]
    lane = lax.broadcasted_iota(jnp.int32, (members, LANES), 1)

    def one(b, carry):
        acc = jnp.zeros((members, LANES), F32)
        for i in range(LANES):
            o = b * LANES + i
            tile = field_ref[block_ref[o]].astype(F32)
            acc = jnp.where(lane == i, pltpu.roll(tile, shift_ref[o], 1), acc)
        out_ref[b] = acc.astype(BF16)
        return carry

    lax.fori_loop(0, count, one, 0)


def observe(block, shift, field):
    members = field.shape[1]
    return pl.pallas_call(
        observe_kernel,
        out_shape=jax.ShapeDtypeStruct((block.shape[0] // LANES, members, LANES), BF16),
        in_specs=[SMEM, SMEM, VMEM],
        out_specs=VMEM,
        compiler_params=params(32),
        name="observe",
    )(block, shift, field)


def eye4():
    row = lax.broadcasted_iota(jnp.int32, (64, 256), 0)
    lane = lax.broadcasted_iota(jnp.int32, (64, 256), 1)
    return jnp.where(row == lane % 64, 1.0, 0.0).astype(F32)


def block_diag(x, low):
    left, right = x[:, :128], x[:, 128:]
    none = jnp.zeros_like(left)
    first, third = left * low, right * low
    top = jnp.concatenate([first, left - first, none, none], 0)
    bottom = jnp.concatenate([none, none, third, right - third], 0)
    return jnp.concatenate([top, bottom], 1)


def mul(a, b):
    return jnp.dot(a, b, preferred_element_type=F32)


def transform_kernel(unroll, slot_ref, lists_ref, ens_ref, obs_ref, wgt_ref, out_ref, cat_ref, rows_ref, sq_ref, force_ref, scale_ref):
    groups = slot_ref.shape[0]
    _, windows, blocks, per, _ = ens_ref.shape
    members = groups * per
    pairs = out_ref.shape[0]
    inflated = (members - 1) / INFL

    def catalog(i, carry):
        w, b = i // blocks, i % blocks
        ens = jnp.concatenate([ens_ref[slot_ref[j], w, b].astype(F32) for j in range(groups)], 0)
        mean = jnp.sum(ens, axis=0, keepdims=True) * (1.0 / members)
        value = obs_ref[w, 0, pl.ds(b, 1), :]
        root = jnp.sqrt(obs_ref[w, 1, pl.ds(b, 1), :])
        anomaly = (ens - mean) * root
        innovation = jnp.broadcast_to((value - mean) * root, ens.shape)
        cat_ref[pl.ds(pl.multiple_of(i * LANES, LANES), LANES), :] = jnp.concatenate([anomaly, innovation], 0).T
        return carry

    lax.fori_loop(0, windows * blocks, catalog, 0)

    ident = eye4()
    lane = lax.broadcasted_iota(jnp.int32, (64, 128), 1)
    lower = lane < 64

    def gather(g, carry):
        for half in range(2):
            q = g * 2 + half
            grams = []
            bounds = []
            for r in range(2):
                p = half * 2 + r
                for l in range(LANES):
                    rows_ref[p, pl.ds(l, 1), :] = cat_ref[pl.ds(lists_ref[r, q, l], 1), :]
                rows = rows_ref[p]
                weighted = rows.T[:64] * wgt_ref[r, pl.ds(q, 1), :]
                both = mul(weighted.astype(BF16), rows.astype(BF16))
                total = jnp.sum(jnp.where(lower, jnp.abs(both), 0.0), axis=0, keepdims=True)
                bounds.append(inflated + jnp.max(total, axis=1, keepdims=True))
                grams.append(both)
            turned = [pltpu.roll(x, 64, 1) for x in grams]
            bound = jnp.where(lower[:1], bounds[0], bounds[1])
            inv = 1.0 / bound
            gram = jnp.where(lower, grams[0], turned[1])
            force = jnp.where(lower, turned[0], grams[1])
            sl = slice(half * 128, half * 128 + 128)
            sq_ref[g, :, sl] = (gram + inflated * ident[:, :128]) * inv
            force_ref[g, :, sl] = force.astype(BF16)
            scale_ref[g, :, sl] = jnp.broadcast_to(inv, (8, 128))
        return carry

    lax.fori_loop(0, pairs, gather, 0)

    low = jnp.where(lane < 64, 1.0, 0.0).astype(BF16)

    def solve(s, carry):
        gs = [s * unroll + u for u in range(unroll)]
        n = range(unroll)
        sq = [sq_ref[g] for g in gs]
        h = [(1.5 - SHIFT) * ident - 0.5 * x for x in sq]
        inv = [SHIFT * ident + x for x in h]
        bd = [block_diag(x.astype(BF16), low) for x in h]
        sq = [SHIFT * sq[u] + mul(sq[u].astype(BF16), bd[u]) for u in n]
        for sweep in range(1, NS_ITERS):
            m = [mul(inv[u].astype(BF16), block_diag(sq[u].astype(BF16), low)) for u in n]
            bd = [block_diag(((1.5 - SHIFT) * ident - 0.5 * x).astype(BF16), low) for x in m]
            if sweep < NS_ITERS - 1:
                both = [jnp.concatenate([sq[u], inv[u]], 0) for u in n]
                both = [SHIFT * both[u] + mul(both[u].astype(BF16), bd[u]) for u in n]
                sq = [x[:64] for x in both]
                inv = [x[64:] for x in both]
            else:
                inv = [SHIFT * inv[u] + mul(inv[u].astype(BF16), bd[u]) for u in n]
        lhs = [x.astype(BF16) for x in inv]
        f = [mul(lhs[u], block_diag(force_ref[gs[u]], low)) for u in n]
        f = [mul(lhs[u], block_diag(f[u].astype(BF16), low)) for u in n]
        for u in n:
            scale = scale_ref[gs[u]][:1]
            out_ref[gs[u]] = (math.sqrt(members - 1.0) * jnp.sqrt(scale)) * inv[u] + scale * f[u]
        return carry

    lax.fori_loop(0, pairs // unroll, solve, 0)


def transforms(slots, lists, ens, obs, wgt):
    columns = lists.shape[1]
    pairs = columns // 2
    _, windows, blocks, _, _ = ens.shape
    return pl.pallas_call(
        functools.partial(transform_kernel, 4),
        out_shape=jax.ShapeDtypeStruct((pairs, 64, 256), F32),
        in_specs=[SMEM, SMEM, VMEM, VMEM, VMEM],
        out_specs=VMEM,
        scratch_shapes=[
            pltpu.VMEM((windows * blocks * LANES, LANES), F32),
            pltpu.VMEM((4, LANES, LANES), F32),
            pltpu.VMEM((pairs, 64, 256), F32),
            pltpu.VMEM((pairs, 64, 256), BF16),
            pltpu.VMEM((pairs, 8, 256), F32),
        ],
        compiler_params=params(48),
        name="transforms",
    )(slots, lists, ens, obs, wgt)


def update_kernel(state_ref, transform_ref, out_ref, cells_ref, center_ref):
    groups, levels, _, per, width = state_ref.shape
    members = groups * per
    pairs = transform_ref.shape[0]

    def enter(z, carry):
        parts = []
        for r in range(2):
            state = jnp.concatenate([state_ref[j, z, r].astype(F32) for j in range(groups)], 0)
            center = jnp.sum(state, axis=0, keepdims=True) * (1.0 / members)
            center_ref[z, pl.ds(r, 1), :] = center
            parts.append(state - center)
        cells_ref[pl.ds(pl.multiple_of(z * width, width), width), :] = jnp.concatenate(parts, 0).T
        return carry

    lax.fori_loop(0, levels, enter, 0)

    ident = eye4()
    lane = lax.broadcasted_iota(jnp.int32, (64, 128), 1)
    low = jnp.where(lane < 64, 1.0, 0.0).astype(BF16)

    def apply(g, carry):
        halves = []
        for half in range(2):
            q = g * 2 + half
            halves.append(jnp.concatenate([cells_ref[pl.ds(2 * q + c, levels, stride=width), :] for c in range(2)], 0))
        x = jnp.concatenate(halves, 1)
        t = transform_ref[g]
        on = t * ident
        diag = jnp.sum(on, axis=0, keepdims=True)
        y = x * diag + mul(x.astype(BF16), block_diag((t - on).astype(BF16), low))
        for half in range(2):
            q = g * 2 + half
            for c in range(2):
                cells_ref[pl.ds(2 * q + c, levels, stride=width), :] = y[c * levels : (c + 1) * levels, half * 128 : half * 128 + 128]
        return carry

    lax.fori_loop(0, pairs, apply, 0)

    def leave(z, carry):
        back = cells_ref[pl.ds(pl.multiple_of(z * width, width), width), :].T
        for r in range(2):
            out_ref[z, r] = (back[r * members : (r + 1) * members] + center_ref[z, pl.ds(r, 1), :]).astype(BF16)
        return carry

    lax.fori_loop(0, levels, leave, 0)


def update(state, transform):
    groups, levels, rows, per, width = state.shape
    return pl.pallas_call(
        update_kernel,
        out_shape=jax.ShapeDtypeStruct((levels, rows, groups * per, width), BF16),
        in_specs=[VMEM, VMEM],
        out_specs=VMEM,
        scratch_shapes=[
            pltpu.VMEM((levels * width, LANES), F32),
            pltpu.VMEM((levels, 8, width), F32),
        ],
        compiler_params=params(48),
        name="update",
    )(state, transform)


def bit_reversed(value, bits):
    return sum(((value >> b) & 1) << (bits - 1 - b) for b in range(bits))


def on_device(prior, coefficients, measured, precision, location, lists, counts, loc_weight):
    slabs = lax.axis_size("slab")
    groups = lax.axis_size("mem")
    bits = groups.bit_length() - 1
    me = lax.axis_index("mem")
    up = [(i, i + 1) for i in range(slabs - 1)]
    down = [(i + 1, i) for i in range(slabs - 1)]
    swap = [(i, i ^ 1) for i in range(slabs)]
    skip = [(i, i + 2) for i in range(0, slabs - 2, 2)] + [(i, i - 2) for i in range(3, slabs, 2)]
    odd = lax.axis_index("slab") % 2 == 1
    columns = prior.shape[3]
    nobs = measured.shape[0]

    own = jnp.transpose(prior, (1, 2, 0, 3))
    coef = jnp.transpose(coefficients, (0, 2, 1, 3))
    cprev = lax.ppermute(coef[:, 1].astype(BF16), "slab", up)
    cnext = lax.ppermute(coef[:, 0].astype(BF16), "slab", down)
    beside = lax.ppermute(own, "slab", swap)
    beyond = lax.ppermute(beside, "slab", skip)
    prev = jnp.where(odd, beside, beyond)
    following = jnp.where(odd, beyond, beside)
    ship, field = forecast(own, prev, following, coef, cprev.astype(F32), cnext.astype(F32), groups)

    zr, col = location // columns, location % columns
    block = zr * (columns // LANES) + col // LANES
    shift = (jnp.arange(nobs, dtype=jnp.int32) - col) % LANES
    seen = observe(block, shift, field)
    window = jnp.stack([lax.ppermute(seen, "slab", up), seen, lax.ppermute(seen, "slab", down)], 0)
    ens = window[None]
    step = groups // 2
    while step:
        ens = jnp.concatenate([ens, lax.ppermute(ens, "mem", [(i, i ^ step) for i in range(groups)])], 0)
        step //= 2
    slots = bit_reversed(jnp.arange(groups, dtype=jnp.int32) ^ me, bits)

    extras = jnp.stack([measured, precision], 0).reshape(2, nobs // LANES, LANES)
    obs = jnp.stack([lax.ppermute(extras, "slab", up), extras, lax.ppermute(extras, "slab", down)], 0)
    position = lax.broadcasted_iota(jnp.int32, loc_weight.shape, 2)
    wgt = jnp.where(position < counts[..., None], loc_weight, 0.0)
    transform = transforms(slots, lists, ens, obs, wgt)

    state = lax.all_to_all(ship, "mem", 0, 0, tiled=False)
    result = update(state, transform)
    return jnp.transpose(result, (2, 0, 1, 3))


def solution(mesh):
    return jax.shard_map(
        on_device,
        mesh=mesh,
        in_specs=(
            P("mem", None, "slab", None),
            P(None, None, "slab", None),
            P("slab"),
            P("slab"),
            P("slab"),
            P("slab", "mem", None),
            P("slab", "mem"),
            P("slab", "mem", None),
        ),
        out_specs=P(None, None, "slab", "mem"),
        check_vma=False,
    )
```

time: 756 us -> 302 us (0.40); the launches traced: 741 us -> 299 us
  local copies, waits for them, and re-layouts: 315 us -> 10.5 us
  matrix products: 209 us -> 0 us
  Pallas kernels: 0 us -> 135 us
  waiting for transfers between devices: 152 us -> 114 us
  other arithmetic: 27.1 us -> 7.92 us
  starting transfers between devices: 23 us -> 32 us
  blocking collectives: 8.34 us -> 0 us
    dot_general x32 -> x0, matrix products: 209 us -> none  [the longest x8 54.3 us: analyse(): jnp.einsum('pij,pjk->pik', inverse, square, precision=HIGH)]
    gather x5 -> x0, local copies, waits for them, and re-layouts: 153 us -> none  [the longest x4 131 us: analyse_row(): picked = jnp.take(measurement_catalog, lists_row, axis=0)]
    pallas_call x0 -> x4, Pallas kernels: none -> 135 us  [the longest x1 90.5 us: transforms(): pl.pallas_call(functools.partial(transform_kernel, 4), out_shape=jax.Shap...]
    dynamic_update_slice x4 -> x0, local copies, waits for them, and re-layouts: 86.4 us -> none  [on_device(): result = lax.map(analyse_row, jnp.arange(row_total, dtype=jnp.int32))]
    ppermute x6 -> x10, waiting for transfers between devices: 152 us -> 114 us  [the longest x1 45.4 us: on_device(): beside = lax.ppermute(own, 'slab', swap)]
    unnamed x19 -> x22, local copies, waits for them, and re-layouts: 21.3 us -> 5.58 us
    convert_element_type x4 -> x1, local copies, waits for them, and re-layouts: 12.6 us -> 0.03 us  [on_device(): cnext = lax.ppermute(coef[:, 0].astype(BF16), 'slab', down)]
    add x1 -> x0, local copies, waits for them, and re-layouts: 11.5 us -> none  [stencil(): return center - 0.5 * advect + coeffs[2] * laplace]
  transfers between devices with their start and end apart: 7 -> 11, of which waited for: 5 -> 5; matrix products, arithmetic and copies ran while one was open for 4% -> 2% of each run, Pallas kernels for 0% -> 30%
where the time goes in v1:
time: 302 us; the launch traced here: 299 us
  Pallas kernels  135 us (45%)
  waiting for transfers between devices  114 us (38%)
  starting transfers between devices  32 us (11%)
  local copies, waits for them, and re-layouts  10.5 us (3%)
  other arithmetic  7.92 us (3%)
    pallas_call x1, Pallas kernels, transforms(): pl.pallas_call(functools.partial(transform_kernel, 4), out_shape=jax.Shap...  90.5 us
    ppermute x1, waiting for transfers between devices, on_device(): beside = lax.ppermute(own, 'slab', swap)  45.4 us
    ppermute x2, waiting for transfers between devices, on_device(): lax.ppermute(ens, 'mem', [(i, i ^ step) for i in range(groups)])  31.7 us
    ppermute x1, waiting for transfers between devices, on_device(): beyond = lax.ppermute(beside, 'slab', skip)  30.5 us
    pallas_call x1, Pallas kernels, update(): pl.pallas_call(update_kernel, out_shape=jax.ShapeDtypeStruct((levels, row...  21.7 us
    pallas_call x1, Pallas kernels, forecast(): pl.pallas_call(functools.partial(forecast_kernel, groups), out_shape=[jax...  12.6 us
    pallas_call x1, Pallas kernels, observe(): pl.pallas_call(observe_kernel, out_shape=jax.ShapeDtypeStruct((block.shap...  9.84 us
    all_to_all x1, starting transfers between devices, on_device(): state = lax.all_to_all(ship, 'mem', 0, 0, tiled=False)  6.62 us
  transfers between devices with their start and end apart: 11, of which 5 were waited for; matrix products, arithmetic and copies ran while one was open for 2% of the time, Pallas kernels for 30%

profile of v1, /device:TPU:9, one launch (start us, length us, event | category | flops | bytes accessed | tf_op | source)
XLA Modules:
  0.0 299.4 jit_solution(11397567787332184269)
XLA Ops:
  0.0 3.4 %copy.17 = bf16[16,32,2,1024]{3,0,2,1:T(8,128)(2,1)S(1)} copy(bf16[16,32,2,1024]{3,2,1,0:T(2,128)(2,1)} %param.8) | data formatting | bytes 4194304 | tf_op args[0]
  3.4 1.3 collective-permute-start
  4.7 45.4 %collective-permute-done = bf16[32,2,16,1024]{3,2,1,0:T(8,128)(2,1)} collective-permute-done((bf16[32,2,16,1024]{3,2,1,0:T(8,128)(2,1)S(1)}, bf16[32,2,16,1024]{3,2,1,0:T(8,128)(2,1)}, u32[]{:S(2)}, u32[]{:S(2)}) %collective-permute-start) | collective-permute-done | bytes 2097184 | tf_op jit(solution)/shard_map/ppermute | solution.py:311
  50.1 3.2 %collective-permute-start.1 = (bf16[32,2,16,1024]{3,2,1,0:T(8,128)(2,1)}, bf16[32,2,16,1024]{3,2,1,0:T(8,128)(2,1)}, u32[]{:S(2)}, u32[]{:S(2)}) collective-permute-start(bf16[32,2,16,1024]{3,2,1,0:T(8,128)(2,1)} %collective-permute-done), channel_id=1, source_target_pairs={{0,2},{2,4},{4,6},{3,1},{5,3},{7,5},{8,10},{10,12},{12,14},{11,9},... | collective-permute-start | bytes 6291464 | tf_op jit(solution)/shard_map/ppermute | solution.py:312
  53.6 2.0 collective-permute-start.2
  55.6 4.2 %collective-permute-start.3 = (bf16[3,32,1024]{2,1,0:T(8,128)(2,1)S(1)}, bf16[3,32,1024]{2,1,0:T(8,128)(2,1)S(1)}, u32[]{:S(2)}, u32[]{:S(2)}) collective-permute-start(bf16[3,32,1024]{2,1,0:T(8,128)(2,1)S(1)} %get-tuple-element.11), channel_id=1, source_target_pairs={{1,0},{2,1},{3,2},{4,3},{5,4},{6,5},{7,6},{9,8},{10,9},{11,10},{12... | collective-permute-start | bytes 589832 | tf_op jit(solution)/shard_map/ppermute | solution.py:310
  59.8 1.4 copy.18
  62.2 5.2 %collective-permute-done.3 = bf16[3,32,1024]{2,1,0:T(8,128)(2,1)S(1)} collective-permute-done((bf16[3,32,1024]{2,1,0:T(8,128)(2,1)S(1)}, bf16[3,32,1024]{2,1,0:T(8,128)(2,1)S(1)}, u32[]{:S(2)}, u32[]{:S(2)}) %collective-permute-start.3) | collective-permute-done | bytes 196640 | tf_op jit(solution)/shard_map/ppermute | solution.py:310
  67.4 30.5 %collective-permute-done.1 = bf16[32,2,16,1024]{3,2,1,0:T(8,128)(2,1)} collective-permute-done((bf16[32,2,16,1024]{3,2,1,0:T(8,128)(2,1)}, bf16[32,2,16,1024]{3,2,1,0:T(8,128)(2,1)}, u32[]{:S(2)}, u32[]{:S(2)}) %collective-permute-start.1) | collective-permute-done | bytes 2097184 | tf_op jit(solution)/shard_map/ppermute | solution.py:312
  97.9 4.5 %broadcast_select_fusion = (bf16[32,2,16,1024]{3,2,1,0:T(8,128)(2,1)}, bf16[32,2,16,1024]{3,2,1,0:T(8,128)(2,1)}) fusion(bf16[32,2,16,1024]{3,2,1,0:T(8,128)(2,1)} %collective-permute-done.1, bf16[32,2,16,1024]{3,2,1,0:T(8,128)(2,1)} %collective-permute-done, pred[]{:T(512)S(6)} %eq.8), kind=kLoop, calls=%fused_computation.1 | loop fusion | flops 2097152 | bytes 8388609 | tf_op jit(solution)/shard_map/jit(_where)/select_n | solution.py:314
  102.4 12.6 %forecast.1 = (bf16[4,32,2,16,256]{4,3,2,1,0:T(8,128)(2,1)S(1)}, bf16[512,16,128]{2,1,0:T(8,128)(2,1)S(1)}) custom-call(bf16[32,2,16,1024]{3,2,1,0:T(8,128)(2,1)} %bitcast.29, bf16[32,2,16,1024]{3,2,1,0:T(8,128)(2,1)} %get-tuple-element.10.prev_ref, bf16[32,2,16,1024]{3,2,1,0:T(8,128)(2,1)} %get-tuple-element.9.next_ref, f32[3,2,32,1024]{3,2,1,0:T(8,128)S(1)} %bitcast.26, ...), custom_call_target="tpu_custom_call" | custom-call | tf_op jit(solution)/shard_map/forecast/pallas_call | solution.py:61
  115.0 9.8 %observe.1 = bf16[32,16,128]{2,1,0:T(8,128)(2,1)S(1)} custom-call(s32[4096]{0:T(1024)S(1)} %get-tuple-element.14.block_ref, s32[4096]{0:T(1024)S(1)} %get-tuple-element.13.shift_ref, bf16[512,16,128]{2,1,0:T(8,128)(2,1)S(1)} %get-tuple-element.8.field_ref), custom_call_target="tpu_custom_call" | custom-call | tf_op jit(solution)/shard_map/observe/pallas_call | solution.py:93
  124.9 3.1 %collective-permute-start.4 = (bf16[32,16,128]{2,1,0:T(8,128)(2,1)S(1)}, bf16[32,16,128]{2,1,0:T(8,128)(2,1)S(1)}, u32[]{:S(2)}, u32[]{:S(2)}) collective-permute-start(bf16[32,16,128]{2,1,0:T(8,128)(2,1)S(1)} %observe.1), channel_id=1, source_target_pairs={{0,1},{1,2},{2,3},{3,4},{4,5},{5,6},{6,7},{8,9},{9,10},{10,11},{11... | collective-permute-start | bytes 393224 | tf_op jit(solution)/shard_map/ppermute | solution.py:321
  128.0 3.0 %collective-permute-start.5 = (bf16[32,16,128]{2,1,0:T(8,128)(2,1)S(1)}, bf16[32,16,128]{2,1,0:T(8,128)(2,1)S(1)}, u32[]{:S(2)}, u32[]{:S(2)}) collective-permute-start(bf16[32,16,128]{2,1,0:T(8,128)(2,1)S(1)} %observe.1), channel_id=1, source_target_pairs={{1,0},{2,1},{3,2},{4,3},{5,4},{6,5},{7,6},{9,8},{10,9},{11,10},{12... | collective-permute-start | bytes 393224 | tf_op jit(solution)/shard_map/ppermute | solution.py:321
  131.1 6.6 %all-to-all-start = ((bf16[4,32,2,16,256]{4,3,2,1,0:T(8,128)(2,1)}), bf16[4,32,2,16,256]{4,3,2,1,0:T(8,128)(2,1)S(1)}, u32[]{:S(2)}, u32[]{:S(2)}) async-start(bf16[4,32,2,16,256]{4,3,2,1,0:T(8,128)(2,1)} %copy-done.1), calls=%async_computation | async-start | bytes 4194304 | tf_op jit(solution)/shard_map/all_to_all | solution.py:335
  137.8 1.5 collective-permute-start.6
  139.2 31.7 %collective-permute-done.6 = bf16[1,3,32,16,128]{4,3,2,1,0:T(8,128)(2,1)S(1)} collective-permute-done((bf16[1,3,32,16,128]{4,3,2,1,0:T(8,128)(2,1)S(1)}, bf16[1,3,32,16,128]{4,3,2,1,0:T(8,128)(2,1)S(1)}, u32[]{:S(2)}, u32[]{:S(2)}) %collective-permute-start.6) | collective-permute-done | bytes 393248 | tf_op jit(solution)/shard_map/ppermute | solution.py:325
  172.8 2.2 collective-permute-start.8
  175.0 3.9 %collective-permute-start.9 = (f32[2,32,128]{2,1,0:T(8,128)S(1)}, f32[2,32,128]{2,1,0:T(8,128)S(1)}, u32[]{:S(2)}, u32[]{:S(2)}) collective-permute-start(f32[2,32,128]{2,1,0:T(8,128)S(1)} %pad_maximum_fusion.3), channel_id=1, source_target_pairs={{1,0},{2,1},{3,2},{4,3},{5,4},{6,5},{7,6},{9,8},{10,9},{11,10},{12... | collective-permute-start | bytes 98312 | tf_op jit(solution)/shard_map/ppermute | solution.py:330
  180.4 1.3 pad_maximum_fusion.ens_ref
  181.7 90.5 %transforms.1.transform_ref = f32[64,64,256]{2,1,0:T(8,128)S(1)} custom-call(s32[4]{0:T(128)S(1)} %shift-left_add_fusion.slot_ref, s32[2,128,128]{2,1,0:T(8,128)S(1)} %copy-done.2, bf16[4,3,32,16,128]{4,3,2,1,0:T(8,128)(2,1)S(1)} %pad_maximum_fusion.ens_ref, f32[3,2,32,128]{3,2,1,0:T(8,128)S(1)} %pad_maximum_fusion.2.obs_ref, f32[2,128,128]{2,1,0:T(8,128)S(1)} %fusion.wgt_ref), custom_call_target="tpu_custom_call" | custom-call | tf_op jit(solution)/shard_map/transforms/pallas_call | solution.py:209
  272.2 1.9 copy-done
  274.2 21.7 %update.1 = bf16[32,2,64,256]{3,2,1,0:T(8,128)(2,1)S(1)} custom-call(bf16[4,32,2,16,256]{4,3,2,1,0:T(8,128)(2,1)S(1)} %all-to-all-done.state_ref, f32[64,64,256]{2,1,0:T(8,128)} %copy-done), custom_call_target="tpu_custom_call" | custom-call | tf_op jit(solution)/shard_map/update/pallas_call | solution.py:276
  295.9 3.5 %copy.12 = bf16[64,32,2,256]{3,2,1,0:T(2,128)(2,1)} copy(bf16[64,32,2,256]{3,0,2,1:T(8,128)(2,1)S(1)} %bitcast.25) | data formatting | bytes 4194304 | tf_op jit(solution)/shard_map/transpose | solution.py:337
  (38 shorter events, 4.6 us)
Async XLA Ops:
  0.0 53.3 %copy-start.4 = (f32[3,32,2,1024]{3,2,1,0:T(2,128)S(1)}, f32[3,32,2,1024]{3,2,1,0:T(2,128)}, u32[]{:S(2)}) copy-start(f32[3,32,2,1024]{3,2,1,0:T(2,128)} %param.9) | copy-start | bytes 2359300
  3.4 58.8 %copy-start.3 = (bf16[16,32,2,1024]{3,0,2,1:T(8,128)(2,1)}, bf16[16,32,2,1024]{3,0,2,1:T(8,128)(2,1)S(1)}, u32[]{:S(2)}) copy-start(bf16[16,32,2,1024]{3,0,2,1:T(8,128)(2,1)S(1)} %copy.17) | copy-start | bytes 6291460
  3.4 57.8 %copy-start.8 = (s32[4096]{0:T(1024)S(1)}, s32[4096]{0:T(1024)}, u32[]{:S(2)}) copy-start(s32[4096]{0:T(1024)} %param.12) | copy-start | bytes 49156
  3.4 46.7 %collective-permute-start = (bf16[32,2,16,1024]{3,2,1,0:T(8,128)(2,1)S(1)}, bf16[32,2,16,1024]{3,2,1,0:T(8,128)(2,1)}, u32[]{:S(2)}, u32[]{:S(2)}) collective-permute-start(bf16[32,2,16,1024]{3,2,1,0:T(8,128)(2,1)S(1)} %bitcast.28), channel_id=1, source_target_pairs={{0,1},{1,0},{2,3},{3,2},{4,5},{5,4},{6,7},{7,6},{8,9},{9,8},{10,11... | collective-permute-start | bytes 6291464 | tf_op jit(solution)/shard_map/ppermute | solution.py:311
  50.1 47.8 %collective-permute-start.1 = (bf16[32,2,16,1024]{3,2,1,0:T(8,128)(2,1)}, bf16[32,2,16,1024]{3,2,1,0:T(8,128)(2,1)}, u32[]{:S(2)}, u32[]{:S(2)}) collective-permute-start(bf16[32,2,16,1024]{3,2,1,0:T(8,128)(2,1)} %collective-permute-done), channel_id=1, source_target_pairs={{0,2},{2,4},{4,6},{3,1},{5,3},{7,5},{8,10},{10,12},{12,14},{11,9},... | collective-permute-start | bytes 6291464 | tf_op jit(solution)/shard_map/ppermute | solution.py:312
  53.6 7.7 %collective-permute-start.2 = (bf16[3,32,1024]{2,1,0:T(8,128)(2,1)S(1)}, bf16[3,32,1024]{2,1,0:T(8,128)(2,1)}, u32[]{:S(2)}, u32[]{:S(2)}) collective-permute-start(bf16[3,32,1024]{2,1,0:T(8,128)(2,1)S(1)} %get-tuple-element.12), channel_id=1, source_target_pairs={{0,1},{1,2},{2,3},{3,4},{4,5},{5,6},{6,7},{8,9},{9,10},{10,11},{11... | collective-permute-start | bytes 589832 | tf_op jit(solution)/shard_map/ppermute | solution.py:309
  55.6 11.8 %collective-permute-start.3 = (bf16[3,32,1024]{2,1,0:T(8,128)(2,1)S(1)}, bf16[3,32,1024]{2,1,0:T(8,128)(2,1)S(1)}, u32[]{:S(2)}, u32[]{:S(2)}) collective-permute-start(bf16[3,32,1024]{2,1,0:T(8,128)(2,1)S(1)} %get-tuple-element.11), channel_id=1, source_target_pairs={{1,0},{2,1},{3,2},{4,3},{5,4},{6,5},{7,6},{9,8},{10,9},{11,10},{12... | collective-permute-start | bytes 589832 | tf_op jit(solution)/shard_map/ppermute | solution.py:310
  115.0 16.1 %copy-start.1 = (bf16[4,32,2,16,256]{4,3,2,1,0:T(8,128)(2,1)}, bf16[4,32,2,16,256]{4,3,2,1,0:T(8,128)(2,1)S(1)}, u32[]{:S(2)}) copy-start(bf16[4,32,2,16,256]{4,3,2,1,0:T(8,128)(2,1)S(1)} %get-tuple-element.7) | copy-start | bytes 6291460
  124.9 12.8 %collective-permute-start.4 = (bf16[32,16,128]{2,1,0:T(8,128)(2,1)S(1)}, bf16[32,16,128]{2,1,0:T(8,128)(2,1)S(1)}, u32[]{:S(2)}, u32[]{:S(2)}) collective-permute-start(bf16[32,16,128]{2,1,0:T(8,128)(2,1)S(1)} %observe.1), channel_id=1, source_target_pairs={{0,1},{1,2},{2,3},{3,4},{4,5},{5,6},{6,7},{8,9},{9,10},{10,11},{11... | collective-permute-start | bytes 393224 | tf_op jit(solution)/shard_map/ppermute | solution.py:321
  128.0 9.7 %collective-permute-start.5 = (bf16[32,16,128]{2,1,0:T(8,128)(2,1)S(1)}, bf16[32,16,128]{2,1,0:T(8,128)(2,1)S(1)}, u32[]{:S(2)}, u32[]{:S(2)}) collective-permute-start(bf16[32,16,128]{2,1,0:T(8,128)(2,1)S(1)} %observe.1), channel_id=1, source_target_pairs={{1,0},{2,1},{3,2},{4,3},{5,4},{6,5},{7,6},{9,8},{10,9},{11,10},{12... | collective-permute-start | bytes 393224 | tf_op jit(solution)/shard_map/ppermute | solution.py:321
  131.1 143.1 %all-to-all-start = ((bf16[4,32,2,16,256]{4,3,2,1,0:T(8,128)(2,1)}), bf16[4,32,2,16,256]{4,3,2,1,0:T(8,128)(2,1)S(1)}, u32[]{:S(2)}, u32[]{:S(2)}) async-start(bf16[4,32,2,16,256]{4,3,2,1,0:T(8,128)(2,1)} %copy-done.1), calls=%async_computation | async-start | bytes 4194304 | tf_op jit(solution)/shard_map/all_to_all | solution.py:335
  137.7 35.1 %copy-start.6 = (f32[4096]{0:T(1024)S(1)}, f32[4096]{0:T(1024)}, u32[]{:S(2)}) copy-start(f32[4096]{0:T(1024)} %param.11) | copy-start | bytes 49156
  137.7 35.1 %copy-start.7 = (f32[4096]{0:T(1024)S(1)}, f32[4096]{0:T(1024)}, u32[]{:S(2)}) copy-start(f32[4096]{0:T(1024)} %param.10) | copy-start | bytes 49156
  137.7 41.3 %copy-start.5 = (f32[2,128,128]{2,1,0:T(8,128)S(1)}, f32[2,128,128]{2,1,0:T(8,128)}, u32[]{:S(2)}) copy-start(f32[2,128,128]{2,1,0:T(8,128)} %param.15) | copy-start | bytes 393220
  137.7 41.3 %copy-start.9 = (s32[2,128]{1,0:T(2,128)S(1)}, s32[2,128]{1,0:T(2,128)}, u32[]{:S(2)}) copy-start(s32[2,128]{1,0:T(2,128)} %param.14) | copy-start | bytes 3076
  137.8 33.2 %collective-permute-start.6 = (bf16[1,3,32,16,128]{4,3,2,1,0:T(8,128)(2,1)S(1)}, bf16[1,3,32,16,128]{4,3,2,1,0:T(8,128)(2,1)S(1)}, u32[]{:S(2)}, u32[]{:S(2)}) collective-permute-start(bf16[1,3,32,16,128]{4,3,2,1,0:T(8,128)(2,1)S(1)} %maximum_bitcast_fusion), channel_id=1, source_target_pairs={{0,16},{8,24},{16,0},{24,8},{1,17},{9,25},{17,1},{25,9},{2,18},{10... | collective-permute-start | bytes 1179656 | tf_op jit(solution)/shard_map/ppermute | solution.py:325
  171.9 9.8 %copy-start.2 = (s32[2,128,128]{2,1,0:T(8,128)S(1)}, s32[2,128,128]{2,1,0:T(8,128)}, u32[]{:S(2)}) copy-start(s32[2,128,128]{2,1,0:T(8,128)} %lists_ref.1) | copy-start | bytes 393220
  171.9 8.5 %collective-permute-start.7 = (bf16[2,3,32,16,128]{4,3,2,1,0:T(8,128)(2,1)}, bf16[2,3,32,16,128]{4,3,2,1,0:T(8,128)(2,1)}, u32[]{:S(2)}, u32[]{:S(2)}) collective-permute-start(bf16[2,3,32,16,128]{4,3,2,1,0:T(8,128)(2,1)} %pad_maximum_fusion.1), channel_id=1, source_target_pairs={{0,8},{8,0},{16,24},{24,16},{1,9},{9,1},{17,25},{25,17},{2,10},{10... | collective-permute-start | bytes 2359304 | tf_op jit(solution)/shard_map/ppermute | solution.py:325
  172.8 6.3 %collective-permute-start.8 = (f32[2,32,128]{2,1,0:T(8,128)S(1)}, f32[2,32,128]{2,1,0:T(8,128)S(1)}, u32[]{:S(2)}, u32[]{:S(2)}) collective-permute-start(f32[2,32,128]{2,1,0:T(8,128)S(1)} %pad_maximum_fusion.3), channel_id=1, source_target_pairs={{0,1},{1,2},{2,3},{3,4},{4,5},{5,6},{6,7},{8,9},{9,10},{10,11},{11... | collective-permute-start | bytes 98312 | tf_op jit(solution)/shard_map/ppermute | solution.py:330
  175.0 5.3 %collective-permute-start.9 = (f32[2,32,128]{2,1,0:T(8,128)S(1)}, f32[2,32,128]{2,1,0:T(8,128)S(1)}, u32[]{:S(2)}, u32[]{:S(2)}) collective-permute-start(f32[2,32,128]{2,1,0:T(8,128)S(1)} %pad_maximum_fusion.3), channel_id=1, source_target_pairs={{1,0},{2,1},{3,2},{4,3},{5,4},{6,5},{7,6},{9,8},{10,9},{11,10},{12... | collective-permute-start | bytes 98312 | tf_op jit(solution)/shard_map/ppermute | solution.py:330
  272.2 1.9 copy-start

commit v2 on v1

v2 whole, which is shorter than its diff:
```python
import functools
import math

import jax
import jax.numpy as jnp
from jax import lax
from jax.experimental import pallas as pl
from jax.experimental.pallas import tpu as pltpu
from jax.sharding import PartitionSpec as P

NS_ITERS = 4
INFL = 1.1
SHIFT = 1.25
LANES = 128
F32 = jnp.float32
BF16 = jnp.bfloat16
VMEM = pl.BlockSpec(memory_space=pltpu.VMEM)
SMEM = pl.BlockSpec(memory_space=pltpu.SMEM)


def params(mib):
    return pltpu.CompilerParams(vmem_limit_bytes=mib * 1024 * 1024)


def advance(upper, lower, center, c):
    width = center.shape[1]
    east = pltpu.roll(center, width - 1, 1)
    west = pltpu.roll(center, 1, 1)
    advect = c[0] * (upper - lower) + c[1] * (east - west)
    laplace = upper + lower + east + west - 4.0 * center
    return center - 0.5 * advect + c[2] * laplace


def forecast_kernel(first, odd_ref, own_ref, beside_ref, beyond_ref, coef_ref, cprev_ref, cnext_ref, field_ref):
    levels, width = field_ref.shape[0], own_ref.shape[2]
    odd = odd_ref[0] == 1

    def level(z, carry):
        beside = [beside_ref[2 * z + r].astype(F32) for r in range(2)]
        beyond = [beyond_ref[2 * z + r].astype(F32) for r in range(2)]
        rows = [jnp.where(odd, beside[r], beyond[r]) for r in range(2)]
        rows += [own_ref[2 * z + r].astype(F32) for r in range(2)]
        rows += [jnp.where(odd, beyond[r], beside[r]) for r in range(2)]
        at = pl.ds(first + z, 1)
        coeffs = [
            [cprev_ref[k, at, :] for k in range(3)],
            [coef_ref[k, 0, at, :] for k in range(3)],
            [coef_ref[k, 1, at, :] for k in range(3)],
            [cnext_ref[k, at, :] for k in range(3)],
        ]
        once = [advance(rows[i + 2], rows[i], rows[i + 1], coeffs[i]) for i in range(4)]
        for r in range(2):
            twice = advance(once[r + 2], once[r], once[r + 1], coeffs[r + 1]).astype(BF16)
            for t in range(width // LANES):
                field_ref[z, r, t] = twice[:, t * LANES : (t + 1) * LANES]
        return carry

    lax.fori_loop(0, levels, level, 0)


def forecast(span, odd, own, beside, beyond, coef, cprev, cnext):
    first, levels, rows = span[0], span[1] - span[0], coef.shape[1]
    _, members, width = own.shape
    return pl.pallas_call(
        functools.partial(forecast_kernel, first),
        out_shape=jax.ShapeDtypeStruct((levels, rows, width // LANES, members, LANES), BF16),
        in_specs=[SMEM] + [VMEM] * 6,
        out_specs=VMEM,
        compiler_params=params(32),
        name="forecast",
    )(odd, own, beside, beyond, coef, cprev, cnext)


def observe_kernel(block_ref, shift_ref, *refs):
    *part_refs, out_ref, field_ref = refs
    first = 0
    for part in part_refs:
        field_ref[first : first + part.shape[0]] = part[...]
        first += part.shape[0]
    count = out_ref.shape[0]
    members = out_ref.shape[1]
    lane = lax.broadcasted_iota(jnp.int32, (members, LANES), 1)

    def one(b, carry):
        acc = jnp.zeros((members, LANES), F32)
        for i in range(LANES):
            o = b * LANES + i
            tile = field_ref[block_ref[o]].astype(F32)
            acc = jnp.where(lane == i, pltpu.roll(tile, shift_ref[o], 1), acc)
        out_ref[b] = acc.astype(BF16)
        return carry

    lax.fori_loop(0, count, one, 0)


def observe(block, shift, fields):
    parts = [f.reshape((-1,) + f.shape[3:]) for f in fields]
    members = parts[0].shape[1]
    return pl.pallas_call(
        observe_kernel,
        out_shape=jax.ShapeDtypeStruct((block.shape[0] // LANES, members, LANES), BF16),
        in_specs=[SMEM, SMEM] + [VMEM] * len(parts),
        out_specs=VMEM,
        scratch_shapes=[pltpu.VMEM((sum(p.shape[0] for p in parts), members, LANES), BF16)],
        compiler_params=params(32),
        name="observe",
    )(block, shift, *parts)


def eye4():
    row = lax.broadcasted_iota(jnp.int32, (64, 256), 0)
    lane = lax.broadcasted_iota(jnp.int32, (64, 256), 1)
    return jnp.where(row == lane % 64, 1.0, 0.0).astype(F32)


def block_diag(x, low):
    left, right = x[:, :128], x[:, 128:]
    none = jnp.zeros_like(left)
    first, third = left * low, right * low
    top = jnp.concatenate([first, left - first, none, none], 0)
    bottom = jnp.concatenate([none, none, third, right - third], 0)
    return jnp.concatenate([top, bottom], 1)


def mul(a, b):
    return jnp.dot(a, b, preferred_element_type=F32)


GROUPS = 4


def gather_block(lists_ref, wgt_ref, first, cat_ref, rows_ref, sq_ref, force_ref, scale_ref, ident, lower, inflated):
    for q in range(2 * GROUPS):
        grams = []
        bounds = []
        for r in range(2):
            p = (2 * q + r) % rows_ref.shape[0]
            for l in range(LANES):
                rows_ref[p, pl.ds(l, 1), :] = cat_ref[pl.ds(lists_ref[2 * q + r, l], 1), :]
            rows = rows_ref[p]
            weighted = rows.T[:64] * wgt_ref[r, pl.ds(first + q, 1), :]
            both = mul(weighted.astype(BF16), rows.astype(BF16))
            total = jnp.sum(jnp.where(lower, jnp.abs(both), 0.0), axis=0, keepdims=True)
            bounds.append(inflated + jnp.max(total, axis=1, keepdims=True))
            grams.append(both)
        turned = [pltpu.roll(x, 64, 1) for x in grams]
        inv = 1.0 / jnp.where(lower[:1], bounds[0], bounds[1])
        gram = jnp.where(lower, grams[0], turned[1])
        force = jnp.where(lower, turned[0], grams[1])
        g, half = q // 2, q % 2
        sl = slice(half * 128, half * 128 + 128)
        sq_ref[g, :, sl] = (gram + inflated * ident[:, :128]) * inv
        force_ref[g, :, sl] = force.astype(BF16)
        scale_ref[g, :, sl] = jnp.broadcast_to(inv, (8, 128))


def solve_block(sq_ref, force_ref, scale_ref, out_ref, first, ident, low, members):
    n = range(GROUPS)
    sq = [sq_ref[g] for g in n]
    h = [(1.5 - SHIFT) * ident - 0.5 * x for x in sq]
    inv = [SHIFT * ident + x for x in h]
    bd = [block_diag(x.astype(BF16), low) for x in h]
    sq = [SHIFT * sq[u] + mul(sq[u].astype(BF16), bd[u]) for u in n]
    for sweep in range(1, NS_ITERS):
        m = [mul(inv[u].astype(BF16), block_diag(sq[u].astype(BF16), low)) for u in n]
        bd = [block_diag(((1.5 - SHIFT) * ident - 0.5 * x).astype(BF16), low) for x in m]
        if sweep < NS_ITERS - 1:
            both = [jnp.concatenate([sq[u], inv[u]], 0) for u in n]
            both = [SHIFT * both[u] + mul(both[u].astype(BF16), bd[u]) for u in n]
            sq = [x[:64] for x in both]
            inv = [x[64:] for x in both]
        else:
            inv = [SHIFT * inv[u] + mul(inv[u].astype(BF16), bd[u]) for u in n]
    lhs = [x.astype(BF16) for x in inv]
    f = [mul(lhs[u], block_diag(force_ref[u], low)) for u in n]
    f = [mul(lhs[u], block_diag(f[u].astype(BF16), low)) for u in n]
    for u in n:
        scale = scale_ref[u][:1]
        out_ref[first + u] = (math.sqrt(members - 1.0) * jnp.sqrt(scale)) * inv[u] + scale * f[u]


def transform_kernel(slot_ref, ens_ref, obs_ref, wgt_ref, lists_ref, out_ref, cat_ref, rows_ref, *scratch):
    work, (lists_a, lists_b, sems) = (scratch[:3], scratch[3:6]), scratch[6:]
    smem = (lists_a, lists_b)
    groups = slot_ref.shape[0]
    _, windows, blocks, per, _ = ens_ref.shape
    members = groups * per
    count = lists_ref.shape[0]
    inflated = (members - 1) / INFL

    def fetch(b, half):
        return pltpu.make_async_copy(lists_ref.at[b], smem[half], sems.at[half])

    for half in range(2):
        fetch(half, half).start()

    def catalog(i, carry):
        w, b = i // blocks, i % blocks
        ens = jnp.concatenate([ens_ref[slot_ref[j], w, b].astype(F32) for j in range(groups)], 0)
        mean = jnp.sum(ens, axis=0, keepdims=True) * (1.0 / members)
        value = obs_ref[w, 0, pl.ds(b, 1), :]
        root = jnp.sqrt(obs_ref[w, 1, pl.ds(b, 1), :])
        anomaly = (ens - mean) * root
        innovation = jnp.broadcast_to((value - mean) * root, ens.shape)
        cat_ref[pl.ds(pl.multiple_of(i * LANES, LANES), LANES), :] = jnp.concatenate([anomaly, innovation], 0).T
        return carry

    lax.fori_loop(0, windows * blocks, catalog, 0, unroll=4)

    ident = eye4()
    lane = lax.broadcasted_iota(jnp.int32, (64, 128), 1)
    lower = lane < 64
    low = jnp.where(lower, 1.0, 0.0).astype(BF16)

    def pair(i, carry):
        for half in range(2):
            b = 2 * i + half
            fetch(b, half).wait()
            solve_block(*work[1 - half], out_ref, jnp.maximum(b - 1, 0) * GROUPS, ident, low, members)
            gather_block(smem[half], wgt_ref, b * 2 * GROUPS, cat_ref, rows_ref, *work[half], ident, lower, inflated)

            @pl.when(b + 2 < count)
            def _():
                fetch(b + 2, half).start()

        return carry

    lax.fori_loop(0, count // 2, pair, 0)
    solve_block(*work[1], out_ref, (count - 1) * GROUPS, ident, low, members)


def transforms(slots, lists, ens, obs, wgt):
    columns = lists.shape[1]
    pairs = columns // 2
    _, windows, blocks, _, _ = ens.shape
    lists = lists.reshape(2, pairs // GROUPS, 2 * GROUPS, LANES).transpose(1, 2, 0, 3).reshape(-1, 4 * GROUPS, LANES)
    work = [
        pltpu.VMEM((GROUPS, 64, 256), F32),
        pltpu.VMEM((GROUPS, 64, 256), BF16),
        pltpu.VMEM((GROUPS, 8, 256), F32),
    ]
    return pl.pallas_call(
        transform_kernel,
        out_shape=jax.ShapeDtypeStruct((pairs, 64, 256), F32),
        in_specs=[SMEM] + [VMEM] * 4,
        out_specs=VMEM,
        scratch_shapes=[
            pltpu.VMEM((windows * blocks * LANES, LANES), F32),
            pltpu.VMEM((8, LANES, LANES), F32),
            *work,
            *work,
            pltpu.SMEM((4 * GROUPS, LANES), jnp.int32),
            pltpu.SMEM((4 * GROUPS, LANES), jnp.int32),
            pltpu.SemaphoreType.DMA((2,)),
        ],
        compiler_params=params(48),
        name="transforms",
    )(slots, ens, obs, wgt, lists)


def update_kernel(state_ref, transform_ref, out_ref, cells_ref, moved_ref, center_ref):
    groups, levels, _, tiles, per, _ = state_ref.shape
    width = tiles * LANES
    members = groups * per
    pairs = transform_ref.shape[0]

    def enter(z, carry):
        parts = []
        for r in range(2):
            blocks = [[state_ref[j, z, r, t].astype(F32) for j in range(groups)] for t in range(tiles)]
            state = jnp.concatenate([jnp.concatenate(b, 0) for b in blocks], 1)
            center = jnp.sum(state, axis=0, keepdims=True) * (1.0 / members)
            center_ref[z, pl.ds(r, 1), :] = center
            parts.append(state - center)
        cells_ref[pl.ds(pl.multiple_of(z * width, width), width), :] = jnp.concatenate(parts, 0).T
        return carry

    lax.fori_loop(0, levels, enter, 0, unroll=4)

    ident = eye4()
    lane = lax.broadcasted_iota(jnp.int32, (64, 128), 1)
    low = jnp.where(lane < 64, 1.0, 0.0).astype(BF16)

    def apply(g, carry):
        halves = []
        for half in range(2):
            q = g * 2 + half
            halves.append(jnp.concatenate([cells_ref[pl.ds(2 * q + c, levels, stride=width), :] for c in range(2)], 0))
        x = jnp.concatenate(halves, 1)
        t = transform_ref[g]
        on = t * ident
        diag = jnp.sum(on, axis=0, keepdims=True)
        y = x * diag + mul(x.astype(BF16), block_diag((t - on).astype(BF16), low))
        for half in range(2):
            q = g * 2 + half
            for c in range(2):
                moved_ref[pl.ds(2 * q + c, levels, stride=width), :] = y[c * levels : (c + 1) * levels, half * 128 : half * 128 + 128]
        return carry

    lax.fori_loop(0, pairs, apply, 0, unroll=4)

    def leave(z, carry):
        back = moved_ref[pl.ds(pl.multiple_of(z * width, width), width), :].T
        for r in range(2):
            out_ref[z, r] = (back[r * members : (r + 1) * members] + center_ref[z, pl.ds(r, 1), :]).astype(BF16)
        return carry

    lax.fori_loop(0, levels, leave, 0, unroll=4)


def update(state, transform):
    groups, levels, rows, tiles, per, _ = state.shape
    width = tiles * LANES
    return pl.pallas_call(
        update_kernel,
        out_shape=jax.ShapeDtypeStruct((levels, rows, groups * per, width), BF16),
        in_specs=[VMEM, VMEM],
        out_specs=VMEM,
        scratch_shapes=[
            pltpu.VMEM((levels * width, LANES), F32),
            pltpu.VMEM((levels * width, LANES), F32),
            pltpu.VMEM((levels, 8, width), F32),
        ],
        compiler_params=params(48),
        name="update",
    )(state, transform)


def cuts(levels):
    eighth = levels // 8
    ends = [0, eighth, 3 * eighth, 5 * eighth, 7 * eighth, levels]
    return list(zip(ends[:-1], ends[1:]))


def bit_reversed(value, bits):
    return sum(((value >> b) & 1) << (bits - 1 - b) for b in range(bits))


def on_device(prior, coefficients, measured, precision, location, lists, counts, loc_weight):
    slabs = lax.axis_size("slab")
    groups = lax.axis_size("mem")
    bits = groups.bit_length() - 1
    me = lax.axis_index("mem")
    up = [(i, i + 1) for i in range(slabs - 1)]
    down = [(i + 1, i) for i in range(slabs - 1)]
    swap = [(i, i ^ 1) for i in range(slabs)]
    skip = [(i, i + 2) for i in range(0, slabs - 2, 2)] + [(i, i - 2) for i in range(3, slabs, 2)]
    odd = lax.axis_index("slab") % 2 == 1
    columns = prior.shape[3]
    nobs = measured.shape[0]

    levels, members = prior.shape[1], prior.shape[0]
    own = jnp.transpose(prior, (1, 2, 0, 3))
    coef = jnp.transpose(coefficients, (0, 2, 1, 3))
    spans = cuts(levels)
    pieces = [own[first:last].reshape(-1, members, columns) for first, last in spans]
    extra = coef.astype(BF16).reshape(-1, members, columns)
    pieces[0] = jnp.concatenate([pieces[0], extra], 0)
    pieces = lax.optimization_barrier(pieces)
    flag = odd.astype(jnp.int32).reshape(1)
    besides, beyonds, fields = [], [], []

    def advance_piece(i):
        nonlocal cprev, cnext
        if i == 0:
            sides = [x[0][-extra.shape[0] :].reshape(coef.shape).astype(F32) for x in (besides, beyonds)]
            cprev = jnp.where(odd, sides[0][:, 1], sides[1][:, 1])
            cnext = jnp.where(odd, sides[1][:, 0], sides[0][:, 0])
        fields.append(forecast(spans[i], flag, pieces[i], besides[i], beyonds[i], coef, cprev, cnext))

    cprev = cnext = None
    for i, piece in enumerate(pieces):
        if i >= 3:
            advance_piece(i - 3)
            fields[i - 3], piece = lax.optimization_barrier((fields[i - 3], piece))
        besides.append(lax.ppermute(piece, "slab", swap))
        if i >= 2:
            beyonds.append(lax.ppermute(besides[i - 2], "slab", skip))
    beyonds += [lax.ppermute(beside, "slab", skip) for beside in besides[-2:]]
    for i in range(len(fields), len(pieces)):
        advance_piece(i)

    zr, col = location // columns, location % columns
    block = zr * (columns // LANES) + col // LANES
    shift = (jnp.arange(nobs, dtype=jnp.int32) - col) % LANES
    seen = observe(block, shift, fields)
    extras = jnp.stack([measured, precision], 0)
    high = extras.astype(BF16)
    extras = jnp.concatenate([high, (extras - high.astype(F32)).astype(BF16)], 0)
    sent = jnp.concatenate([seen, extras.reshape((-1,) + seen.shape[1:])], 0)
    window = jnp.stack([lax.ppermute(sent, "slab", up), sent, lax.ppermute(sent, "slab", down)], 0)
    obs = window[:, seen.shape[0] :].reshape(3, 2, 2, nobs // LANES, LANES).astype(F32)
    obs = obs[:, 0] + obs[:, 1]
    window = window[:, : seen.shape[0]]
    ens = window[None]
    step = groups // 2
    while step:
        ens = jnp.concatenate([ens, lax.ppermute(ens, "mem", [(i, i ^ step) for i in range(groups)])], 0)
        step //= 2
    slots = bit_reversed(jnp.arange(groups, dtype=jnp.int32) ^ me, bits)

    position = lax.broadcasted_iota(jnp.int32, loc_weight.shape, 2)
    wgt = jnp.where(position < counts[..., None], loc_weight, 0.0)
    transform = transforms(slots, lists, ens, obs, wgt)

    tiles = columns // groups // LANES
    ship = jnp.concatenate(fields, 0)
    ship = ship.reshape(ship.shape[:2] + (groups, tiles) + ship.shape[3:])
    ship, _ = lax.optimization_barrier((jnp.transpose(ship, (2, 0, 1, 3, 4, 5)), ens))
    state = lax.all_to_all(ship, "mem", 0, 0, tiled=False)
    result = update(state, transform)
    return jnp.transpose(result, (2, 0, 1, 3))


def solution(mesh):
    return jax.shard_map(
        on_device,
        mesh=mesh,
        in_specs=(
            P("mem", None, "slab", None),
            P(None, None, "slab", None),
            P("slab"),
            P("slab"),
            P("slab"),
            P("slab", "mem", None),
            P("slab", "mem"),
            P("slab", "mem", None),
        ),
        out_specs=P(None, None, "slab", "mem"),
        check_vma=False,
    )
```

time: 302 us -> 206 us (0.68)
  waiting for transfers between devices: 114 us -> 49.9 us
  Pallas kernels: 135 us -> 96 us
  local copies, waits for them, and re-layouts: 10.5 us -> 19.4 us
  other arithmetic: 7.92 us -> 2.1 us
  starting transfers between devices: 32 us -> 36.9 us
    ppermute x8 -> x12, waiting for transfers between devices: 82.2 us -> 44.4 us  [the longest x5 32.4 us: on_device(): besides.append(lax.ppermute(piece, 'slab', swap))]
    pallas_call x2 -> x6, Pallas kernels: 103 us -> 74.7 us  [the longest x1 58.8 us: transforms(): pl.pallas_call(transform_kernel, out_shape=jax.ShapeDtypeStruct((pairs, 6...]
    ppermute x2, waiting for transfers between devices: 31.7 us -> 5.42 us  [on_device(): lax.ppermute(ens, 'mem', [(i, i ^ step) for i in range(groups)])]
    pallas_call x1, Pallas kernels: 21.7 us -> 11.3 us  [update(): pl.pallas_call(update_kernel, out_shape=jax.ShapeDtypeStruct((levels, row...]
    slice x0 -> x9, local copies, waits for them, and re-layouts: none -> 8.16 us  [the longest x7 6.11 us: on_device(): own[first:last].reshape(-1, members, columns)]
    ppermute x2, starting transfers between devices: 2.32 us -> 7.43 us  [on_device(): lax.ppermute(ens, 'mem', [(i, i ^ step) for i in range(groups)])]
    select_n x1, other arithmetic: 4.51 us -> 0.1 us  [advance_piece(): cnext = jnp.where(odd, sides[1][:, 0], sides[0][:, 0])]
    ppermute x8 -> x12, starting transfers between devices: 23 us -> 25.6 us  [the longest x3 9.59 us: on_device(): beyonds.append(lax.ppermute(besides[i - 2], 'slab', skip))]
  transfers between devices with their start and end apart: 11 -> 15, of which waited for: 5 -> 8; matrix products, arithmetic and copies ran while one was open for 2% -> 3% of each run, Pallas kernels for 30% -> 35%
where the time goes in v2:
time: 206 us; the launch traced here: 205 us
  Pallas kernels  96 us (47%)
  waiting for transfers between devices  49.9 us (24%)
  starting transfers between devices  36.9 us (18%)
  local copies, waits for them, and re-layouts  19.4 us (9%)
  other arithmetic  2.1 us (1%)
    pallas_call x1, Pallas kernels, transforms(): pl.pallas_call(transform_kernel, out_shape=jax.ShapeDtypeStruct((pairs, 6...  58.8 us
    ppermute x5, waiting for transfers between devices, on_device(): besides.append(lax.ppermute(piece, 'slab', swap))  32.4 us
    pallas_call x5, Pallas kernels, forecast(): pl.pallas_call(functools.partial(forecast_kernel, first), out_shape=jax.S...  15.9 us
    pallas_call x1, Pallas kernels, update(): pl.pallas_call(update_kernel, out_shape=jax.ShapeDtypeStruct((levels, row...  11.3 us
    pallas_call x1, Pallas kernels, observe(): pl.pallas_call(observe_kernel, out_shape=jax.ShapeDtypeStruct((block.shap...  9.96 us
    ppermute x3, starting transfers between devices, on_device(): beyonds.append(lax.ppermute(besides[i - 2], 'slab', skip))  9.59 us
    ppermute x2, starting transfers between devices, on_device(): lax.ppermute(ens, 'mem', [(i, i ^ step) for i in range(groups)])  7.43 us
    ppermute x2, starting transfers between devices, on_device(): beyonds += [lax.ppermute(beside, 'slab', skip) for beside in besides[-2:]]  7.19 us
  transfers between devices with their start and end apart: 15, of which 8 were waited for; matrix products, arithmetic and copies ran while one was open for 3% of the time, Pallas kernels for 35%

profile of v2, /device:TPU:9, one launch (start us, length us, event | category | flops | bytes accessed | tf_op | source)
XLA Modules:
  0.0 204.8 jit_solution(45664257434324762)
XLA Ops:
  1.5 2.7 %fusion.17 = (bf16[8,2,16,1024]{3,1,0,2:T(2,128)(2,1)S(1)}, bf16[8,2,16,1024]{3,1,0,2:T(2,128)(2,1)S(1)}, bf16[8,2,16,1024]{3,1,0,2:T(2,128)(2,1)S(1)}) fusion(bf16[32,2,16,1024]{3,1,0,2:T(2,128)(2,1)} %bitcast.101), kind=kLoop, calls=%fused_computation.56 | loop fusion | bytes 3145728 | tf_op jit(solution)/shard_map/slice | solution.py:356
  7.8 14.5 %collective-permute-done.beside_ref = bf16[20,16,1024]{2,1,0:T(8,128)(2,1)} collective-permute-done((bf16[20,16,1024]{2,1,0:T(8,128)(2,1)S(1)}, bf16[20,16,1024]{2,1,0:T(8,128)(2,1)}, u32[]{:S(2)}, u32[]{:S(2)}) %collective-permute-start) | collective-permute-done | bytes 655392 | tf_op jit(solution)/shard_map/ppermute | solution.py:376
  22.2 3.2 %collective-permute-start.1 = (bf16[20,16,1024]{2,1,0:T(8,128)(2,1)}, bf16[20,16,1024]{2,1,0:T(8,128)(2,1)}, u32[]{:S(2)}, u32[]{:S(2)}) collective-permute-start(bf16[20,16,1024]{2,1,0:T(8,128)(2,1)} %collective-permute-done.beside_ref), channel_id=1, source_target_pairs={{0,2},{2,4},{4,6},{3,1},{5,3},{7,5},{8,10},{10,12},{12,14},{11,9},... | collective-permute-start | bytes 1966088 | tf_op jit(solution)/shard_map/ppermute | solution.py:378
  28.4 8.8 %collective-permute-done.2.beside_ref = bf16[16,16,1024]{2,1,0:T(8,128)(2,1)} collective-permute-done((bf16[16,16,1024]{2,1,0:T(8,128)(2,1)S(1)}, bf16[16,16,1024]{2,1,0:T(8,128)(2,1)}, u32[]{:S(2)}, u32[]{:S(2)}) %collective-permute-start.2) | collective-permute-done | bytes 524320 | tf_op jit(solution)/shard_map/ppermute | solution.py:376
  37.2 3.2 %collective-permute-start.3 = (bf16[16,16,1024]{2,1,0:T(8,128)(2,1)}, bf16[16,16,1024]{2,1,0:T(8,128)(2,1)S(1)}, u32[]{:S(2)}, u32[]{:S(2)}) collective-permute-start(bf16[16,16,1024]{2,1,0:T(8,128)(2,1)} %collective-permute-done.2.beside_ref), channel_id=1, source_target_pairs={{0,2},{2,4},{4,6},{3,1},{5,3},{7,5},{8,10},{10,12},{12,14},{11,9},... | collective-permute-start | bytes 1572872 | tf_op jit(solution)/shard_map/ppermute | solution.py:378
  42.8 2.6 %forecast.5 = bf16[4,2,8,16,128]{4,3,2,1,0:T(8,128)(2,1)S(1)} custom-call(s32[1]{0:T(128)} %bitcast.odd_ref, bf16[20,16,1024]{2,1,0:T(8,128)(2,1)S(1)} %pad_maximum_fusion.2.own_ref, bf16[20,16,1024]{2,1,0:T(8,128)(2,1)} %collective-permute-done.beside_ref, bf16[20,16,1024]{2,1,0:T(8,128)(2,1)} %collective-permute-done.1.beyond_ref, ...), custom_call_target="tpu_custom_call" | custom-call | tf_op jit(solution)/shard_map/forecast/pallas_call | solution.py:64
  47.7 3.6 %forecast.6 = bf16[8,2,8,16,128]{4,3,2,1,0:T(8,128)(2,1)S(1)} custom-call(s32[1]{0:T(128)} %bitcast.odd_ref, bf16[16,16,1024]{2,1,0:T(8,128)(2,1)S(1)} %bitcast.94, bf16[16,16,1024]{2,1,0:T(8,128)(2,1)} %collective-permute-done.2.beside_ref, bf16[16,16,1024]{2,1,0:T(8,128)(2,1)S(1)} %collective-permute-done.3.beyond_ref, f32[3,2,32,1024]{3,2,1,0:T(8,128)S(1)} %bitcast.79, ...), custom_call_target="tpu_custom_call" | custom-call | tf_op jit(solution)/shard_map/forecast/pallas_call | solution.py:64
  52.0 3.2 %collective-permute-start.5 = (bf16[16,16,1024]{2,1,0:T(8,128)(2,1)}, bf16[16,16,1024]{2,1,0:T(8,128)(2,1)}, u32[]{:S(2)}, u32[]{:S(2)}) collective-permute-start(bf16[16,16,1024]{2,1,0:T(8,128)(2,1)} %collective-permute-done.4.beside_ref), channel_id=1, source_target_pairs={{0,2},{2,4},{4,6},{3,1},{5,3},{7,5},{8,10},{10,12},{12,14},{11,9},... | collective-permute-start | bytes 1572872 | tf_op jit(solution)/shard_map/ppermute | solution.py:378
  55.2 9.1 %collective-permute-done.8.beside_ref = bf16[8,16,1024]{2,1,0:T(8,128)(2,1)} collective-permute-done((bf16[8,16,1024]{2,1,0:T(8,128)(2,1)S(1)}, bf16[8,16,1024]{2,1,0:T(8,128)(2,1)}, u32[]{:S(2)}, u32[]{:S(2)}) %collective-permute-start.8) | collective-permute-done | bytes 262176 | tf_op jit(solution)/shard_map/ppermute | solution.py:376
  64.2 4.0 %collective-permute-start.9 = (bf16[8,16,1024]{2,1,0:T(8,128)(2,1)}, bf16[8,16,1024]{2,1,0:T(8,128)(2,1)}, u32[]{:S(2)}, u32[]{:S(2)}) collective-permute-start(bf16[8,16,1024]{2,1,0:T(8,128)(2,1)} %collective-permute-done.8.beside_ref), channel_id=1, source_target_pairs={{0,2},{2,4},{4,6},{3,1},{5,3},{7,5},{8,10},{10,12},{12,14},{11,9},... | collective-permute-start | bytes 786440 | tf_op jit(solution)/shard_map/ppermute | solution.py:379
  68.3 3.2 %collective-permute-start.7 = (bf16[16,16,1024]{2,1,0:T(8,128)(2,1)}, bf16[16,16,1024]{2,1,0:T(8,128)(2,1)}, u32[]{:S(2)}, u32[]{:S(2)}) collective-permute-start(bf16[16,16,1024]{2,1,0:T(8,128)(2,1)} %collective-permute-done.6.beside_ref), channel_id=1, source_target_pairs={{0,2},{2,4},{4,6},{3,1},{5,3},{7,5},{8,10},{10,12},{12,14},{11,9},... | collective-permute-start | bytes 1572872 | tf_op jit(solution)/shard_map/ppermute | solution.py:379
  72.2 3.8 %forecast.7 = bf16[8,2,8,16,128]{4,3,2,1,0:T(8,128)(2,1)S(1)} custom-call(s32[1]{0:T(128)} %bitcast.odd_ref, bf16[16,16,1024]{2,1,0:T(8,128)(2,1)S(1)} %bitcast.92, bf16[16,16,1024]{2,1,0:T(8,128)(2,1)} %collective-permute-done.4.beside_ref, bf16[16,16,1024]{2,1,0:T(8,128)(2,1)} %collective-permute-done.5.beyond_ref, f32[3,2,32,1024]{3,2,1,0:T(8,128)S(1)} %bitcast.80, ...), custom_call_target="tpu_custom_call" | custom-call | tf_op jit(solution)/shard_map/forecast/pallas_call | solution.py:64
  76.0 2.3 %forecast.9 = bf16[4,2,8,16,128]{4,3,2,1,0:T(8,128)(2,1)S(1)} custom-call(s32[1]{0:T(128)} %bitcast.odd_ref, bf16[8,16,1024]{2,1,0:T(8,128)(2,1)S(1)} %bitcast.96, bf16[8,16,1024]{2,1,0:T(8,128)(2,1)} %collective-permute-done.8.beside_ref, bf16[8,16,1024]{2,1,0:T(8,128)(2,1)} %collective-permute-done.9.beyond_ref, f32[3,2,32,1024]{3,2,1,0:T(8,128)S(1)} %bitcast.81, ...), custom_call_target="tpu_custom_call" | custom-call | tf_op jit(solution)/shard_map/forecast/pallas_call | solution.py:64
  78.3 5.9 %collective-permute-done.7.beyond_ref = bf16[16,16,1024]{2,1,0:T(8,128)(2,1)} collective-permute-done((bf16[16,16,1024]{2,1,0:T(8,128)(2,1)}, bf16[16,16,1024]{2,1,0:T(8,128)(2,1)}, u32[]{:S(2)}, u32[]{:S(2)}) %collective-permute-start.7) | collective-permute-done | bytes 524320 | tf_op jit(solution)/shard_map/ppermute | solution.py:379
  84.2 3.7 %forecast.8 = bf16[8,2,8,16,128]{4,3,2,1,0:T(8,128)(2,1)S(1)} custom-call(s32[1]{0:T(128)} %bitcast.odd_ref, bf16[16,16,1024]{2,1,0:T(8,128)(2,1)S(1)} %bitcast.90, bf16[16,16,1024]{2,1,0:T(8,128)(2,1)} %collective-permute-done.6.beside_ref, bf16[16,16,1024]{2,1,0:T(8,128)(2,1)} %collective-permute-done.7.beyond_ref, f32[3,2,32,1024]{3,2,1,0:T(8,128)S(1)} %bitcast.82, ...), custom_call_target="tpu_custom_call" | custom-call | tf_op jit(solution)/shard_map/forecast/pallas_call | solution.py:64
  87.9 10.0 %observe.1 = bf16[32,16,128]{2,1,0:T(8,128)(2,1)S(1)} custom-call(s32[4096]{0:T(1024)S(1)} %get-tuple-element.35.block_ref, s32[4096]{0:T(1024)S(1)} %get-tuple-element.34.shift_ref, bf16[64,16,128]{2,1,0:T(8,128)(2,1)S(1)} %bitcast.87, bf16[128,16,128]{2,1,0:T(8,128)(2,1)S(1)} %bitcast.84, bf16[128,16,128]{2,1,0:T(8,128)(2,1)S(1)} %bitcast.85, ...), custom_call_target="tpu_custom_call" | custom-call | tf_op jit(solution)/shard_map/observe/pallas_call | solution.py:99
  100.1 3.1 %collective-permute-start.10 = (bf16[40,16,128]{2,1,0:T(8,128)(2,1)S(1)}, bf16[40,16,128]{2,1,0:T(8,128)(2,1)S(1)}, u32[]{:S(2)}, u32[]{:S(2)}) collective-permute-start(bf16[40,16,128]{2,1,0:T(8,128)(2,1)S(1)} %get-tuple-element.33), channel_id=1, source_target_pairs={{0,1},{1,2},{2,3},{3,4},{4,5},{5,6},{6,7},{8,9},{9,10},{10,11},{11... | collective-permute-start | bytes 491528 | tf_op jit(solution)/shard_map/ppermute | solution.py:391
  104.0 3.2 %collective-permute-done.10 = bf16[40,16,128]{2,1,0:T(8,128)(2,1)S(1)} collective-permute-done((bf16[40,16,128]{2,1,0:T(8,128)(2,1)S(1)}, bf16[40,16,128]{2,1,0:T(8,128)(2,1)S(1)}, u32[]{:S(2)}, u32[]{:S(2)}) %collective-permute-start.10) | collective-permute-done | bytes 163872 | tf_op jit(solution)/shard_map/ppermute | solution.py:391
  108.6 5.4 %collective-permute-done.12 = bf16[1,3,32,16,128]{4,3,2,1,0:T(8,128)(2,1)S(1)} collective-permute-done((bf16[1,3,32,16,128]{4,3,2,1,0:T(8,128)(2,1)S(1)}, bf16[1,3,32,16,128]{4,3,2,1,0:T(8,128)(2,1)S(1)}, u32[]{:S(2)}, u32[]{:S(2)}) %collective-permute-start.12) | collective-permute-done | bytes 393248 | tf_op jit(solution)/shard_map/ppermute | solution.py:398
  114.1 6.2 %collective-permute-start.13 = (bf16[2,3,32,16,128]{4,3,2,1,0:T(8,128)(2,1)S(1)}, bf16[2,3,32,16,128]{4,3,2,1,0:T(8,128)(2,1)S(1)}, u32[]{:S(2)}, u32[]{:S(2)}) collective-permute-start(bf16[2,3,32,16,128]{4,3,2,1,0:T(8,128)(2,1)S(1)} %pad_maximum_fusion.1), channel_id=1, source_target_pairs={{0,8},{8,0},{16,24},{24,16},{1,9},{9,1},{17,25},{25,17},{2,10},{10... | collective-permute-start | bytes 2359304 | tf_op jit(solution)/shard_map/ppermute | solution.py:398
  123.9 3.9 %all-to-all-start = ((bf16[4,32,2,2,16,128]{5,4,3,2,1,0:T(8,128)(2,1)}), bf16[4,32,2,2,16,128]{5,4,3,2,1,0:T(8,128)(2,1)S(1)}, u32[]{:S(2)}, u32[]{:S(2)}) async-start(bf16[4,32,2,2,16,128]{5,4,3,2,1,0:T(8,128)(2,1)} %bitcast.98), calls=%async_computation | async-start | bytes 4194304 | tf_op jit(solution)/shard_map/all_to_all | solution.py:410
  129.2 58.8 %transforms.1.transform_ref = f32[64,64,256]{2,1,0:T(8,128)S(1)} custom-call(s32[4]{0:T(128)S(1)} %shift-left_add_fusion.slot_ref, bf16[4,3,32,16,128]{4,3,2,1,0:T(8,128)(2,1)S(1)} %copy-done.1, f32[3,2,32,128]{3,2,1,0:T(8,128)S(1)} %fusion.6.obs_ref, f32[2,128,128]{2,1,0:T(8,128)S(1)} %fusion.4.wgt_ref, s32[16,16,128]{2,1,0:T(8,128)S(1)} %bitcast.97), custom_call_target="tpu_custom_call" | custom-call | tf_op jit(solution)/shard_map/transforms/pallas_call | solution.py:242
  190.0 11.3 %update.1 = bf16[32,2,64,256]{3,2,1,0:T(8,128)(2,1)S(1)} custom-call(bf16[4,32,2,2,16,128]{5,4,3,2,1,0:T(8,128)(2,1)S(1)} %all-to-all-done.state_ref, f32[64,64,256]{2,1,0:T(8,128)} %copy-done), custom_call_target="tpu_custom_call" | custom-call | tf_op jit(solution)/shard_map/update/pallas_call | solution.py:314
  201.3 3.5 %copy.31 = bf16[64,32,2,256]{3,2,1,0:T(2,128)(2,1)} copy(bf16[64,32,2,256]{3,0,2,1:T(8,128)(2,1)S(1)} %bitcast.83) | data formatting | bytes 4194304 | tf_op jit(solution)/shard_map/transpose | solution.py:412
  (80 shorter events, 25.2 us)
Async XLA Ops:
  0.0 4.2 %copy-start.6 = (f32[3,32,2,1024]{3,2,1,0:T(2,128)S(1)}, f32[3,32,2,1024]{3,2,1,0:T(2,128)}, u32[]{:S(2)}) copy-start(f32[3,32,2,1024]{3,2,1,0:T(2,128)} %param.9) | copy-start | bytes 2359300
  4.9 23.4 %copy-start.2 = (bf16[8,2,16,1024]{3,2,1,0:T(8,128)(2,1)}, bf16[8,2,16,1024]{3,2,1,0:T(8,128)(2,1)S(1)}, u32[]{:S(2)}) copy-start(bf16[8,2,16,1024]{3,2,1,0:T(8,128)(2,1)S(1)} %copy.19) | copy-start | bytes 1572868
  6.5 15.8 %collective-permute-start = (bf16[20,16,1024]{2,1,0:T(8,128)(2,1)S(1)}, bf16[20,16,1024]{2,1,0:T(8,128)(2,1)}, u32[]{:S(2)}, u32[]{:S(2)}) collective-permute-start(bf16[20,16,1024]{2,1,0:T(8,128)(2,1)S(1)} %pad_maximum_fusion.2.own_ref), channel_id=1, source_target_pairs={{0,1},{1,0},{2,3},{3,2},{4,5},{5,4},{6,7},{7,6},{8,9},{9,8},{10,11... | collective-permute-start | bytes 1966088 | tf_op jit(solution)/shard_map/ppermute | solution.py:376
  22.2 19.3 %collective-permute-start.1 = (bf16[20,16,1024]{2,1,0:T(8,128)(2,1)}, bf16[20,16,1024]{2,1,0:T(8,128)(2,1)}, u32[]{:S(2)}, u32[]{:S(2)}) collective-permute-start(bf16[20,16,1024]{2,1,0:T(8,128)(2,1)} %collective-permute-done.beside_ref), channel_id=1, source_target_pairs={{0,2},{2,4},{4,6},{3,1},{5,3},{7,5},{8,10},{10,12},{12,14},{11,9},... | collective-permute-start | bytes 1966088 | tf_op jit(solution)/shard_map/ppermute | solution.py:378
  25.4 11.8 %collective-permute-start.2 = (bf16[16,16,1024]{2,1,0:T(8,128)(2,1)S(1)}, bf16[16,16,1024]{2,1,0:T(8,128)(2,1)}, u32[]{:S(2)}, u32[]{:S(2)}) collective-permute-start(bf16[16,16,1024]{2,1,0:T(8,128)(2,1)S(1)} %bitcast.93), channel_id=1, source_target_pairs={{0,1},{1,0},{2,3},{3,2},{4,5},{5,4},{6,7},{7,6},{8,9},{9,8},{10,11... | collective-permute-start | bytes 1572872 | tf_op jit(solution)/shard_map/ppermute | solution.py:376
  25.6 26.3 %collective-permute-start.4 = (bf16[16,16,1024]{2,1,0:T(8,128)(2,1)S(1)}, bf16[16,16,1024]{2,1,0:T(8,128)(2,1)}, u32[]{:S(2)}, u32[]{:S(2)}) collective-permute-start(bf16[16,16,1024]{2,1,0:T(8,128)(2,1)S(1)} %bitcast.91), channel_id=1, source_target_pairs={{0,1},{1,0},{2,3},{3,2},{4,5},{5,4},{6,7},{7,6},{8,9},{9,8},{10,11... | collective-permute-start | bytes 1572872 | tf_op jit(solution)/shard_map/ppermute | solution.py:376
  37.2 10.5 %collective-permute-start.3 = (bf16[16,16,1024]{2,1,0:T(8,128)(2,1)}, bf16[16,16,1024]{2,1,0:T(8,128)(2,1)S(1)}, u32[]{:S(2)}, u32[]{:S(2)}) collective-permute-start(bf16[16,16,1024]{2,1,0:T(8,128)(2,1)} %collective-permute-done.2.beside_ref), channel_id=1, source_target_pairs={{0,2},{2,4},{4,6},{3,1},{5,3},{7,5},{8,10},{10,12},{12,14},{11,9},... | collective-permute-start | bytes 1572872 | tf_op jit(solution)/shard_map/ppermute | solution.py:378
  42.8 5.0 %copy-start.3 = (bf16[8,2,16,1024]{3,2,1,0:T(8,128)(2,1)S(1)}, bf16[8,2,16,1024]{3,2,1,0:T(8,128)(2,1)}, u32[]{:S(2)}) copy-start(bf16[8,2,16,1024]{3,2,1,0:T(8,128)(2,1)} %copy-done.2) | copy-start | bytes 1572868
  45.4 5.9 %copy-start.4 = (bf16[4,2,16,1024]{3,2,1,0:T(8,128)(2,1)S(1)}, bf16[4,2,16,1024]{3,2,1,0:T(8,128)(2,1)}, u32[]{:S(2)}) copy-start(bf16[4,2,16,1024]{3,2,1,0:T(8,128)(2,1)} %copy.22) | copy-start | bytes 786436
  45.4 26.8 %copy-start.12 = (s32[4096]{0:T(1024)S(1)}, s32[4096]{0:T(1024)}, u32[]{:S(2)}) copy-start(s32[4096]{0:T(1024)} %param.12) | copy-start | bytes 49156
  45.4 22.8 %collective-permute-start.6 = (bf16[16,16,1024]{2,1,0:T(8,128)(2,1)S(1)}, bf16[16,16,1024]{2,1,0:T(8,128)(2,1)}, u32[]{:S(2)}, u32[]{:S(2)}) collective-permute-start(bf16[16,16,1024]{2,1,0:T(8,128)(2,1)S(1)} %bitcast.89), channel_id=1, source_target_pairs={{0,1},{1,0},{2,3},{3,2},{4,5},{5,4},{6,7},{7,6},{8,9},{9,8},{10,11... | collective-permute-start | bytes 1572872 | tf_op jit(solution)/shard_map/ppermute | solution.py:376
  51.3 12.9 %collective-permute-start.8 = (bf16[8,16,1024]{2,1,0:T(8,128)(2,1)S(1)}, bf16[8,16,1024]{2,1,0:T(8,128)(2,1)}, u32[]{:S(2)}, u32[]{:S(2)}) collective-permute-start(bf16[8,16,1024]{2,1,0:T(8,128)(2,1)S(1)} %bitcast.95), channel_id=1, source_target_pairs={{0,1},{1,0},{2,3},{3,2},{4,5},{5,4},{6,7},{7,6},{8,9},{9,8},{10,11... | collective-permute-start | bytes 786440 | tf_op jit(solution)/shard_map/ppermute | solution.py:376
  52.0 20.3 %collective-permute-start.5 = (bf16[16,16,1024]{2,1,0:T(8,128)(2,1)}, bf16[16,16,1024]{2,1,0:T(8,128)(2,1)}, u32[]{:S(2)}, u32[]{:S(2)}) collective-permute-start(bf16[16,16,1024]{2,1,0:T(8,128)(2,1)} %collective-permute-done.4.beside_ref), channel_id=1, source_target_pairs={{0,2},{2,4},{4,6},{3,1},{5,3},{7,5},{8,10},{10,12},{12,14},{11,9},... | collective-permute-start | bytes 1572872 | tf_op jit(solution)/shard_map/ppermute | solution.py:378
  64.2 11.7 %collective-permute-start.9 = (bf16[8,16,1024]{2,1,0:T(8,128)(2,1)}, bf16[8,16,1024]{2,1,0:T(8,128)(2,1)}, u32[]{:S(2)}, u32[]{:S(2)}) collective-permute-start(bf16[8,16,1024]{2,1,0:T(8,128)(2,1)} %collective-permute-done.8.beside_ref), channel_id=1, source_target_pairs={{0,2},{2,4},{4,6},{3,1},{5,3},{7,5},{8,10},{10,12},{12,14},{11,9},... | collective-permute-start | bytes 786440 | tf_op jit(solution)/shard_map/ppermute | solution.py:379
  68.3 15.9 %collective-permute-start.7 = (bf16[16,16,1024]{2,1,0:T(8,128)(2,1)}, bf16[16,16,1024]{2,1,0:T(8,128)(2,1)}, u32[]{:S(2)}, u32[]{:S(2)}) collective-permute-start(bf16[16,16,1024]{2,1,0:T(8,128)(2,1)} %collective-permute-done.6.beside_ref), channel_id=1, source_target_pairs={{0,2},{2,4},{4,6},{3,1},{5,3},{7,5},{8,10},{10,12},{12,14},{11,9},... | collective-permute-start | bytes 1572872 | tf_op jit(solution)/shard_map/ppermute | solution.py:379
  78.3 19.6 %copy-start.9 = (bf16[8,16,128]{2,1,0:T(8,128)(2,1)S(1)}, bf16[8,16,128]{2,1,0:T(8,128)(2,1)}, u32[]{:S(2)}) copy-start(bf16[8,16,128]{2,1,0:T(8,128)(2,1)} %reshape.79) | copy-start | bytes 98308
  97.9 6.1 %collective-permute-start.11 = (bf16[40,16,128]{2,1,0:T(8,128)(2,1)S(1)}, bf16[40,16,128]{2,1,0:T(8,128)(2,1)S(1)}, u32[]{:S(2)}, u32[]{:S(2)}) collective-permute-start(bf16[40,16,128]{2,1,0:T(8,128)(2,1)S(1)} %get-tuple-element.33), channel_id=1, source_target_pairs={{1,0},{2,1},{3,2},{4,3},{5,4},{6,5},{7,6},{9,8},{10,9},{11,10},{12... | collective-permute-start | bytes 491528 | tf_op jit(solution)/shard_map/ppermute | solution.py:391
  100.1 7.1 %collective-permute-start.10 = (bf16[40,16,128]{2,1,0:T(8,128)(2,1)S(1)}, bf16[40,16,128]{2,1,0:T(8,128)(2,1)S(1)}, u32[]{:S(2)}, u32[]{:S(2)}) collective-permute-start(bf16[40,16,128]{2,1,0:T(8,128)(2,1)S(1)} %get-tuple-element.33), channel_id=1, source_target_pairs={{0,1},{1,2},{2,3},{3,4},{4,5},{5,6},{6,7},{8,9},{9,10},{10,11},{11... | collective-permute-start | bytes 491528 | tf_op jit(solution)/shard_map/ppermute | solution.py:391
  107.3 6.7 %collective-permute-start.12 = (bf16[1,3,32,16,128]{4,3,2,1,0:T(8,128)(2,1)S(1)}, bf16[1,3,32,16,128]{4,3,2,1,0:T(8,128)(2,1)S(1)}, u32[]{:S(2)}, u32[]{:S(2)}) collective-permute-start(bf16[1,3,32,16,128]{4,3,2,1,0:T(8,128)(2,1)S(1)} %slice_bitcast_fusion), channel_id=1, source_target_pairs={{0,16},{8,24},{16,0},{24,8},{1,17},{9,25},{17,1},{25,9},{2,18},{10... | collective-permute-start | bytes 1179656 | tf_op jit(solution)/shard_map/ppermute | solution.py:398
  114.1 8.4 %collective-permute-start.13 = (bf16[2,3,32,16,128]{4,3,2,1,0:T(8,128)(2,1)S(1)}, bf16[2,3,32,16,128]{4,3,2,1,0:T(8,128)(2,1)S(1)}, u32[]{:S(2)}, u32[]{:S(2)}) collective-permute-start(bf16[2,3,32,16,128]{4,3,2,1,0:T(8,128)(2,1)S(1)} %pad_maximum_fusion.1), channel_id=1, source_target_pairs={{0,8},{8,0},{16,24},{24,16},{1,9},{9,1},{17,25},{25,17},{2,10},{10... | collective-permute-start | bytes 2359304 | tf_op jit(solution)/shard_map/ppermute | solution.py:398
  123.9 3.9 %copy-start.7 = (s32[2,128,128]{2,1,0:T(8,128)S(1)}, s32[2,128,128]{2,1,0:T(8,128)}, u32[]{:S(2)}) copy-start(s32[2,128,128]{2,1,0:T(8,128)} %param.13) | copy-start | bytes 393220
  123.9 4.1 %copy-start.8 = (f32[2,128,128]{2,1,0:T(8,128)S(1)}, f32[2,128,128]{2,1,0:T(8,128)}, u32[]{:S(2)}) copy-start(f32[2,128,128]{2,1,0:T(8,128)} %param.15) | copy-start | bytes 393220
  123.9 4.1 %copy-start.13 = (s32[2,128]{1,0:T(2,128)S(1)}, s32[2,128]{1,0:T(2,128)}, u32[]{:S(2)}) copy-start(s32[2,128]{1,0:T(2,128)} %param.14) | copy-start | bytes 3076
  123.9 66.1 %all-to-all-start = ((bf16[4,32,2,2,16,128]{5,4,3,2,1,0:T(8,128)(2,1)}), bf16[4,32,2,2,16,128]{5,4,3,2,1,0:T(8,128)(2,1)S(1)}, u32[]{:S(2)}, u32[]{:S(2)}) async-start(bf16[4,32,2,2,16,128]{5,4,3,2,1,0:T(8,128)(2,1)} %bitcast.98), calls=%async_computation | async-start | bytes 4194304 | tf_op jit(solution)/shard_map/all_to_all | solution.py:410
  (5 other events, 12.7 us)

commit v3 on v2

--- a/solution.py
+++ b/solution.py
@@ -71,40 +71,64 @@
     )(odd, own, beside, beyond, coef, cprev, cnext)
 
 
-def observe_kernel(block_ref, shift_ref, *refs):
-    *part_refs, out_ref, field_ref = refs
+BATCH = 4
+
+
+def observe_kernel(index_ref, *refs):
+    *part_refs, out_ref, field_ref, smem_a, smem_b, sems = refs
+    smem = (smem_a, smem_b)
+    count = index_ref.shape[0]
+    members = out_ref.shape[1]
+    lane = lax.broadcasted_iota(jnp.int32, (members, LANES), 1)
+
+    def fetch(b, half):
+        return pltpu.make_async_copy(index_ref.at[b], smem[half], sems.at[half])
+
+    for half in range(2):
+        fetch(half, half).start()
     first = 0
     for part in part_refs:
         field_ref[first : first + part.shape[0]] = part[...]
         first += part.shape[0]
-    count = out_ref.shape[0]
-    members = out_ref.shape[1]
-    lane = lax.broadcasted_iota(jnp.int32, (members, LANES), 1)
-
-    def one(b, carry):
-        acc = jnp.zeros((members, LANES), F32)
-        for i in range(LANES):
-            o = b * LANES + i
-            tile = field_ref[block_ref[o]].astype(F32)
-            acc = jnp.where(lane == i, pltpu.roll(tile, shift_ref[o], 1), acc)
-        out_ref[b] = acc.astype(BF16)
-        return carry
-
-    lax.fori_loop(0, count, one, 0)
+
+    def pair(i, carry):
+        for half in range(2):
+            b = 2 * i + half
+            fetch(b, half).wait()
+            for j in range(BATCH):
+                acc = jnp.zeros((members, LANES), F32)
+                for o in range(LANES):
+                    tile = field_ref[smem[half][2 * j, o]].astype(F32)
+                    acc = jnp.where(lane == o, pltpu.roll(tile, smem[half][2 * j + 1, o], 1), acc)
+                out_ref[b * BATCH + j] = acc.astype(BF16)
+
+            @pl.when(b + 2 < count)
+            def _():
+                fetch(b + 2, half).start()
+
+        return carry
+
+    lax.fori_loop(0, count // 2, pair, 0)
 
 
 def observe(block, shift, fields):
     parts = [f.reshape((-1,) + f.shape[3:]) for f in fields]
     members = parts[0].shape[1]
+    index = jnp.stack([block.reshape(-1, LANES), shift.reshape(-1, LANES)], 1).reshape(-1, 2 * BATCH, LANES)
     return pl.pallas_call(
         observe_kernel,
         out_shape=jax.ShapeDtypeStruct((block.shape[0] // LANES, members, LANES), BF16),
-        in_specs=[SMEM, SMEM] + [VMEM] * len(parts),
+        in_specs=[VMEM] + [VMEM] * len(parts),
         out_specs=VMEM,
-        scratch_shapes=[pltpu.VMEM((sum(p.shape[0] for p in parts), members, LANES), BF16)],
+        scratch_shapes=[
+            pltpu.VMEM((sum(p.shape[0] for p in parts), members, LANES), BF16),
+            pltpu.SMEM((2 * BATCH, LANES), jnp.int32),
+            pltpu.SMEM((2 * BATCH, LANES), jnp.int32),
+            pltpu.SemaphoreType.DMA((2,)),
+        ],
         compiler_params=params(32),
         name="observe",
-    )(block, shift, *parts)
+    )(index, *parts)
 
 
 def eye4():
@@ -126,61 +150,88 @@
     return jnp.dot(a, b, preferred_element_type=F32)
 
 
+LEAD = 120
 GROUPS = 4
 
 
-def gather_block(lists_ref, wgt_ref, first, cat_ref, rows_ref, sq_ref, force_ref, scale_ref, ident, lower, inflated):
-    for q in range(2 * GROUPS):
-        grams = []
-        bounds = []
+def gather_rows(q, lists_ref, cat_ref, rows_ref):
+    for l in range(LANES):
         for r in range(2):
-            p = (2 * q + r) % rows_ref.shape[0]
-            for l in range(LANES):
-                rows_ref[p, pl.ds(l, 1), :] = cat_ref[pl.ds(lists_ref[2 * q + r, l], 1), :]
-            rows = rows_ref[p]
-            weighted = rows.T[:64] * wgt_ref[r, pl.ds(first + q, 1), :]
-            both = mul(weighted.astype(BF16), rows.astype(BF16))
-            total = jnp.sum(jnp.where(lower, jnp.abs(both), 0.0), axis=0, keepdims=True)
-            bounds.append(inflated + jnp.max(total, axis=1, keepdims=True))
-            grams.append(both)
-        turned = [pltpu.roll(x, 64, 1) for x in grams]
-        inv = 1.0 / jnp.where(lower[:1], bounds[0], bounds[1])
-        gram = jnp.where(lower, grams[0], turned[1])
-        force = jnp.where(lower, turned[0], grams[1])
-        g, half = q // 2, q % 2
-        sl = slice(half * 128, half * 128 + 128)
-        sq_ref[g, :, sl] = (gram + inflated * ident[:, :128]) * inv
-        force_ref[g, :, sl] = force.astype(BF16)
-        scale_ref[g, :, sl] = jnp.broadcast_to(inv, (8, 128))
-
-
-def solve_block(sq_ref, force_ref, scale_ref, out_ref, first, ident, low, members):
-    n = range(GROUPS)
-    sq = [sq_ref[g] for g in n]
-    h = [(1.5 - SHIFT) * ident - 0.5 * x for x in sq]
-    inv = [SHIFT * ident + x for x in h]
-    bd = [block_diag(x.astype(BF16), low) for x in h]
-    sq = [SHIFT * sq[u] + mul(sq[u].astype(BF16), bd[u]) for u in n]
-    for sweep in range(1, NS_ITERS):
-        m = [mul(inv[u].astype(BF16), block_diag(sq[u].astype(BF16), low)) for u in n]
-        bd = [block_diag(((1.5 - SHIFT) * ident - 0.5 * x).astype(BF16), low) for x in m]
-        if sweep < NS_ITERS - 1:
-            both = [jnp.concatenate([sq[u], inv[u]], 0) for u in n]
-            both = [SHIFT * both[u] + mul(both[u].astype(BF16), bd[u]) for u in n]
-            sq = [x[:64] for x in both]
-            inv = [x[64:] for x in both]
-        else:
-            inv = [SHIFT * inv[u] + mul(inv[u].astype(BF16), bd[u]) for u in n]
-    lhs = [x.astype(BF16) for x in inv]
-    f = [mul(lhs[u], block_diag(force_ref[u], low)) for u in n]
-    f = [mul(lhs[u], block_diag(f[u].astype(BF16), low)) for u in n]
-    for u in n:
-        scale = scale_ref[u][:1]
-        out_ref[first + u] = (math.sqrt(members - 1.0) * jnp.sqrt(scale)) * inv[u] + scale * f[u]
+            rows_ref[q % 2, r, pl.ds(l, 1), :] = cat_ref[pl.ds(lists_ref[2 * q + r, l], 1), :]
+        yield
+
+
+def gram_pair(q, rows_ref, wgt_ref, first, work, consts):
+    sq_ref, force_ref, scale_ref = work
+    ident, lower, _, inflated = consts
+    bounds = []
+    rows = [rows_ref[q % 2, r] for r in range(2)]
+    weighted = [(rows[r].T[:64] * wgt_ref[r, pl.ds(first + q, 1), :]).astype(BF16) for r in range(2)]
+    yield
+    grams = [mul(weighted[r], rows[r].astype(BF16)) for r in range(2)]
+    yield
+    for both in grams:
+        total = jnp.sum(jnp.where(lower, jnp.abs(both), 0.0), axis=0, keepdims=True)
+        bounds.append(inflated + jnp.max(total, axis=1, keepdims=True))
+    turned = [pltpu.roll(x, 64, 1) for x in grams]
+    inv = 1.0 / jnp.where(lower[:1], bounds[0], bounds[1])
+    gram = jnp.where(lower, grams[0], turned[1])
+    force = jnp.where(lower, turned[0], grams[1])
+    sl = slice(q % 2 * 128, q % 2 * 128 + 128)
+    sq_ref[q // 2, :, sl] = (gram + inflated * ident[:, :128]) * inv
+    force_ref[q // 2, :, sl] = force.astype(BF16)
+    scale_ref[q // 2, :, sl] = jnp.broadcast_to(inv, (8, 128))
+
+
+def solve_stage(u, stage, held, work, consts, out_ref, first, members):
+    state_ref, factor_ref = held
+    sq_ref, force_ref, scale_ref = work
+    ident, _, low, _ = consts
+    last = 2 * NS_ITERS
+    if stage == 0:
+        h = (1.5 - SHIFT) * ident - 0.5 * sq_ref[u]
+        product = mul(sq_ref[u].astype(BF16), block_diag(h.astype(BF16), low))
+        yield
+        state_ref[u, 64:] = SHIFT * ident + (1.5 - SHIFT) * ident - 0.5 * sq_ref[u]
+        state_ref[u, :64] = SHIFT * sq_ref[u] + product
+    elif stage < last - 1 and stage % 2 == 1:
+        square = mul(state_ref[u, 64:].astype(BF16), block_diag(state_ref[u, :64].astype(BF16), low))
+        yield
+        factor_ref[u] = ((1.5 - SHIFT) * ident - 0.5 * square).astype(BF16)
+    elif stage < last - 1:
+        sl = slice(0 if stage < last - 2 else 64, 128)
+        product = mul(state_ref[u, sl].astype(BF16), block_diag(factor_ref[u], low))
+        yield
+        state_ref[u, sl] = SHIFT * state_ref[u, sl] + product
+    elif stage == last - 1:
+        product = mul(state_ref[u, 64:].astype(BF16), block_diag(force_ref[u], low))
+        yield
+        factor_ref[u] = product.astype(BF16)
+    else:
+        shift = mul(state_ref[u, 64:].astype(BF16), block_diag(factor_ref[u], low))
+        yield
+        scale = scale_ref[u, :1]
+        out_ref[first + u] = (math.sqrt(members - 1.0) * jnp.sqrt(scale)) * state_ref[u, 64:] + scale * shift
+
+
+def run(steps, filler, share):
+    for unit in steps:
+        next(unit, None)
+        for _ in range(share):
+            next(filler, None)
+
+
+def segment(units, gram, filler):
+    middle = len(units) // 2
+    begin = [gram] + units[:middle] + [gram] + units[middle:]
+    run(begin, filler, LEAD // len(begin))
+    run(units + [gram], filler, (LANES - LEAD) // (len(units) + 1) + 1)
+    for _ in filler:
+        pass
 
 
 def transform_kernel(slot_ref, ens_ref, obs_ref, wgt_ref, lists_ref, out_ref, cat_ref, rows_ref, *scratch):
-    work, (lists_a, lists_b, sems) = (scratch[:3], scratch[3:6]), scratch[6:]
+    work, (lists_a, lists_b, sems), held = (scratch[:3], scratch[3:6]), scratch[6:9], scratch[9:]
     smem = (lists_a, lists_b)
     groups = slot_ref.shape[0]
     _, windows, blocks, per, _ = ens_ref.shape
@@ -207,17 +258,34 @@
 
     lax.fori_loop(0, windows * blocks, catalog, 0, unroll=4)
 
-    ident = eye4()
-    lane = lax.broadcasted_iota(jnp.int32, (64, 128), 1)
-    lower = lane < 64
-    low = jnp.where(lower, 1.0, 0.0).astype(BF16)
-
-    def pair(i, carry):
+    lower = lax.broadcasted_iota(jnp.int32, (64, 128), 1) < 64
+    consts = (eye4(), lower, jnp.where(lower, 1.0, 0.0).astype(BF16), inflated)
+    pairs = 2 * GROUPS
+    last = 2 * NS_ITERS
+
+    def solve(stage, block, half):
+        at = jnp.maximum(block, 0) * GROUPS
+        return [solve_stage(u, stage, held, work[half], consts, out_ref, at, members) for u in range(GROUPS)]
+
+    def gram(q, block, half):
+        return gram_pair(q, rows_ref, wgt_ref, jnp.maximum(block, 0) * pairs, work[half], consts)
+
+    def step(i, carry):
         for half in range(2):
             b = 2 * i + half
-            fetch(b, half).wait()
-            solve_block(*work[1 - half], out_ref, jnp.maximum(b - 1, 0) * GROUPS, ident, low, members)
-            gather_block(smem[half], wgt_ref, b * 2 * GROUPS, cat_ref, rows_ref, *work[half], ident, lower, inflated)
+            for q in range(pairs):
+
+                @pl.when(slot_ref[0] >= 0)
+                def _():
+                    if q == 0:
+                        fetch(b, half).wait()
+                        units = solve(last - 1, b - 2, half)
+                        before = gram(pairs - 1, b - 1, 1 - half)
+                    else:
+                        units = solve(last, b - 2, half) if q == 1 else []
+                        units += solve(q - 1, b - 1, 1 - half)
+                        before = gram(q - 1, b, half)
+                    segment(units, before, gather_rows(q, smem[half], cat_ref, rows_ref))
 
             @pl.when(b + 2 < count)
             def _():
@@ -225,8 +293,16 @@
 
         return carry
 
-    lax.fori_loop(0, count // 2, pair, 0)
-    solve_block(*work[1], out_ref, (count - 1) * GROUPS, ident, low, members)
+    lax.fori_loop(0, count // 2, step, 0)
+    def finish(units):
+        for _ in range(3):
+            run(units, iter(()), 0)
+
+    for stage in (last - 1, last):
+        finish(solve(stage, count - 2, 0))
+    finish([gram(pairs - 1, count - 1, 1)])
+    for stage in range(last + 1):
+        finish(solve(stage, count - 1, 1))
 
 
 def transforms(slots, lists, ens, obs, wgt):
@@ -246,12 +322,14 @@
         out_specs=VMEM,
         scratch_shapes=[
             pltpu.VMEM((windows * blocks * LANES, LANES), F32),
-            pltpu.VMEM((8, LANES, LANES), F32),
+            pltpu.VMEM((2, 2, LANES, LANES), F32),
             *work,
             *work,
             pltpu.SMEM((4 * GROUPS, LANES), jnp.int32),
             pltpu.SMEM((4 * GROUPS, LANES), jnp.int32),
             pltpu.SemaphoreType.DMA((2,)),
+            pltpu.VMEM((GROUPS, 128, 256), F32),
+            pltpu.VMEM((GROUPS, 64, 256), BF16),
         ],
         compiler_params=params(48),
         name="transforms",

time: 206 us -> 191 us (0.927)
  Pallas kernels: 96 us -> 84.4 us
  waiting for transfers between devices: 49.9 us -> 44 us
  starting transfers between devices: 36.9 us -> 39.6 us
    pallas_call x1, Pallas kernels: 58.8 us -> 50.5 us  [transforms(): pl.pallas_call(transform_kernel, out_shape=jax.ShapeDtypeStruct((pairs, 6...]
    pallas_call x1, Pallas kernels: 9.96 us -> 6.67 us  [observe(): pl.pallas_call(observe_kernel, out_shape=jax.ShapeDtypeStruct((block.shap...]
    ppermute x2, waiting for transfers between devices: 5.91 us -> 3.25 us  [on_device(): beyonds += [lax.ppermute(beside, 'slab', skip) for beside in besides[-2:]]]
    ppermute x3, waiting for transfers between devices: 2.17 us -> 0.01 us  [on_device(): beyonds.append(lax.ppermute(besides[i - 2], 'slab', skip))]
    ppermute x2, starting transfers between devices: 7.43 us -> 9.54 us  [on_device(): lax.ppermute(ens, 'mem', [(i, i ^ step) for i in range(groups)])]
    unnamed x34 -> x30, local copies, waits for them, and re-layouts: 4.94 us -> 4.94 us
  transfers between devices with their start and end apart: 15 -> 15, of which waited for: 8 -> 9; matrix products, arithmetic and copies ran while one was open for 3% -> 4% of each run, Pallas kernels for 35% -> 33%
where the time goes in v3:
time: 191 us; the launch traced here: 190 us
  Pallas kernels  84.4 us (44%)
  waiting for transfers between devices  44 us (23%)
  starting transfers between devices  39.6 us (21%)
  local copies, waits for them, and re-layouts  19.4 us (10%)
  other arithmetic  2.14 us (1%)
    pallas_call x1, Pallas kernels, transforms(): pl.pallas_call(transform_kernel, out_shape=jax.ShapeDtypeStruct((pairs, 6...  50.5 us
    ppermute x5, waiting for transfers between devices, on_device(): besides.append(lax.ppermute(piece, 'slab', swap))  30.3 us
    pallas_call x5, Pallas kernels, forecast(): pl.pallas_call(functools.partial(forecast_kernel, first), out_shape=jax.S...  15.9 us
    pallas_call x1, Pallas kernels, update(): pl.pallas_call(update_kernel, out_shape=jax.ShapeDtypeStruct((levels, row...  11.3 us
    ppermute x3, starting transfers between devices, on_device(): beyonds.append(lax.ppermute(besides[i - 2], 'slab', skip))  9.58 us
    ppermute x2, starting transfers between devices, on_device(): lax.ppermute(ens, 'mem', [(i, i ^ step) for i in range(groups)])  9.54 us
    ppermute x2, starting transfers between devices, on_device(): beyonds += [lax.ppermute(beside, 'slab', skip) for beside in besides[-2:]]  8.03 us
    pallas_call x1, Pallas kernels, observe(): pl.pallas_call(observe_kernel, out_shape=jax.ShapeDtypeStruct((block.shap...  6.67 us
  transfers between devices with their start and end apart: 15, of which 9 were waited for; matrix products, arithmetic and copies ran while one was open for 4% of the time, Pallas kernels for 33%

profile of v3, /device:TPU:9, one launch (start us, length us, event | category | flops | bytes accessed | tf_op | source)
XLA Modules:
  0.0 190.1 jit_solution(7531180639735735273)
XLA Ops:
  1.5 2.7 %fusion.17 = (bf16[8,2,16,1024]{3,1,0,2:T(2,128)(2,1)S(1)}, bf16[8,2,16,1024]{3,1,0,2:T(2,128)(2,1)S(1)}, bf16[8,2,16,1024]{3,1,0,2:T(2,128)(2,1)S(1)}) fusion(bf16[32,2,16,1024]{3,1,0,2:T(2,128)(2,1)} %bitcast.103), kind=kLoop, calls=%fused_computation.57 | loop fusion | bytes 3145728 | tf_op jit(solution)/shard_map/slice | solution.py:434
  7.8 14.5 %collective-permute-done.beside_ref = bf16[20,16,1024]{2,1,0:T(8,128)(2,1)} collective-permute-done((bf16[20,16,1024]{2,1,0:T(8,128)(2,1)S(1)}, bf16[20,16,1024]{2,1,0:T(8,128)(2,1)}, u32[]{:S(2)}, u32[]{:S(2)}) %collective-permute-start) | collective-permute-done | bytes 655392 | tf_op jit(solution)/shard_map/ppermute | solution.py:454
  22.2 3.2 %collective-permute-start.1 = (bf16[20,16,1024]{2,1,0:T(8,128)(2,1)}, bf16[20,16,1024]{2,1,0:T(8,128)(2,1)}, u32[]{:S(2)}, u32[]{:S(2)}) collective-permute-start(bf16[20,16,1024]{2,1,0:T(8,128)(2,1)} %collective-permute-done.beside_ref), channel_id=1, source_target_pairs={{0,2},{2,4},{4,6},{3,1},{5,3},{7,5},{8,10},{10,12},{12,14},{11,9},... | collective-permute-start | bytes 1966088 | tf_op jit(solution)/shard_map/ppermute | solution.py:456
  28.4 8.8 %collective-permute-done.2.beside_ref = bf16[16,16,1024]{2,1,0:T(8,128)(2,1)} collective-permute-done((bf16[16,16,1024]{2,1,0:T(8,128)(2,1)S(1)}, bf16[16,16,1024]{2,1,0:T(8,128)(2,1)}, u32[]{:S(2)}, u32[]{:S(2)}) %collective-permute-start.2) | collective-permute-done | bytes 524320 | tf_op jit(solution)/shard_map/ppermute | solution.py:454
  37.2 3.2 %collective-permute-start.3 = (bf16[16,16,1024]{2,1,0:T(8,128)(2,1)}, bf16[16,16,1024]{2,1,0:T(8,128)(2,1)S(1)}, u32[]{:S(2)}, u32[]{:S(2)}) collective-permute-start(bf16[16,16,1024]{2,1,0:T(8,128)(2,1)} %collective-permute-done.2.beside_ref), channel_id=1, source_target_pairs={{0,2},{2,4},{4,6},{3,1},{5,3},{7,5},{8,10},{10,12},{12,14},{11,9},... | collective-permute-start | bytes 1572872 | tf_op jit(solution)/shard_map/ppermute | solution.py:456
  42.8 2.6 %forecast.5 = bf16[4,2,8,16,128]{4,3,2,1,0:T(8,128)(2,1)S(1)} custom-call(s32[1]{0:T(128)} %bitcast.odd_ref, bf16[20,16,1024]{2,1,0:T(8,128)(2,1)S(1)} %pad_maximum_fusion.2.own_ref, bf16[20,16,1024]{2,1,0:T(8,128)(2,1)} %collective-permute-done.beside_ref, bf16[20,16,1024]{2,1,0:T(8,128)(2,1)} %collective-permute-done.1.beyond_ref, ...), custom_call_target="tpu_custom_call" | custom-call | tf_op jit(solution)/shard_map/forecast/pallas_call | solution.py:64
  45.6 2.8 %collective-permute-done.4.beside_ref = bf16[16,16,1024]{2,1,0:T(8,128)(2,1)} collective-permute-done((bf16[16,16,1024]{2,1,0:T(8,128)(2,1)S(1)}, bf16[16,16,1024]{2,1,0:T(8,128)(2,1)}, u32[]{:S(2)}, u32[]{:S(2)}) %collective-permute-start.4) | collective-permute-done | bytes 524320 | tf_op jit(solution)/shard_map/ppermute | solution.py:454
  48.4 3.2 %collective-permute-start.5 = (bf16[16,16,1024]{2,1,0:T(8,128)(2,1)}, bf16[16,16,1024]{2,1,0:T(8,128)(2,1)}, u32[]{:S(2)}, u32[]{:S(2)}) collective-permute-start(bf16[16,16,1024]{2,1,0:T(8,128)(2,1)} %collective-permute-done.4.beside_ref), channel_id=1, source_target_pairs={{0,2},{2,4},{4,6},{3,1},{5,3},{7,5},{8,10},{10,12},{12,14},{11,9},... | collective-permute-start | bytes 1572872 | tf_op jit(solution)/shard_map/ppermute | solution.py:456
  51.6 3.6 %forecast.6 = bf16[8,2,8,16,128]{4,3,2,1,0:T(8,128)(2,1)S(1)} custom-call(s32[1]{0:T(128)} %bitcast.odd_ref, bf16[16,16,1024]{2,1,0:T(8,128)(2,1)S(1)} %bitcast.97, bf16[16,16,1024]{2,1,0:T(8,128)(2,1)} %collective-permute-done.2.beside_ref, bf16[16,16,1024]{2,1,0:T(8,128)(2,1)S(1)} %collective-permute-done.3.beyond_ref, f32[3,2,32,1024]{3,2,1,0:T(8,128)S(1)} %bitcast.82, ...), custom_call_target="tpu_custom_call" | custom-call | tf_op jit(solution)/shard_map/forecast/pallas_call | solution.py:64
  55.3 3.3 %collective-permute-done.6.beside_ref = bf16[16,16,1024]{2,1,0:T(8,128)(2,1)} collective-permute-done((bf16[16,16,1024]{2,1,0:T(8,128)(2,1)S(1)}, bf16[16,16,1024]{2,1,0:T(8,128)(2,1)}, u32[]{:S(2)}, u32[]{:S(2)}) %collective-permute-start.6) | collective-permute-done | bytes 524320 | tf_op jit(solution)/shard_map/ppermute | solution.py:454
  58.6 4.0 %collective-permute-start.7 = (bf16[16,16,1024]{2,1,0:T(8,128)(2,1)}, bf16[16,16,1024]{2,1,0:T(8,128)(2,1)}, u32[]{:S(2)}, u32[]{:S(2)}) collective-permute-start(bf16[16,16,1024]{2,1,0:T(8,128)(2,1)} %collective-permute-done.6.beside_ref), channel_id=1, source_target_pairs={{0,2},{2,4},{4,6},{3,1},{5,3},{7,5},{8,10},{10,12},{12,14},{11,9},... | collective-permute-start | bytes 1572872 | tf_op jit(solution)/shard_map/ppermute | solution.py:457
  64.2 4.0 %collective-permute-start.9 = (bf16[8,16,1024]{2,1,0:T(8,128)(2,1)}, bf16[8,16,1024]{2,1,0:T(8,128)(2,1)S(1)}, u32[]{:S(2)}, u32[]{:S(2)}) collective-permute-start(bf16[8,16,1024]{2,1,0:T(8,128)(2,1)} %collective-permute-done.8.beside_ref), channel_id=1, source_target_pairs={{0,2},{2,4},{4,6},{3,1},{5,3},{7,5},{8,10},{10,12},{12,14},{11,9},... | collective-permute-start | bytes 786440 | tf_op jit(solution)/shard_map/ppermute | solution.py:457
  68.4 3.7 %forecast.7 = bf16[8,2,8,16,128]{4,3,2,1,0:T(8,128)(2,1)S(1)} custom-call(s32[1]{0:T(128)} %bitcast.odd_ref, bf16[16,16,1024]{2,1,0:T(8,128)(2,1)S(1)} %bitcast.95, bf16[16,16,1024]{2,1,0:T(8,128)(2,1)} %collective-permute-done.4.beside_ref, bf16[16,16,1024]{2,1,0:T(8,128)(2,1)} %collective-permute-done.5.beyond_ref, f32[3,2,32,1024]{3,2,1,0:T(8,128)S(1)} %bitcast.83, ...), custom_call_target="tpu_custom_call" | custom-call | tf_op jit(solution)/shard_map/forecast/pallas_call | solution.py:64
  72.1 3.3 %collective-permute-done.9.beyond_ref = bf16[8,16,1024]{2,1,0:T(8,128)(2,1)S(1)} collective-permute-done((bf16[8,16,1024]{2,1,0:T(8,128)(2,1)}, bf16[8,16,1024]{2,1,0:T(8,128)(2,1)S(1)}, u32[]{:S(2)}, u32[]{:S(2)}) %collective-permute-start.9) | collective-permute-done | bytes 262176 | tf_op jit(solution)/shard_map/ppermute | solution.py:457
  77.7 3.7 %forecast.8 = bf16[8,2,8,16,128]{4,3,2,1,0:T(8,128)(2,1)S(1)} custom-call(s32[1]{0:T(128)} %bitcast.odd_ref, bf16[16,16,1024]{2,1,0:T(8,128)(2,1)S(1)} %bitcast.93, bf16[16,16,1024]{2,1,0:T(8,128)(2,1)} %collective-permute-done.6.beside_ref, bf16[16,16,1024]{2,1,0:T(8,128)(2,1)} %collective-permute-done.7.beyond_ref, f32[3,2,32,1024]{3,2,1,0:T(8,128)S(1)} %bitcast.85, ...), custom_call_target="tpu_custom_call" | custom-call | tf_op jit(solution)/shard_map/forecast/pallas_call | solution.py:64
  81.4 6.7 %observe.1 = bf16[32,16,128]{2,1,0:T(8,128)(2,1)S(1)} custom-call(s32[8,8,128]{2,1,0:T(8,128)S(1)} %bitcast.99, bf16[64,16,128]{2,1,0:T(8,128)(2,1)S(1)} %bitcast.90, bf16[128,16,128]{2,1,0:T(8,128)(2,1)S(1)} %bitcast.87, bf16[128,16,128]{2,1,0:T(8,128)(2,1)S(1)} %bitcast.88, bf16[128,16,128]{2,1,0:T(8,128)(2,1)S(1)} %bitcast.89, ...), custom_call_target="tpu_custom_call" | custom-call | tf_op jit(solution)/shard_map/observe/pallas_call | solution.py:118
  88.1 3.6 %collective-permute-start.11 = (bf16[40,16,128]{2,1,0:T(8,128)(2,1)S(1)}, bf16[40,16,128]{2,1,0:T(8,128)(2,1)S(1)}, u32[]{:S(2)}, u32[]{:S(2)}) collective-permute-start(bf16[40,16,128]{2,1,0:T(8,128)(2,1)S(1)} %get-tuple-element.33), channel_id=1, source_target_pairs={{1,0},{2,1},{3,2},{4,3},{5,4},{6,5},{7,6},{9,8},{10,9},{11,10},{12... | collective-permute-start | bytes 491528 | tf_op jit(solution)/shard_map/ppermute | solution.py:469
  94.2 4.5 %collective-permute-done.10 = bf16[40,16,128]{2,1,0:T(8,128)(2,1)S(1)} collective-permute-done((bf16[40,16,128]{2,1,0:T(8,128)(2,1)S(1)}, bf16[40,16,128]{2,1,0:T(8,128)(2,1)S(1)}, u32[]{:S(2)}, u32[]{:S(2)}) %collective-permute-start.10) | collective-permute-done | bytes 163872 | tf_op jit(solution)/shard_map/ppermute | solution.py:469
  100.1 5.4 %collective-permute-done.12 = bf16[1,3,32,16,128]{4,3,2,1,0:T(8,128)(2,1)S(1)} collective-permute-done((bf16[1,3,32,16,128]{4,3,2,1,0:T(8,128)(2,1)S(1)}, bf16[1,3,32,16,128]{4,3,2,1,0:T(8,128)(2,1)S(1)}, u32[]{:S(2)}, u32[]{:S(2)}) %collective-permute-start.12) | collective-permute-done | bytes 393248 | tf_op jit(solution)/shard_map/ppermute | solution.py:476
  105.6 8.3 %collective-permute-start.13 = (bf16[2,3,32,16,128]{4,3,2,1,0:T(8,128)(2,1)S(1)}, bf16[2,3,32,16,128]{4,3,2,1,0:T(8,128)(2,1)S(1)}, u32[]{:S(2)}, u32[]{:S(2)}) collective-permute-start(bf16[2,3,32,16,128]{4,3,2,1,0:T(8,128)(2,1)S(1)} %pad_maximum_fusion.1), channel_id=1, source_target_pairs={{0,8},{8,0},{16,24},{24,16},{1,9},{9,1},{17,25},{25,17},{2,10},{10... | collective-permute-start | bytes 2359304 | tf_op jit(solution)/shard_map/ppermute | solution.py:476
  117.5 3.9 %all-to-all-start = ((bf16[4,32,2,2,16,128]{5,4,3,2,1,0:T(8,128)(2,1)}), bf16[4,32,2,2,16,128]{5,4,3,2,1,0:T(8,128)(2,1)S(1)}, u32[]{:S(2)}, u32[]{:S(2)}) async-start(bf16[4,32,2,2,16,128]{5,4,3,2,1,0:T(8,128)(2,1)} %bitcast.100), calls=%async_computation | async-start | bytes 4194304 | tf_op jit(solution)/shard_map/all_to_all | solution.py:488
  122.8 50.5 %transforms.1.transform_ref = f32[64,64,256]{2,1,0:T(8,128)S(1)} custom-call(s32[4]{0:T(128)S(1)} %shift-left_add_fusion.slot_ref, bf16[4,3,32,16,128]{4,3,2,1,0:T(8,128)(2,1)S(1)} %copy-done.1, f32[3,2,32,128]{3,2,1,0:T(8,128)S(1)} %fusion.6.obs_ref, f32[2,128,128]{2,1,0:T(8,128)S(1)} %fusion.4.wgt_ref, s32[16,16,128]{2,1,0:T(8,128)S(1)} %bitcast.98), custom_call_target="tpu_custom_call" | custom-call | tf_op jit(solution)/shard_map/transforms/pallas_call | solution.py:318
  175.3 11.3 %update.1 = bf16[32,2,64,256]{3,2,1,0:T(8,128)(2,1)S(1)} custom-call(bf16[4,32,2,2,16,128]{5,4,3,2,1,0:T(8,128)(2,1)S(1)} %all-to-all-done.state_ref, f32[64,64,256]{2,1,0:T(8,128)} %copy-done), custom_call_target="tpu_custom_call" | custom-call | tf_op jit(solution)/shard_map/update/pallas_call | solution.py:392
  186.6 3.5 %copy.31 = bf16[64,32,2,256]{3,2,1,0:T(2,128)(2,1)} copy(bf16[64,32,2,256]{3,0,2,1:T(8,128)(2,1)S(1)} %bitcast.86) | data formatting | bytes 4194304 | tf_op jit(solution)/shard_map/transpose | solution.py:490
  (77 shorter events, 25.2 us)
Async XLA Ops:
  0.0 4.2 %copy-start.4 = (f32[3,32,2,1024]{3,2,1,0:T(2,128)S(1)}, f32[3,32,2,1024]{3,2,1,0:T(2,128)}, u32[]{:S(2)}) copy-start(f32[3,32,2,1024]{3,2,1,0:T(2,128)} %param.9) | copy-start | bytes 2359300
  4.9 23.4 %copy-start.2 = (bf16[8,2,16,1024]{3,2,1,0:T(8,128)(2,1)}, bf16[8,2,16,1024]{3,2,1,0:T(8,128)(2,1)S(1)}, u32[]{:S(2)}) copy-start(bf16[8,2,16,1024]{3,2,1,0:T(8,128)(2,1)S(1)} %copy.19) | copy-start | bytes 1572868
  6.5 15.8 %collective-permute-start = (bf16[20,16,1024]{2,1,0:T(8,128)(2,1)S(1)}, bf16[20,16,1024]{2,1,0:T(8,128)(2,1)}, u32[]{:S(2)}, u32[]{:S(2)}) collective-permute-start(bf16[20,16,1024]{2,1,0:T(8,128)(2,1)S(1)} %pad_maximum_fusion.2.own_ref), channel_id=1, source_target_pairs={{0,1},{1,0},{2,3},{3,2},{4,5},{5,4},{6,7},{7,6},{8,9},{9,8},{10,11... | collective-permute-start | bytes 1966088 | tf_op jit(solution)/shard_map/ppermute | solution.py:454
  22.2 19.3 %collective-permute-start.1 = (bf16[20,16,1024]{2,1,0:T(8,128)(2,1)}, bf16[20,16,1024]{2,1,0:T(8,128)(2,1)}, u32[]{:S(2)}, u32[]{:S(2)}) collective-permute-start(bf16[20,16,1024]{2,1,0:T(8,128)(2,1)} %collective-permute-done.beside_ref), channel_id=1, source_target_pairs={{0,2},{2,4},{4,6},{3,1},{5,3},{7,5},{8,10},{10,12},{12,14},{11,9},... | collective-permute-start | bytes 1966088 | tf_op jit(solution)/shard_map/ppermute | solution.py:456
  25.4 11.8 %collective-permute-start.2 = (bf16[16,16,1024]{2,1,0:T(8,128)(2,1)S(1)}, bf16[16,16,1024]{2,1,0:T(8,128)(2,1)}, u32[]{:S(2)}, u32[]{:S(2)}) collective-permute-start(bf16[16,16,1024]{2,1,0:T(8,128)(2,1)S(1)} %bitcast.96), channel_id=1, source_target_pairs={{0,1},{1,0},{2,3},{3,2},{4,5},{5,4},{6,7},{7,6},{8,9},{9,8},{10,11... | collective-permute-start | bytes 1572872 | tf_op jit(solution)/shard_map/ppermute | solution.py:454
  25.6 22.8 %collective-permute-start.4 = (bf16[16,16,1024]{2,1,0:T(8,128)(2,1)S(1)}, bf16[16,16,1024]{2,1,0:T(8,128)(2,1)}, u32[]{:S(2)}, u32[]{:S(2)}) collective-permute-start(bf16[16,16,1024]{2,1,0:T(8,128)(2,1)S(1)} %bitcast.94), channel_id=1, source_target_pairs={{0,1},{1,0},{2,3},{3,2},{4,5},{5,4},{6,7},{7,6},{8,9},{9,8},{10,11... | collective-permute-start | bytes 1572872 | tf_op jit(solution)/shard_map/ppermute | solution.py:454
  37.2 14.4 %collective-permute-start.3 = (bf16[16,16,1024]{2,1,0:T(8,128)(2,1)}, bf16[16,16,1024]{2,1,0:T(8,128)(2,1)S(1)}, u32[]{:S(2)}, u32[]{:S(2)}) collective-permute-start(bf16[16,16,1024]{2,1,0:T(8,128)(2,1)} %collective-permute-done.2.beside_ref), channel_id=1, source_target_pairs={{0,2},{2,4},{4,6},{3,1},{5,3},{7,5},{8,10},{10,12},{12,14},{11,9},... | collective-permute-start | bytes 1572872 | tf_op jit(solution)/shard_map/ppermute | solution.py:456
  42.7 2.7 %copy-start.8 = (f32[4096]{0:T(1024)S(1)}, f32[4096]{0:T(1024)}, u32[]{:S(2)}) copy-start(f32[4096]{0:T(1024)} %param.11) | copy-start | bytes 49156
  42.8 8.9 %copy-start.3 = (bf16[8,2,16,1024]{3,2,1,0:T(8,128)(2,1)S(1)}, bf16[8,2,16,1024]{3,2,1,0:T(8,128)(2,1)}, u32[]{:S(2)}) copy-start(bf16[8,2,16,1024]{3,2,1,0:T(8,128)(2,1)} %copy-done.2) | copy-start | bytes 1572868
  45.4 22.9 %copy-start.10 = (s32[4096]{0:T(1024)S(1)}, s32[4096]{0:T(1024)}, u32[]{:S(2)}) copy-start(s32[4096]{0:T(1024)} %param.12) | copy-start | bytes 49156
  45.4 13.2 %collective-permute-start.6 = (bf16[16,16,1024]{2,1,0:T(8,128)(2,1)S(1)}, bf16[16,16,1024]{2,1,0:T(8,128)(2,1)}, u32[]{:S(2)}, u32[]{:S(2)}) collective-permute-start(bf16[16,16,1024]{2,1,0:T(8,128)(2,1)S(1)} %bitcast.92), channel_id=1, source_target_pairs={{0,1},{1,0},{2,3},{3,2},{4,5},{5,4},{6,7},{7,6},{8,9},{9,8},{10,11... | collective-permute-start | bytes 1572872 | tf_op jit(solution)/shard_map/ppermute | solution.py:454
  48.4 19.9 %collective-permute-start.5 = (bf16[16,16,1024]{2,1,0:T(8,128)(2,1)}, bf16[16,16,1024]{2,1,0:T(8,128)(2,1)}, u32[]{:S(2)}, u32[]{:S(2)}) collective-permute-start(bf16[16,16,1024]{2,1,0:T(8,128)(2,1)} %collective-permute-done.4.beside_ref), channel_id=1, source_target_pairs={{0,2},{2,4},{4,6},{3,1},{5,3},{7,5},{8,10},{10,12},{12,14},{11,9},... | collective-permute-start | bytes 1572872 | tf_op jit(solution)/shard_map/ppermute | solution.py:456
  55.2 9.0 %collective-permute-start.8 = (bf16[8,16,1024]{2,1,0:T(8,128)(2,1)}, bf16[8,16,1024]{2,1,0:T(8,128)(2,1)}, u32[]{:S(2)}, u32[]{:S(2)}) collective-permute-start(bf16[8,16,1024]{2,1,0:T(8,128)(2,1)} %bitcast.8.own_ref), channel_id=1, source_target_pairs={{0,1},{1,0},{2,3},{3,2},{4,5},{5,4},{6,7},{7,6},{8,9},{9,8},{10,11... | collective-permute-start | bytes 786440 | tf_op jit(solution)/shard_map/ppermute | solution.py:454
  58.6 19.0 %collective-permute-start.7 = (bf16[16,16,1024]{2,1,0:T(8,128)(2,1)}, bf16[16,16,1024]{2,1,0:T(8,128)(2,1)}, u32[]{:S(2)}, u32[]{:S(2)}) collective-permute-start(bf16[16,16,1024]{2,1,0:T(8,128)(2,1)} %collective-permute-done.6.beside_ref), channel_id=1, source_target_pairs={{0,2},{2,4},{4,6},{3,1},{5,3},{7,5},{8,10},{10,12},{12,14},{11,9},... | collective-permute-start | bytes 1572872 | tf_op jit(solution)/shard_map/ppermute | solution.py:457
  64.2 11.1 %collective-permute-start.9 = (bf16[8,16,1024]{2,1,0:T(8,128)(2,1)}, bf16[8,16,1024]{2,1,0:T(8,128)(2,1)S(1)}, u32[]{:S(2)}, u32[]{:S(2)}) collective-permute-start(bf16[8,16,1024]{2,1,0:T(8,128)(2,1)} %collective-permute-done.8.beside_ref), channel_id=1, source_target_pairs={{0,2},{2,4},{4,6},{3,1},{5,3},{7,5},{8,10},{10,12},{12,14},{11,9},... | collective-permute-start | bytes 786440 | tf_op jit(solution)/shard_map/ppermute | solution.py:457
  77.6 10.4 %copy-start.7 = (bf16[8,16,128]{2,1,0:T(8,128)(2,1)S(1)}, bf16[8,16,128]{2,1,0:T(8,128)(2,1)}, u32[]{:S(2)}) copy-start(bf16[8,16,128]{2,1,0:T(8,128)(2,1)} %reshape.83) | copy-start | bytes 98308
  88.1 6.1 %collective-permute-start.11 = (bf16[40,16,128]{2,1,0:T(8,128)(2,1)S(1)}, bf16[40,16,128]{2,1,0:T(8,128)(2,1)S(1)}, u32[]{:S(2)}, u32[]{:S(2)}) collective-permute-start(bf16[40,16,128]{2,1,0:T(8,128)(2,1)S(1)} %get-tuple-element.33), channel_id=1, source_target_pairs={{1,0},{2,1},{3,2},{4,3},{5,4},{6,5},{7,6},{9,8},{10,9},{11,10},{12... | collective-permute-start | bytes 491528 | tf_op jit(solution)/shard_map/ppermute | solution.py:469
  91.8 7.0 %collective-permute-start.10 = (bf16[40,16,128]{2,1,0:T(8,128)(2,1)S(1)}, bf16[40,16,128]{2,1,0:T(8,128)(2,1)S(1)}, u32[]{:S(2)}, u32[]{:S(2)}) collective-permute-start(bf16[40,16,128]{2,1,0:T(8,128)(2,1)S(1)} %get-tuple-element.33), channel_id=1, source_target_pairs={{0,1},{1,2},{2,3},{3,4},{4,5},{5,6},{6,7},{8,9},{9,10},{10,11},{11... | collective-permute-start | bytes 491528 | tf_op jit(solution)/shard_map/ppermute | solution.py:469
  98.8 6.7 %collective-permute-start.12 = (bf16[1,3,32,16,128]{4,3,2,1,0:T(8,128)(2,1)S(1)}, bf16[1,3,32,16,128]{4,3,2,1,0:T(8,128)(2,1)S(1)}, u32[]{:S(2)}, u32[]{:S(2)}) collective-permute-start(bf16[1,3,32,16,128]{4,3,2,1,0:T(8,128)(2,1)S(1)} %slice_bitcast_fusion), channel_id=1, source_target_pairs={{0,16},{8,24},{16,0},{24,8},{1,17},{9,25},{17,1},{25,9},{2,18},{10... | collective-permute-start | bytes 1179656 | tf_op jit(solution)/shard_map/ppermute | solution.py:476
  105.6 10.6 %collective-permute-start.13 = (bf16[2,3,32,16,128]{4,3,2,1,0:T(8,128)(2,1)S(1)}, bf16[2,3,32,16,128]{4,3,2,1,0:T(8,128)(2,1)S(1)}, u32[]{:S(2)}, u32[]{:S(2)}) collective-permute-start(bf16[2,3,32,16,128]{4,3,2,1,0:T(8,128)(2,1)S(1)} %pad_maximum_fusion.1), channel_id=1, source_target_pairs={{0,8},{8,0},{16,24},{24,16},{1,9},{9,1},{17,25},{25,17},{2,10},{10... | collective-permute-start | bytes 2359304 | tf_op jit(solution)/shard_map/ppermute | solution.py:476
  117.5 3.9 %copy-start.5 = (s32[2,128,128]{2,1,0:T(8,128)S(1)}, s32[2,128,128]{2,1,0:T(8,128)}, u32[]{:S(2)}) copy-start(s32[2,128,128]{2,1,0:T(8,128)} %param.13) | copy-start | bytes 393220
  117.5 4.1 %copy-start.6 = (f32[2,128,128]{2,1,0:T(8,128)S(1)}, f32[2,128,128]{2,1,0:T(8,128)}, u32[]{:S(2)}) copy-start(f32[2,128,128]{2,1,0:T(8,128)} %param.15) | copy-start | bytes 393220
  117.5 4.1 %copy-start.11 = (s32[2,128]{1,0:T(2,128)S(1)}, s32[2,128]{1,0:T(2,128)}, u32[]{:S(2)}) copy-start(s32[2,128]{1,0:T(2,128)} %param.14) | copy-start | bytes 3076
  117.5 57.8 %all-to-all-start = ((bf16[4,32,2,2,16,128]{5,4,3,2,1,0:T(8,128)(2,1)}), bf16[4,32,2,2,16,128]{5,4,3,2,1,0:T(8,128)(2,1)S(1)}, u32[]{:S(2)}, u32[]{:S(2)}) async-start(bf16[4,32,2,2,16,128]{5,4,3,2,1,0:T(8,128)(2,1)} %bitcast.100), calls=%async_computation | async-start | bytes 4194304 | tf_op jit(solution)/shard_map/all_to_all | solution.py:488
  (3 other events, 6.1 us)

commit v4 on v3

--- a/solution.py
+++ b/solution.py
@@ -1,4 +1,5 @@
 import functools
+import itertools
 import math
 
 import jax
@@ -150,14 +151,15 @@
     return jnp.dot(a, b, preferred_element_type=F32)
 
 
-LEAD = 120
+WIDE = 2
+LEAD = 236
 GROUPS = 4
 
 
 def gather_rows(q, lists_ref, cat_ref, rows_ref):
     for l in range(LANES):
         for r in range(2):
-            rows_ref[q % 2, r, pl.ds(l, 1), :] = cat_ref[pl.ds(lists_ref[2 * q + r, l], 1), :]
+            rows_ref[q % (2 * WIDE), r, pl.ds(l, 1), :] = cat_ref[pl.ds(lists_ref[2 * q + r, l], 1), :]
         yield
 
 
@@ -165,7 +167,7 @@
     sq_ref, force_ref, scale_ref = work
     ident, lower, _, inflated = consts
     bounds = []
-    rows = [rows_ref[q % 2, r] for r in range(2)]
+    rows = [rows_ref[q % (2 * WIDE), r] for r in range(2)]
     weighted = [(rows[r].T[:64] * wgt_ref[r, pl.ds(first + q, 1), :]).astype(BF16) for r in range(2)]
     yield
     grams = [mul(weighted[r], rows[r].astype(BF16)) for r in range(2)]
@@ -221,11 +223,15 @@
             next(filler, None)
 
 
-def segment(units, gram, filler):
-    middle = len(units) // 2
-    begin = [gram] + units[:middle] + [gram] + units[middle:]
-    run(begin, filler, LEAD // len(begin))
-    run(units + [gram], filler, (LANES - LEAD) // (len(units) + 1) + 1)
+def segment(stages, grams, filler):
+    steps = grams + stages[0] + grams
+    for i, (before, after) in enumerate(zip(stages[:-1], stages[1:])):
+        for pair in zip(before, after):
+            steps += pair
+        if i == 0:
+            steps += grams
+    run(steps, filler, LEAD // len(steps))
+    run(stages[-1], filler, (WIDE * LANES - LEAD) // len(stages[-1]) + 1)
     for _ in filler:
         pass
 
@@ -262,6 +268,7 @@
     consts = (eye4(), lower, jnp.where(lower, 1.0, 0.0).astype(BF16), inflated)
     pairs = 2 * GROUPS
     last = 2 * NS_ITERS
+    share = (last + 1) * WIDE // pairs
 
     def solve(stage, block, half):
         at = jnp.maximum(block, 0) * GROUPS
@@ -273,19 +280,19 @@
     def step(i, carry):
         for half in range(2):
             b = 2 * i + half
-            for q in range(pairs):
+            for part in range(pairs // WIDE):
 
                 @pl.when(slot_ref[0] >= 0)
                 def _():
-                    if q == 0:
+                    if part == 0:
                         fetch(b, half).wait()
-                        units = solve(last - 1, b - 2, half)
-                        before = gram(pairs - 1, b - 1, 1 - half)
+                        stages = [solve(stage, b - 2, half) for stage in range(pairs // WIDE * share - share, last + 1)]
+                        grams = [gram(q, b - 1, 1 - half) for q in range(pairs - WIDE, pairs)]
                     else:
-                        units = solve(last, b - 2, half) if q == 1 else []
-                        units += solve(q - 1, b - 1, 1 - half)
-                        before = gram(q - 1, b, half)
-                    segment(units, before, gather_rows(q, smem[half], cat_ref, rows_ref))
+                        stages = [solve(stage, b - 1, 1 - half) for stage in range(part * share - share, part * share)]
+                        grams = [gram(q, b, half) for q in range((part - 1) * WIDE, part * WIDE)]
+                    rows = [gather_rows(q, smem[half], cat_ref, rows_ref) for q in range(part * WIDE, (part + 1) * WIDE)]
+                    segment(stages, grams, itertools.chain(*rows))
 
             @pl.when(b + 2 < count)
             def _():
@@ -294,13 +301,14 @@
         return carry
 
     lax.fori_loop(0, count // 2, step, 0)
+
     def finish(units):
         for _ in range(3):
             run(units, iter(()), 0)
 
-    for stage in (last - 1, last):
+    for stage in range(pairs // WIDE * share - share, last + 1):
         finish(solve(stage, count - 2, 0))
-    finish([gram(pairs - 1, count - 1, 1)])
+    finish([gram(q, count - 1, 1) for q in range(pairs - WIDE, pairs)])
     for stage in range(last + 1):
         finish(solve(stage, count - 1, 1))
 
@@ -322,7 +330,7 @@
         out_specs=VMEM,
         scratch_shapes=[
             pltpu.VMEM((windows * blocks * LANES, LANES), F32),
-            pltpu.VMEM((2, 2, LANES, LANES), F32),
+            pltpu.VMEM((2 * WIDE, 2, LANES, LANES), F32),
             *work,
             *work,
             pltpu.SMEM((4 * GROUPS, LANES), jnp.int32),
@@ -331,7 +339,7 @@
             pltpu.VMEM((GROUPS, 128, 256), F32),
             pltpu.VMEM((GROUPS, 64, 256), BF16),
         ],
-        compiler_params=params(48),
+        compiler_params=params(24),
         name="transforms",
     )(slots, ens, obs, wgt, lists)
 
@@ -399,7 +407,7 @@
             pltpu.VMEM((levels * width, LANES), F32),
             pltpu.VMEM((levels, 8, width), F32),
         ],
-        compiler_params=params(48),
+        compiler_params=params(24),
         name="update",
     )(state, transform)
 
@@ -470,21 +478,23 @@
     obs = window[:, seen.shape[0] :].reshape(3, 2, 2, nobs // LANES, LANES).astype(F32)
     obs = obs[:, 0] + obs[:, 1]
     window = window[:, : seen.shape[0]]
+    tiles = columns // groups // LANES
+    ship = jnp.concatenate(fields, 0)
+    ship = jnp.transpose(ship.reshape(ship.shape[:2] + (groups, tiles) + ship.shape[3:]), (2, 0, 1, 3, 4, 5))
     ens = window[None]
-    step = groups // 2
-    while step:
-        ens = jnp.concatenate([ens, lax.ppermute(ens, "mem", [(i, i ^ step) for i in range(groups)])], 0)
-        step //= 2
+    distance = groups // 2
+    while distance:
+        ens = jnp.concatenate([ens, lax.ppermute(ens, "mem", [(i, i ^ distance) for i in range(groups)])], 0)
+        if distance == groups // 2:
+            ens, ship = lax.optimization_barrier((ens, ship))
+        distance //= 2
     slots = bit_reversed(jnp.arange(groups, dtype=jnp.int32) ^ me, bits)
 
     position = lax.broadcasted_iota(jnp.int32, loc_weight.shape, 2)
     wgt = jnp.where(position < counts[..., None], loc_weight, 0.0)
     transform = transforms(slots, lists, ens, obs, wgt)
 
-    tiles = columns // groups // LANES
-    ship = jnp.concatenate(fields, 0)
-    ship = ship.reshape(ship.shape[:2] + (groups, tiles) + ship.shape[3:])
-    ship, _ = lax.optimization_barrier((jnp.transpose(ship, (2, 0, 1, 3, 4, 5)), ens))
+    ship, _ = lax.optimization_barrier((ship, ens))
     state = lax.all_to_all(ship, "mem", 0, 0, tiled=False)
     result = update(state, transform)
     return jnp.transpose(result, (2, 0, 1, 3))

time: 191 us -> 180 us (0.942)
  Pallas kernels: 84.4 us -> 72.1 us
  local copies, waits for them, and re-layouts: 19.4 us -> 22.2 us
    pallas_call x1, Pallas kernels: 50.5 us -> 40.5 us  [transforms(): pl.pallas_call(transform_kernel, out_shape=jax.ShapeDtypeStruct((pairs, 6...]
    unnamed x30 -> x33, local copies, waits for them, and re-layouts: 4.94 us -> 8.45 us
    pallas_call x1, Pallas kernels: 11.3 us -> 9.12 us  [update(): pl.pallas_call(update_kernel, out_shape=jax.ShapeDtypeStruct((levels, row...]
  transfers between devices with their start and end apart: 15 -> 15, of which waited for: 9 -> 10; matrix products, arithmetic and copies ran while one was open for 4% -> 4% of each run, Pallas kernels for 33% -> 29%
where the time goes in v4:
time: 180 us
  Pallas kernels  72.1 us (40%)
  waiting for transfers between devices  44.1 us (24%)
  starting transfers between devices  39.8 us (22%)
  local copies, waits for them, and re-layouts  22.2 us (12%)
    pallas_call x1, Pallas kernels, transforms(): pl.pallas_call(transform_kernel, out_shape=jax.ShapeDtypeStruct((pairs, 6...  40.5 us
    ppermute x5, waiting for transfers between devices, on_device(): besides.append(lax.ppermute(piece, 'slab', swap))  30.9 us
    pallas_call x5, Pallas kernels, forecast(): pl.pallas_call(functools.partial(forecast_kernel, first), out_shape=jax.S...  15.9 us
    ppermute x3, starting transfers between devices, on_device(): beyonds.append(lax.ppermute(besides[i - 2], 'slab', skip))  9.58 us
    ppermute x2, starting transfers between devices, on_device(): lax.ppermute(ens, 'mem', [(i, i ^ distance) for i in range(groups)])  9.54 us
    pallas_call x1, Pallas kernels, update(): pl.pallas_call(update_kernel, out_shape=jax.ShapeDtypeStruct((levels, row...  9.12 us
    unnamed x33, local copies, waits for them, and re-layouts  8.45 us
    ppermute x2, starting transfers between devices, on_device(): beyonds += [lax.ppermute(beside, 'slab', skip) for beside in besides[-2:]]  8.03 us
  transfers between devices with their start and end apart: 15, of which 10 were waited for; matrix products, arithmetic and copies ran while one was open for 4% of the time, Pallas kernels for 29%

profile of v4, /device:TPU:9, one launch (start us, length us, event | category | flops | bytes accessed | tf_op | source)
XLA Modules:
  0.0 179.6 jit_solution(5355446735798611363)
XLA Ops:
  1.5 2.5 %fusion.17 = (bf16[8,2,16,1024]{3,1,0,2:T(2,128)(2,1)S(1)}, bf16[8,2,16,1024]{3,1,0,2:T(2,128)(2,1)S(1)}, bf16[8,2,16,1024]{3,1,0,2:T(2,128)(2,1)S(1)}) fusion(bf16[32,2,16,1024]{3,1,0,2:T(2,128)(2,1)} %bitcast.103), kind=kLoop, calls=%fused_computation.58 | loop fusion | bytes 3145728 | tf_op jit(solution)/shard_map/slice | solution.py:442
  7.5 14.5 %collective-permute-done.beside_ref = bf16[20,16,1024]{2,1,0:T(8,128)(2,1)} collective-permute-done((bf16[20,16,1024]{2,1,0:T(8,128)(2,1)S(1)}, bf16[20,16,1024]{2,1,0:T(8,128)(2,1)}, u32[]{:S(2)}, u32[]{:S(2)}) %collective-permute-start) | collective-permute-done | bytes 655392 | tf_op jit(solution)/shard_map/ppermute | solution.py:462
  22.0 3.2 %collective-permute-start.1 = (bf16[20,16,1024]{2,1,0:T(8,128)(2,1)}, bf16[20,16,1024]{2,1,0:T(8,128)(2,1)}, u32[]{:S(2)}, u32[]{:S(2)}) collective-permute-start(bf16[20,16,1024]{2,1,0:T(8,128)(2,1)} %collective-permute-done.beside_ref), channel_id=1, source_target_pairs={{0,2},{2,4},{4,6},{3,1},{5,3},{7,5},{8,10},{10,12},{12,14},{11,9},... | collective-permute-start | bytes 1966088 | tf_op jit(solution)/shard_map/ppermute | solution.py:464
  28.1 8.8 %collective-permute-done.2.beside_ref = bf16[16,16,1024]{2,1,0:T(8,128)(2,1)} collective-permute-done((bf16[16,16,1024]{2,1,0:T(8,128)(2,1)S(1)}, bf16[16,16,1024]{2,1,0:T(8,128)(2,1)}, u32[]{:S(2)}, u32[]{:S(2)}) %collective-permute-start.2) | collective-permute-done | bytes 524320 | tf_op jit(solution)/shard_map/ppermute | solution.py:462
  37.0 3.2 %collective-permute-start.3 = (bf16[16,16,1024]{2,1,0:T(8,128)(2,1)}, bf16[16,16,1024]{2,1,0:T(8,128)(2,1)S(1)}, u32[]{:S(2)}, u32[]{:S(2)}) collective-permute-start(bf16[16,16,1024]{2,1,0:T(8,128)(2,1)} %collective-permute-done.2.beside_ref), channel_id=1, source_target_pairs={{0,2},{2,4},{4,6},{3,1},{5,3},{7,5},{8,10},{10,12},{12,14},{11,9},... | collective-permute-start | bytes 1572872 | tf_op jit(solution)/shard_map/ppermute | solution.py:464
  42.5 2.6 %forecast.5 = bf16[4,2,8,16,128]{4,3,2,1,0:T(8,128)(2,1)S(1)} custom-call(s32[1]{0:T(128)} %bitcast.3.odd_ref, bf16[20,16,1024]{2,1,0:T(8,128)(2,1)S(1)} %pad_maximum_fusion.1.own_ref, bf16[20,16,1024]{2,1,0:T(8,128)(2,1)} %collective-permute-done.beside_ref, bf16[20,16,1024]{2,1,0:T(8,128)(2,1)} %collective-permute-done.1.beyond_ref, ...), custom_call_target="tpu_custom_call" | custom-call | tf_op jit(solution)/shard_map/forecast/pallas_call | solution.py:65
  45.4 2.8 %collective-permute-done.4.beside_ref = bf16[16,16,1024]{2,1,0:T(8,128)(2,1)} collective-permute-done((bf16[16,16,1024]{2,1,0:T(8,128)(2,1)S(1)}, bf16[16,16,1024]{2,1,0:T(8,128)(2,1)}, u32[]{:S(2)}, u32[]{:S(2)}) %collective-permute-start.4) | collective-permute-done | bytes 524320 | tf_op jit(solution)/shard_map/ppermute | solution.py:462
  48.2 3.2 %collective-permute-start.5 = (bf16[16,16,1024]{2,1,0:T(8,128)(2,1)}, bf16[16,16,1024]{2,1,0:T(8,128)(2,1)}, u32[]{:S(2)}, u32[]{:S(2)}) collective-permute-start(bf16[16,16,1024]{2,1,0:T(8,128)(2,1)} %collective-permute-done.4.beside_ref), channel_id=1, source_target_pairs={{0,2},{2,4},{4,6},{3,1},{5,3},{7,5},{8,10},{10,12},{12,14},{11,9},... | collective-permute-start | bytes 1572872 | tf_op jit(solution)/shard_map/ppermute | solution.py:464
  51.4 3.6 %forecast.6 = bf16[8,2,8,16,128]{4,3,2,1,0:T(8,128)(2,1)S(1)} custom-call(s32[1]{0:T(128)} %bitcast.3.odd_ref, bf16[16,16,1024]{2,1,0:T(8,128)(2,1)S(1)} %bitcast.97, bf16[16,16,1024]{2,1,0:T(8,128)(2,1)} %collective-permute-done.2.beside_ref, bf16[16,16,1024]{2,1,0:T(8,128)(2,1)S(1)} %collective-permute-done.3.beyond_ref, f32[3,2,32,1024]{3,2,1,0:T(8,128)S(1)} %bitcast.82, ...), custom_call_target="tpu_custom_call" | custom-call | tf_op jit(solution)/shard_map/forecast/pallas_call | solution.py:65
  55.1 3.3 %collective-permute-done.6.beside_ref = bf16[16,16,1024]{2,1,0:T(8,128)(2,1)} collective-permute-done((bf16[16,16,1024]{2,1,0:T(8,128)(2,1)S(1)}, bf16[16,16,1024]{2,1,0:T(8,128)(2,1)}, u32[]{:S(2)}, u32[]{:S(2)}) %collective-permute-start.6) | collective-permute-done | bytes 524320 | tf_op jit(solution)/shard_map/ppermute | solution.py:462
  58.4 4.0 %collective-permute-start.7 = (bf16[16,16,1024]{2,1,0:T(8,128)(2,1)}, bf16[16,16,1024]{2,1,0:T(8,128)(2,1)}, u32[]{:S(2)}, u32[]{:S(2)}) collective-permute-start(bf16[16,16,1024]{2,1,0:T(8,128)(2,1)} %collective-permute-done.6.beside_ref), channel_id=1, source_target_pairs={{0,2},{2,4},{4,6},{3,1},{5,3},{7,5},{8,10},{10,12},{12,14},{11,9},... | collective-permute-start | bytes 1572872 | tf_op jit(solution)/shard_map/ppermute | solution.py:465
  64.0 4.0 %collective-permute-start.9 = (bf16[8,16,1024]{2,1,0:T(8,128)(2,1)}, bf16[8,16,1024]{2,1,0:T(8,128)(2,1)S(1)}, u32[]{:S(2)}, u32[]{:S(2)}) collective-permute-start(bf16[8,16,1024]{2,1,0:T(8,128)(2,1)} %collective-permute-done.8.beside_ref), channel_id=1, source_target_pairs={{0,2},{2,4},{4,6},{3,1},{5,3},{7,5},{8,10},{10,12},{12,14},{11,9},... | collective-permute-start | bytes 786440 | tf_op jit(solution)/shard_map/ppermute | solution.py:465
  68.1 3.7 %forecast.7 = bf16[8,2,8,16,128]{4,3,2,1,0:T(8,128)(2,1)S(1)} custom-call(s32[1]{0:T(128)} %bitcast.3.odd_ref, bf16[16,16,1024]{2,1,0:T(8,128)(2,1)S(1)} %bitcast.95, bf16[16,16,1024]{2,1,0:T(8,128)(2,1)} %collective-permute-done.4.beside_ref, bf16[16,16,1024]{2,1,0:T(8,128)(2,1)} %collective-permute-done.5.beyond_ref, f32[3,2,32,1024]{3,2,1,0:T(8,128)S(1)} %bitcast.83, ...), custom_call_target="tpu_custom_call" | custom-call | tf_op jit(solution)/shard_map/forecast/pallas_call | solution.py:65
  71.9 3.3 %collective-permute-done.9.beyond_ref = bf16[8,16,1024]{2,1,0:T(8,128)(2,1)S(1)} collective-permute-done((bf16[8,16,1024]{2,1,0:T(8,128)(2,1)}, bf16[8,16,1024]{2,1,0:T(8,128)(2,1)S(1)}, u32[]{:S(2)}, u32[]{:S(2)}) %collective-permute-start.9) | collective-permute-done | bytes 262176 | tf_op jit(solution)/shard_map/ppermute | solution.py:465
  77.4 3.7 %forecast.8 = bf16[8,2,8,16,128]{4,3,2,1,0:T(8,128)(2,1)S(1)} custom-call(s32[1]{0:T(128)} %bitcast.3.odd_ref, bf16[16,16,1024]{2,1,0:T(8,128)(2,1)S(1)} %bitcast.93, bf16[16,16,1024]{2,1,0:T(8,128)(2,1)} %collective-permute-done.6.beside_ref, bf16[16,16,1024]{2,1,0:T(8,128)(2,1)} %collective-permute-done.7.beyond_ref, f32[3,2,32,1024]{3,2,1,0:T(8,128)S(1)} %bitcast.85, ...), custom_call_target="tpu_custom_call" | custom-call | tf_op jit(solution)/shard_map/forecast/pallas_call | solution.py:65
  81.1 6.7 %observe.1 = bf16[32,16,128]{2,1,0:T(8,128)(2,1)S(1)} custom-call(s32[8,8,128]{2,1,0:T(8,128)S(1)} %bitcast.99, bf16[64,16,128]{2,1,0:T(8,128)(2,1)S(1)} %bitcast.90, bf16[128,16,128]{2,1,0:T(8,128)(2,1)S(1)} %bitcast.87, bf16[128,16,128]{2,1,0:T(8,128)(2,1)S(1)} %bitcast.88, bf16[128,16,128]{2,1,0:T(8,128)(2,1)S(1)} %bitcast.89, ...), custom_call_target="tpu_custom_call" | custom-call | tf_op jit(solution)/shard_map/observe/pallas_call | solution.py:119
  87.9 3.6 %collective-permute-start.11 = (bf16[40,16,128]{2,1,0:T(8,128)(2,1)S(1)}, bf16[40,16,128]{2,1,0:T(8,128)(2,1)S(1)}, u32[]{:S(2)}, u32[]{:S(2)}) collective-permute-start(bf16[40,16,128]{2,1,0:T(8,128)(2,1)S(1)} %get-tuple-element.37), channel_id=1, source_target_pairs={{1,0},{2,1},{3,2},{4,3},{5,4},{6,5},{7,6},{9,8},{10,9},{11,10},{12... | collective-permute-start | bytes 491528 | tf_op jit(solution)/shard_map/ppermute | solution.py:477
  93.9 4.5 %collective-permute-done.10 = bf16[40,16,128]{2,1,0:T(8,128)(2,1)S(1)} collective-permute-done((bf16[40,16,128]{2,1,0:T(8,128)(2,1)S(1)}, bf16[40,16,128]{2,1,0:T(8,128)(2,1)S(1)}, u32[]{:S(2)}, u32[]{:S(2)}) %collective-permute-start.10) | collective-permute-done | bytes 163872 | tf_op jit(solution)/shard_map/ppermute | solution.py:477
  102.1 3.2 %collective-permute-done.12 = bf16[1,3,32,16,128]{4,3,2,1,0:T(8,128)(2,1)S(1)} collective-permute-done((bf16[1,3,32,16,128]{4,3,2,1,0:T(8,128)(2,1)S(1)}, bf16[1,3,32,16,128]{4,3,2,1,0:T(8,128)(2,1)S(1)}, u32[]{:S(2)}, u32[]{:S(2)}) %collective-permute-start.12) | collective-permute-done | bytes 393248 | tf_op jit(solution)/shard_map/ppermute | solution.py:487
  105.3 8.3 %collective-permute-start.13 = (bf16[2,3,32,16,128]{4,3,2,1,0:T(8,128)(2,1)S(1)}, bf16[2,3,32,16,128]{4,3,2,1,0:T(8,128)(2,1)S(1)}, u32[]{:S(2)}, u32[]{:S(2)}) collective-permute-start(bf16[2,3,32,16,128]{4,3,2,1,0:T(8,128)(2,1)S(1)} %pad_maximum_fusion), channel_id=1, source_target_pairs={{0,8},{8,0},{16,24},{24,16},{1,9},{9,1},{17,25},{25,17},{2,10},{10... | collective-permute-start | bytes 2359304 | tf_op jit(solution)/shard_map/ppermute | solution.py:487
  116.9 4.1 %all-to-all-start = ((bf16[4,32,2,2,16,128]{5,4,3,2,1,0:T(8,128)(2,1)}), bf16[4,32,2,2,16,128]{5,4,3,2,1,0:T(8,128)(2,1)S(1)}, u32[]{:S(2)}, u32[]{:S(2)}) async-start(bf16[4,32,2,2,16,128]{5,4,3,2,1,0:T(8,128)(2,1)} %bitcast.100), calls=%async_computation | async-start | bytes 4194304 | tf_op jit(solution)/shard_map/all_to_all | solution.py:498
  122.4 40.5 %transforms.1.transform_ref = f32[64,64,256]{2,1,0:T(8,128)S(1)} custom-call(s32[4]{0:T(128)S(1)} %shift-left_add_fusion.slot_ref, bf16[4,3,32,16,128]{4,3,2,1,0:T(8,128)(2,1)S(1)} %copy-done.3, f32[3,2,32,128]{3,2,1,0:T(8,128)S(1)} %fusion.6.obs_ref, f32[2,128,128]{2,1,0:T(8,128)S(1)} %fusion.4.wgt_ref, s32[16,16,128]{2,1,0:T(8,128)S(1)} %bitcast.98), custom_call_target="tpu_custom_call" | custom-call | tf_op jit(solution)/shard_map/transforms/pallas_call | solution.py:326
  167.0 9.1 %update.1 = bf16[32,2,64,256]{3,2,1,0:T(8,128)(2,1)S(1)} custom-call(bf16[4,32,2,2,16,128]{5,4,3,2,1,0:T(8,128)(2,1)S(1)} %all-to-all-done.state_ref, f32[64,64,256]{2,1,0:T(8,128)S(1)} %copy-done.1), custom_call_target="tpu_custom_call" | custom-call | tf_op jit(solution)/shard_map/update/pallas_call | solution.py:400
  176.1 3.5 %copy.31 = bf16[64,32,2,256]{3,2,1,0:T(2,128)(2,1)} copy(bf16[64,32,2,256]{3,0,2,1:T(8,128)(2,1)S(1)} %bitcast.86) | data formatting | bytes 4194304 | tf_op jit(solution)/shard_map/transpose | solution.py:500
  (80 shorter events, 29.2 us)
Async XLA Ops:
  0.0 4.0 %copy-start.6 = (f32[3,32,2,1024]{3,2,1,0:T(2,128)S(1)}, f32[3,32,2,1024]{3,2,1,0:T(2,128)}, u32[]{:S(2)}) copy-start(f32[3,32,2,1024]{3,2,1,0:T(2,128)} %param.9) | copy-start | bytes 2359300
  4.7 23.4 %copy-start.4 = (bf16[8,2,16,1024]{3,2,1,0:T(8,128)(2,1)}, bf16[8,2,16,1024]{3,2,1,0:T(8,128)(2,1)S(1)}, u32[]{:S(2)}) copy-start(bf16[8,2,16,1024]{3,2,1,0:T(8,128)(2,1)S(1)} %copy.19) | copy-start | bytes 1572868
  6.2 15.8 %collective-permute-start = (bf16[20,16,1024]{2,1,0:T(8,128)(2,1)S(1)}, bf16[20,16,1024]{2,1,0:T(8,128)(2,1)}, u32[]{:S(2)}, u32[]{:S(2)}) collective-permute-start(bf16[20,16,1024]{2,1,0:T(8,128)(2,1)S(1)} %pad_maximum_fusion.1.own_ref), channel_id=1, source_target_pairs={{0,1},{1,0},{2,3},{3,2},{4,5},{5,4},{6,7},{7,6},{8,9},{9,8},{10,11... | collective-permute-start | bytes 1966088 | tf_op jit(solution)/shard_map/ppermute | solution.py:462
  22.0 19.3 %collective-permute-start.1 = (bf16[20,16,1024]{2,1,0:T(8,128)(2,1)}, bf16[20,16,1024]{2,1,0:T(8,128)(2,1)}, u32[]{:S(2)}, u32[]{:S(2)}) collective-permute-start(bf16[20,16,1024]{2,1,0:T(8,128)(2,1)} %collective-permute-done.beside_ref), channel_id=1, source_target_pairs={{0,2},{2,4},{4,6},{3,1},{5,3},{7,5},{8,10},{10,12},{12,14},{11,9},... | collective-permute-start | bytes 1966088 | tf_op jit(solution)/shard_map/ppermute | solution.py:464
  25.2 11.8 %collective-permute-start.2 = (bf16[16,16,1024]{2,1,0:T(8,128)(2,1)S(1)}, bf16[16,16,1024]{2,1,0:T(8,128)(2,1)}, u32[]{:S(2)}, u32[]{:S(2)}) collective-permute-start(bf16[16,16,1024]{2,1,0:T(8,128)(2,1)S(1)} %bitcast.96), channel_id=1, source_target_pairs={{0,1},{1,0},{2,3},{3,2},{4,5},{5,4},{6,7},{7,6},{8,9},{9,8},{10,11... | collective-permute-start | bytes 1572872 | tf_op jit(solution)/shard_map/ppermute | solution.py:462
  25.4 22.8 %collective-permute-start.4 = (bf16[16,16,1024]{2,1,0:T(8,128)(2,1)S(1)}, bf16[16,16,1024]{2,1,0:T(8,128)(2,1)}, u32[]{:S(2)}, u32[]{:S(2)}) collective-permute-start(bf16[16,16,1024]{2,1,0:T(8,128)(2,1)S(1)} %bitcast.94), channel_id=1, source_target_pairs={{0,1},{1,0},{2,3},{3,2},{4,5},{5,4},{6,7},{7,6},{8,9},{9,8},{10,11... | collective-permute-start | bytes 1572872 | tf_op jit(solution)/shard_map/ppermute | solution.py:462
  37.0 14.4 %collective-permute-start.3 = (bf16[16,16,1024]{2,1,0:T(8,128)(2,1)}, bf16[16,16,1024]{2,1,0:T(8,128)(2,1)S(1)}, u32[]{:S(2)}, u32[]{:S(2)}) collective-permute-start(bf16[16,16,1024]{2,1,0:T(8,128)(2,1)} %collective-permute-done.2.beside_ref), channel_id=1, source_target_pairs={{0,2},{2,4},{4,6},{3,1},{5,3},{7,5},{8,10},{10,12},{12,14},{11,9},... | collective-permute-start | bytes 1572872 | tf_op jit(solution)/shard_map/ppermute | solution.py:464
  42.5 2.7 %copy-start.9 = (f32[4096]{0:T(1024)S(1)}, f32[4096]{0:T(1024)}, u32[]{:S(2)}) copy-start(f32[4096]{0:T(1024)} %param.11) | copy-start | bytes 49156
  42.5 2.7 %copy-start.10 = (f32[4096]{0:T(1024)S(1)}, f32[4096]{0:T(1024)}, u32[]{:S(2)}) copy-start(f32[4096]{0:T(1024)} %param.10) | copy-start | bytes 49156
  42.5 8.9 %copy-start.5 = (bf16[8,2,16,1024]{3,2,1,0:T(8,128)(2,1)S(1)}, bf16[8,2,16,1024]{3,2,1,0:T(8,128)(2,1)}, u32[]{:S(2)}) copy-start(bf16[8,2,16,1024]{3,2,1,0:T(8,128)(2,1)} %copy-done.4) | copy-start | bytes 1572868
  45.2 22.9 %copy-start.11 = (s32[4096]{0:T(1024)S(1)}, s32[4096]{0:T(1024)}, u32[]{:S(2)}) copy-start(s32[4096]{0:T(1024)} %param.12) | copy-start | bytes 49156
  45.2 13.2 %collective-permute-start.6 = (bf16[16,16,1024]{2,1,0:T(8,128)(2,1)S(1)}, bf16[16,16,1024]{2,1,0:T(8,128)(2,1)}, u32[]{:S(2)}, u32[]{:S(2)}) collective-permute-start(bf16[16,16,1024]{2,1,0:T(8,128)(2,1)S(1)} %bitcast.92), channel_id=1, source_target_pairs={{0,1},{1,0},{2,3},{3,2},{4,5},{5,4},{6,7},{7,6},{8,9},{9,8},{10,11... | collective-permute-start | bytes 1572872 | tf_op jit(solution)/shard_map/ppermute | solution.py:462
  48.2 19.9 %collective-permute-start.5 = (bf16[16,16,1024]{2,1,0:T(8,128)(2,1)}, bf16[16,16,1024]{2,1,0:T(8,128)(2,1)}, u32[]{:S(2)}, u32[]{:S(2)}) collective-permute-start(bf16[16,16,1024]{2,1,0:T(8,128)(2,1)} %collective-permute-done.4.beside_ref), channel_id=1, source_target_pairs={{0,2},{2,4},{4,6},{3,1},{5,3},{7,5},{8,10},{10,12},{12,14},{11,9},... | collective-permute-start | bytes 1572872 | tf_op jit(solution)/shard_map/ppermute | solution.py:464
  55.0 9.0 %collective-permute-start.8 = (bf16[8,16,1024]{2,1,0:T(8,128)(2,1)}, bf16[8,16,1024]{2,1,0:T(8,128)(2,1)}, u32[]{:S(2)}, u32[]{:S(2)}) collective-permute-start(bf16[8,16,1024]{2,1,0:T(8,128)(2,1)} %bitcast.11.own_ref), channel_id=1, source_target_pairs={{0,1},{1,0},{2,3},{3,2},{4,5},{5,4},{6,7},{7,6},{8,9},{9,8},{10,11... | collective-permute-start | bytes 786440 | tf_op jit(solution)/shard_map/ppermute | solution.py:462
  58.4 19.0 %collective-permute-start.7 = (bf16[16,16,1024]{2,1,0:T(8,128)(2,1)}, bf16[16,16,1024]{2,1,0:T(8,128)(2,1)}, u32[]{:S(2)}, u32[]{:S(2)}) collective-permute-start(bf16[16,16,1024]{2,1,0:T(8,128)(2,1)} %collective-permute-done.6.beside_ref), channel_id=1, source_target_pairs={{0,2},{2,4},{4,6},{3,1},{5,3},{7,5},{8,10},{10,12},{12,14},{11,9},... | collective-permute-start | bytes 1572872 | tf_op jit(solution)/shard_map/ppermute | solution.py:465
  64.0 11.1 %collective-permute-start.9 = (bf16[8,16,1024]{2,1,0:T(8,128)(2,1)}, bf16[8,16,1024]{2,1,0:T(8,128)(2,1)S(1)}, u32[]{:S(2)}, u32[]{:S(2)}) collective-permute-start(bf16[8,16,1024]{2,1,0:T(8,128)(2,1)} %collective-permute-done.8.beside_ref), channel_id=1, source_target_pairs={{0,2},{2,4},{4,6},{3,1},{5,3},{7,5},{8,10},{10,12},{12,14},{11,9},... | collective-permute-start | bytes 786440 | tf_op jit(solution)/shard_map/ppermute | solution.py:465
  87.9 6.1 %collective-permute-start.11 = (bf16[40,16,128]{2,1,0:T(8,128)(2,1)S(1)}, bf16[40,16,128]{2,1,0:T(8,128)(2,1)S(1)}, u32[]{:S(2)}, u32[]{:S(2)}) collective-permute-start(bf16[40,16,128]{2,1,0:T(8,128)(2,1)S(1)} %get-tuple-element.37), channel_id=1, source_target_pairs={{1,0},{2,1},{3,2},{4,3},{5,4},{6,5},{7,6},{9,8},{10,9},{11,10},{12... | collective-permute-start | bytes 491528 | tf_op jit(solution)/shard_map/ppermute | solution.py:477
  91.5 7.0 %collective-permute-start.10 = (bf16[40,16,128]{2,1,0:T(8,128)(2,1)S(1)}, bf16[40,16,128]{2,1,0:T(8,128)(2,1)S(1)}, u32[]{:S(2)}, u32[]{:S(2)}) collective-permute-start(bf16[40,16,128]{2,1,0:T(8,128)(2,1)S(1)} %get-tuple-element.37), channel_id=1, source_target_pairs={{0,1},{1,2},{2,3},{3,4},{4,5},{5,6},{6,7},{8,9},{9,10},{10,11},{11... | collective-permute-start | bytes 491528 | tf_op jit(solution)/shard_map/ppermute | solution.py:477
  98.6 6.7 %collective-permute-start.12 = (bf16[1,3,32,16,128]{4,3,2,1,0:T(8,128)(2,1)S(1)}, bf16[1,3,32,16,128]{4,3,2,1,0:T(8,128)(2,1)S(1)}, u32[]{:S(2)}, u32[]{:S(2)}) collective-permute-start(bf16[1,3,32,16,128]{4,3,2,1,0:T(8,128)(2,1)S(1)} %slice_bitcast_fusion), channel_id=1, source_target_pairs={{0,16},{8,24},{16,0},{24,8},{1,17},{9,25},{17,1},{25,9},{2,18},{10... | collective-permute-start | bytes 1179656 | tf_op jit(solution)/shard_map/ppermute | solution.py:487
  105.3 10.2 %collective-permute-start.13 = (bf16[2,3,32,16,128]{4,3,2,1,0:T(8,128)(2,1)S(1)}, bf16[2,3,32,16,128]{4,3,2,1,0:T(8,128)(2,1)S(1)}, u32[]{:S(2)}, u32[]{:S(2)}) collective-permute-start(bf16[2,3,32,16,128]{4,3,2,1,0:T(8,128)(2,1)S(1)} %pad_maximum_fusion), channel_id=1, source_target_pairs={{0,8},{8,0},{16,24},{24,16},{1,9},{9,1},{17,25},{25,17},{2,10},{10... | collective-permute-start | bytes 2359304 | tf_op jit(solution)/shard_map/ppermute | solution.py:487
  116.9 4.1 %copy-start.7 = (s32[2,128,128]{2,1,0:T(8,128)S(1)}, s32[2,128,128]{2,1,0:T(8,128)}, u32[]{:S(2)}) copy-start(s32[2,128,128]{2,1,0:T(8,128)} %param.13) | copy-start | bytes 393220
  116.9 4.2 %copy-start.8 = (f32[2,128,128]{2,1,0:T(8,128)S(1)}, f32[2,128,128]{2,1,0:T(8,128)}, u32[]{:S(2)}) copy-start(f32[2,128,128]{2,1,0:T(8,128)} %param.15) | copy-start | bytes 393220
  116.9 4.2 %copy-start.12 = (s32[2,128]{1,0:T(2,128)S(1)}, s32[2,128]{1,0:T(2,128)}, u32[]{:S(2)}) copy-start(s32[2,128]{1,0:T(2,128)} %param.14) | copy-start | bytes 3076
  116.9 47.9 %all-to-all-start = ((bf16[4,32,2,2,16,128]{5,4,3,2,1,0:T(8,128)(2,1)}), bf16[4,32,2,2,16,128]{5,4,3,2,1,0:T(8,128)(2,1)S(1)}, u32[]{:S(2)}, u32[]{:S(2)}) async-start(bf16[4,32,2,2,16,128]{5,4,3,2,1,0:T(8,128)(2,1)} %bitcast.100), calls=%async_computation | async-start | bytes 4194304 | tf_op jit(solution)/shard_map/all_to_all | solution.py:498
  (4 other events, 6.7 us)

commit v5 on v4

--- a/solution.py
+++ b/solution.py
@@ -35,6 +35,7 @@
 def forecast_kernel(first, odd_ref, own_ref, beside_ref, beyond_ref, coef_ref, cprev_ref, cnext_ref, field_ref):
     levels, width = field_ref.shape[0], own_ref.shape[2]
     odd = odd_ref[0] == 1
+    share = cprev_ref.shape[2]
 
     def level(z, carry):
         beside = [beside_ref[2 * z + r].astype(F32) for r in range(2)]
@@ -44,10 +45,10 @@
         rows += [jnp.where(odd, beyond[r], beside[r]) for r in range(2)]
         at = pl.ds(first + z, 1)
         coeffs = [
-            [cprev_ref[k, at, :] for k in range(3)],
+            [cprev_ref[(first + z) // share, k, pl.ds((first + z) % share, 1), :] for k in range(3)],
             [coef_ref[k, 0, at, :] for k in range(3)],
             [coef_ref[k, 1, at, :] for k in range(3)],
-            [cnext_ref[k, at, :] for k in range(3)],
+            [cnext_ref[(first + z) // share, k, pl.ds((first + z) % share, 1), :] for k in range(3)],
         ]
         once = [advance(rows[i + 2], rows[i], rows[i + 1], coeffs[i]) for i in range(4)]
         for r in range(2):
@@ -440,25 +441,28 @@
     coef = jnp.transpose(coefficients, (0, 2, 1, 3))
     spans = cuts(levels)
     pieces = [own[first:last].reshape(-1, members, columns) for first, last in spans]
-    extra = coef.astype(BF16).reshape(-1, members, columns)
-    pieces[0] = jnp.concatenate([pieces[0], extra], 0)
-    pieces = lax.optimization_barrier(pieces)
     flag = odd.astype(jnp.int32).reshape(1)
+    share = levels // groups
+    mine = lax.dynamic_slice_in_dim(coef, me * share, share, axis=2).astype(BF16)
+    near = lax.ppermute(mine, "slab", swap)
+    far = lax.ppermute(near, "slab", skip)
+    sides = lax.all_gather(jnp.stack([near, far]), "mem", axis=0, tiled=False)
+    cprev = jnp.where(odd, sides[:, 0, :, 1], sides[:, 1, :, 1]).astype(F32)
+    cnext = jnp.where(odd, sides[:, 1, :, 0], sides[:, 0, :, 0]).astype(F32)
+
     besides, beyonds, fields = [], [], []
 
     def advance_piece(i):
-        nonlocal cprev, cnext
-        if i == 0:
-            sides = [x[0][-extra.shape[0] :].reshape(coef.shape).astype(F32) for x in (besides, beyonds)]
-            cprev = jnp.where(odd, sides[0][:, 1], sides[1][:, 1])
-            cnext = jnp.where(odd, sides[1][:, 0], sides[0][:, 0])
         fields.append(forecast(spans[i], flag, pieces[i], besides[i], beyonds[i], coef, cprev, cnext))
 
-    cprev = cnext = None
     for i, piece in enumerate(pieces):
-        if i >= 3:
-            advance_piece(i - 3)
-            fields[i - 3], piece = lax.optimization_barrier((fields[i - 3], piece))
+        if i == 2:
+            far, piece = lax.optimization_barrier((far, piece))
+        if i == 3:
+            beyonds[0], piece = lax.optimization_barrier((beyonds[0], piece))
+        if i >= 4:
+            advance_piece(i - 4)
+            fields[i - 4], beyonds[i - 3], piece = lax.optimization_barrier((fields[i - 4], beyonds[i - 3], piece))
         besides.append(lax.ppermute(piece, "slab", swap))
         if i >= 2:
             beyonds.append(lax.ppermute(besides[i - 2], "slab", skip))

time: 180 us -> 172 us (0.956); the launches traced: 180 us -> 170 us
  waiting for transfers between devices: 44.1 us -> 21.7 us
  blocking collectives: 0 us -> 11.5 us
  local copies, waits for them, and re-layouts: 22.2 us -> 26.9 us
  starting transfers between devices: 39.8 us -> 36.7 us
    ppermute x5, waiting for transfers between devices: 30.9 us -> 3.98 us  [on_device(): besides.append(lax.ppermute(piece, 'slab', swap))]
    all_gather x0 -> x1, blocking collectives: none -> 11.5 us  [on_device(): sides = lax.all_gather(jnp.stack([near, far]), 'mem', axis=0, tiled=False)]
    ppermute x2, starting transfers between devices: 9.54 us -> 3.5 us  [on_device(): lax.ppermute(ens, 'mem', [(i, i ^ distance) for i in range(groups)])]
    ppermute x0 -> x2, starting transfers between devices: none -> 4.51 us  [the longest x1 3.21 us: on_device(): far = lax.ppermute(near, 'slab', skip)]
    slice x7, local copies, waits for them, and re-layouts: 5.87 us -> 9.83 us  [on_device(): own[first:last].reshape(-1, members, columns)]
    unnamed x33 -> x45, local copies, waits for them, and re-layouts: 8.45 us -> 11.2 us
    ppermute x2, waiting for transfers between devices: 4.93 us -> 7.67 us  [on_device(): lax.ppermute(ens, 'mem', [(i, i ^ distance) for i in range(groups)])]
    ppermute x2, waiting for transfers between devices: 3.25 us -> 5.52 us  [on_device(): beyonds += [lax.ppermute(beside, 'slab', skip) for beside in besides[-2:]]]
  transfers between devices with their start and end apart: 15 -> 17, of which waited for: 10 -> 9; matrix products, arithmetic and copies ran while one was open for 4% -> 8% of each run, Pallas kernels for 29% -> 31%
where the time goes in v5:
time: 172 us; the launch traced here: 170 us
  Pallas kernels  70.8 us (41%)
  starting transfers between devices  36.7 us (21%)
  local copies, waits for them, and re-layouts  26.9 us (16%)
  waiting for transfers between devices  21.7 us (13%)
  blocking collectives  11.5 us (7%)
    pallas_call x1, Pallas kernels, transforms(): pl.pallas_call(transform_kernel, out_shape=jax.ShapeDtypeStruct((pairs, 6...  40.5 us
    pallas_call x5, Pallas kernels, forecast(): pl.pallas_call(functools.partial(forecast_kernel, first), out_shape=jax.S...  14.5 us
    all_gather x1, blocking collectives, on_device(): sides = lax.all_gather(jnp.stack([near, far]), 'mem', axis=0, tiled=False)  11.5 us
    unnamed x45, local copies, waits for them, and re-layouts  11.2 us
    slice x7, local copies, waits for them, and re-layouts, on_device(): own[first:last].reshape(-1, members, columns)  9.83 us
    ppermute x3, starting transfers between devices, on_device(): beyonds.append(lax.ppermute(besides[i - 2], 'slab', skip))  9.6 us
    pallas_call x1, Pallas kernels, update(): pl.pallas_call(update_kernel, out_shape=jax.ShapeDtypeStruct((levels, row...  9.12 us
    ppermute x2, waiting for transfers between devices, on_device(): lax.ppermute(ens, 'mem', [(i, i ^ distance) for i in range(groups)])  7.67 us
  transfers between devices with their start and end apart: 17, of which 9 were waited for; matrix products, arithmetic and copies ran while one was open for 8% of the time, Pallas kernels for 31%

profile of v5, /device:TPU:9, one launch (start us, length us, event | category | flops | bytes accessed | tf_op | source)
XLA Modules:
  0.0 169.6 jit_solution(829855798301738136)
XLA Ops:
  5.4 3.8 %fusion.18 = (bf16[8,2,16,1024]{3,1,0,2:T(2,128)(2,1)}, bf16[8,2,16,1024]{3,1,0,2:T(2,128)(2,1)S(1)}, bf16[8,2,16,1024]{3,1,0,2:T(2,128)(2,1)S(1)}) fusion(bf16[32,2,16,1024]{3,1,0,2:T(2,128)(2,1)} %bitcast.113), kind=kLoop, calls=%fused_computation.60 | loop fusion | bytes 3145728 | tf_op jit(solution)/shard_map/slice | solution.py:443
  10.8 3.2 %collective-permute-start.3 = (bf16[3,2,8,1024]{3,2,1,0:T(8,128)(2,1)S(1)}, bf16[3,2,8,1024]{3,2,1,0:T(8,128)(2,1)}, u32[]{:S(2)}, u32[]{:S(2)}) collective-permute-start(bf16[3,2,8,1024]{3,2,1,0:T(8,128)(2,1)S(1)} %collective-permute-done.2), channel_id=1, source_target_pairs={{0,2},{2,4},{4,6},{3,1},{5,3},{7,5},{8,10},{10,12},{12,14},{11,9},... | collective-permute-start | bytes 294920 | tf_op jit(solution)/shard_map/ppermute | solution.py:448
  14.0 3.2 %collective-permute-start.1 = (bf16[8,16,1024]{2,1,0:T(8,128)(2,1)S(1)}, bf16[8,16,1024]{2,1,0:T(8,128)(2,1)S(1)}, u32[]{:S(2)}, u32[]{:S(2)}) collective-permute-start(bf16[8,16,1024]{2,1,0:T(8,128)(2,1)S(1)} %collective-permute-done.beside_ref), channel_id=1, source_target_pairs={{0,2},{2,4},{4,6},{3,1},{5,3},{7,5},{8,10},{10,12},{12,14},{11,9},... | collective-permute-start | bytes 786440 | tf_op jit(solution)/shard_map/ppermute | solution.py:468
  23.6 3.2 %collective-permute-start.5 = (bf16[16,16,1024]{2,1,0:T(8,128)(2,1)}, bf16[16,16,1024]{2,1,0:T(8,128)(2,1)S(1)}, u32[]{:S(2)}, u32[]{:S(2)}) collective-permute-start(bf16[16,16,1024]{2,1,0:T(8,128)(2,1)} %collective-permute-done.4.beside_ref), channel_id=1, source_target_pairs={{0,2},{2,4},{4,6},{3,1},{5,3},{7,5},{8,10},{10,12},{12,14},{11,9},... | collective-permute-start | bytes 1572872 | tf_op jit(solution)/shard_map/ppermute | solution.py:468
  26.8 11.5 %all-gather = bf16[8,3,2,8,1024]{4,3,2,1,0:T(8,128)(2,1)S(1)} all-gather(bf16[2,3,2,8,1024]{4,3,2,1,0:T(8,128)(2,1)S(1)} %pad_maximum_fusion.2), channel_id=2, replica_groups=mesh['mem'=4,'slab'=8] {'mem'}, dimensions={0}, use_global_device_ids=true | all-gather | bytes 983040 | tf_op jit(solution)/shard_map/all_gather | solution.py:449
  40.6 3.2 %collective-permute-start.7 = (bf16[16,16,1024]{2,1,0:T(8,128)(2,1)}, bf16[16,16,1024]{2,1,0:T(8,128)(2,1)}, u32[]{:S(2)}, u32[]{:S(2)}) collective-permute-start(bf16[16,16,1024]{2,1,0:T(8,128)(2,1)} %collective-permute-done.6.beside_ref), channel_id=1, source_target_pairs={{0,2},{2,4},{4,6},{3,1},{5,3},{7,5},{8,10},{10,12},{12,14},{11,9},... | collective-permute-start | bytes 1572872 | tf_op jit(solution)/shard_map/ppermute | solution.py:468
  45.6 3.7 %collective-permute-start.9 = (bf16[16,16,1024]{2,1,0:T(8,128)(2,1)}, bf16[16,16,1024]{2,1,0:T(8,128)(2,1)}, u32[]{:S(2)}, u32[]{:S(2)}) collective-permute-start(bf16[16,16,1024]{2,1,0:T(8,128)(2,1)} %collective-permute-done.8.beside_ref), channel_id=1, source_target_pairs={{0,2},{2,4},{4,6},{3,1},{5,3},{7,5},{8,10},{10,12},{12,14},{11,9},... | collective-permute-start | bytes 1572872 | tf_op jit(solution)/shard_map/ppermute | solution.py:469
  49.4 3.0 %collective-permute-done.10.beside_ref = bf16[8,16,1024]{2,1,0:T(8,128)(2,1)} collective-permute-done((bf16[8,16,1024]{2,1,0:T(8,128)(2,1)}, bf16[8,16,1024]{2,1,0:T(8,128)(2,1)}, u32[]{:S(2)}, u32[]{:S(2)}) %collective-permute-start.10) | collective-permute-done | bytes 262176 | tf_op jit(solution)/shard_map/ppermute | solution.py:466
  52.4 2.9 %collective-permute-start.11 = (bf16[8,16,1024]{2,1,0:T(8,128)(2,1)}, bf16[8,16,1024]{2,1,0:T(8,128)(2,1)S(1)}, u32[]{:S(2)}, u32[]{:S(2)}) collective-permute-start(bf16[8,16,1024]{2,1,0:T(8,128)(2,1)} %collective-permute-done.10.beside_ref), channel_id=1, source_target_pairs={{0,2},{2,4},{4,6},{3,1},{5,3},{7,5},{8,10},{10,12},{12,14},{11,9},... | collective-permute-start | bytes 786440 | tf_op jit(solution)/shard_map/ppermute | solution.py:469
  56.4 3.6 %forecast.6 = bf16[8,2,8,16,128]{4,3,2,1,0:T(8,128)(2,1)S(1)} custom-call(s32[1]{0:T(128)} %bitcast.3.odd_ref, bf16[16,16,1024]{2,1,0:T(8,128)(2,1)S(1)} %bitcast.100, bf16[16,16,1024]{2,1,0:T(8,128)(2,1)} %collective-permute-done.4.beside_ref, bf16[16,16,1024]{2,1,0:T(8,128)(2,1)S(1)} %copy-done.7, f32[3,2,32,1024]{3,2,1,0:T(8,128)S(1)} %bitcast.89, ...), custom_call_target="tpu_custom_call" | custom-call | tf_op jit(solution)/shard_map/forecast/pallas_call | solution.py:66
  60.0 3.7 %forecast.7 = bf16[8,2,8,16,128]{4,3,2,1,0:T(8,128)(2,1)S(1)} custom-call(s32[1]{0:T(128)} %bitcast.3.odd_ref, bf16[16,16,1024]{2,1,0:T(8,128)(2,1)S(1)} %bitcast.104, bf16[16,16,1024]{2,1,0:T(8,128)(2,1)} %collective-permute-done.6.beside_ref, bf16[16,16,1024]{2,1,0:T(8,128)(2,1)} %collective-permute-done.7.beyond_ref, f32[3,2,32,1024]{3,2,1,0:T(8,128)S(1)} %bitcast.90, ...), custom_call_target="tpu_custom_call" | custom-call | tf_op jit(solution)/shard_map/forecast/pallas_call | solution.py:66
  63.7 3.7 %collective-permute-done.9.beyond_ref = bf16[16,16,1024]{2,1,0:T(8,128)(2,1)} collective-permute-done((bf16[16,16,1024]{2,1,0:T(8,128)(2,1)}, bf16[16,16,1024]{2,1,0:T(8,128)(2,1)}, u32[]{:S(2)}, u32[]{:S(2)}) %collective-permute-start.9) | collective-permute-done | bytes 524320 | tf_op jit(solution)/shard_map/ppermute | solution.py:469
  67.4 3.7 %forecast.8 = bf16[8,2,8,16,128]{4,3,2,1,0:T(8,128)(2,1)S(1)} custom-call(s32[1]{0:T(128)} %bitcast.3.odd_ref, bf16[16,16,1024]{2,1,0:T(8,128)(2,1)S(1)} %bitcast.102, bf16[16,16,1024]{2,1,0:T(8,128)(2,1)} %collective-permute-done.8.beside_ref, bf16[16,16,1024]{2,1,0:T(8,128)(2,1)} %collective-permute-done.9.beyond_ref, f32[3,2,32,1024]{3,2,1,0:T(8,128)S(1)} %bitcast.91, ...), custom_call_target="tpu_custom_call" | custom-call | tf_op jit(solution)/shard_map/forecast/pallas_call | solution.py:66
  72.9 2.3 %forecast.9 = bf16[4,2,8,16,128]{4,3,2,1,0:T(8,128)(2,1)S(1)} custom-call(s32[1]{0:T(128)} %bitcast.3.odd_ref, bf16[8,16,1024]{2,1,0:T(8,128)(2,1)} %bitcast.15.own_ref, bf16[8,16,1024]{2,1,0:T(8,128)(2,1)} %collective-permute-done.10.beside_ref, bf16[8,16,1024]{2,1,0:T(8,128)(2,1)S(1)} %collective-permute-done.11.beyond_ref, ...), custom_call_target="tpu_custom_call" | custom-call | tf_op jit(solution)/shard_map/forecast/pallas_call | solution.py:66
  75.2 6.7 %observe.1 = bf16[32,16,128]{2,1,0:T(8,128)(2,1)S(1)} custom-call(s32[8,8,128]{2,1,0:T(8,128)S(1)} %bitcast.108, bf16[64,16,128]{2,1,0:T(8,128)(2,1)S(1)} %bitcast.97, bf16[128,16,128]{2,1,0:T(8,128)(2,1)S(1)} %bitcast.94, bf16[128,16,128]{2,1,0:T(8,128)(2,1)S(1)} %bitcast.95, bf16[128,16,128]{2,1,0:T(8,128)(2,1)S(1)} %bitcast.96, ...), custom_call_target="tpu_custom_call" | custom-call | tf_op jit(solution)/shard_map/observe/pallas_call | solution.py:120
  83.9 3.4 %collective-permute-start.12 = (bf16[40,16,128]{2,1,0:T(8,128)(2,1)S(1)}, bf16[40,16,128]{2,1,0:T(8,128)(2,1)S(1)}, u32[]{:S(2)}, u32[]{:S(2)}) collective-permute-start(bf16[40,16,128]{2,1,0:T(8,128)(2,1)S(1)} %get-tuple-element.31), channel_id=1, source_target_pairs={{0,1},{1,2},{2,3},{3,4},{4,5},{5,6},{6,7},{8,9},{9,10},{10,11},{11... | collective-permute-start | bytes 491528 | tf_op jit(solution)/shard_map/ppermute | solution.py:481
  88.6 3.2 %collective-permute-done.12 = bf16[40,16,128]{2,1,0:T(8,128)(2,1)S(1)} collective-permute-done((bf16[40,16,128]{2,1,0:T(8,128)(2,1)S(1)}, bf16[40,16,128]{2,1,0:T(8,128)(2,1)S(1)}, u32[]{:S(2)}, u32[]{:S(2)}) %collective-permute-start.12) | collective-permute-done | bytes 163872 | tf_op jit(solution)/shard_map/ppermute | solution.py:481
  94.4 5.9 %collective-permute-done.14 = bf16[1,3,32,16,128]{4,3,2,1,0:T(8,128)(2,1)S(1)} collective-permute-done((bf16[1,3,32,16,128]{4,3,2,1,0:T(8,128)(2,1)S(1)}, bf16[1,3,32,16,128]{4,3,2,1,0:T(8,128)(2,1)S(1)}, u32[]{:S(2)}, u32[]{:S(2)}) %collective-permute-start.14) | collective-permute-done | bytes 393248 | tf_op jit(solution)/shard_map/ppermute | solution.py:491
  100.4 3.2 %collective-permute-start.15 = (bf16[2,3,32,16,128]{4,3,2,1,0:T(8,128)(2,1)S(1)}, bf16[2,3,32,16,128]{4,3,2,1,0:T(8,128)(2,1)S(1)}, u32[]{:S(2)}, u32[]{:S(2)}) collective-permute-start(bf16[2,3,32,16,128]{4,3,2,1,0:T(8,128)(2,1)S(1)} %pad_maximum_fusion), channel_id=1, source_target_pairs={{0,8},{8,0},{16,24},{24,16},{1,9},{9,1},{17,25},{25,17},{2,10},{10... | collective-permute-start | bytes 2359304 | tf_op jit(solution)/shard_map/ppermute | solution.py:491
  106.9 4.1 %all-to-all-start = ((bf16[4,32,2,2,16,128]{5,4,3,2,1,0:T(8,128)(2,1)}), bf16[4,32,2,2,16,128]{5,4,3,2,1,0:T(8,128)(2,1)S(1)}, u32[]{:S(2)}, u32[]{:S(2)}) async-start(bf16[4,32,2,2,16,128]{5,4,3,2,1,0:T(8,128)(2,1)} %bitcast.109), calls=%async_computation | async-start | bytes 4194304 | tf_op jit(solution)/shard_map/all_to_all | solution.py:502
  112.4 40.5 %transforms.1.transform_ref = f32[64,64,256]{2,1,0:T(8,128)S(1)} custom-call(s32[4]{0:T(128)S(1)} %shift-left_add_fusion.slot_ref, bf16[4,3,32,16,128]{4,3,2,1,0:T(8,128)(2,1)S(1)} %copy-done.3, f32[3,2,32,128]{3,2,1,0:T(8,128)S(1)} %fusion.9.obs_ref, f32[2,128,128]{2,1,0:T(8,128)S(1)} %fusion.6.wgt_ref, s32[16,16,128]{2,1,0:T(8,128)S(1)} %bitcast.107), custom_call_target="tpu_custom_call" | custom-call | tf_op jit(solution)/shard_map/transforms/pallas_call | solution.py:327
  154.8 2.2 %copy-done.1 = f32[64,64,256]{2,1,0:T(8,128)S(1)} copy-done((f32[64,64,256]{2,1,0:T(8,128)S(1)}, f32[64,64,256]{2,1,0:T(8,128)}, u32[]{:S(2)}) %copy-start.1) | copy-done | bytes 4194328
  157.0 9.1 %update.1 = bf16[32,2,64,256]{3,2,1,0:T(8,128)(2,1)S(1)} custom-call(bf16[4,32,2,2,16,128]{5,4,3,2,1,0:T(8,128)(2,1)S(1)} %all-to-all-done.state_ref, f32[64,64,256]{2,1,0:T(8,128)S(1)} %copy-done.1), custom_call_target="tpu_custom_call" | custom-call | tf_op jit(solution)/shard_map/update/pallas_call | solution.py:401
  166.2 3.5 %copy.48 = bf16[64,32,2,256]{3,2,1,0:T(2,128)(2,1)} copy(bf16[64,32,2,256]{3,0,2,1:T(8,128)(2,1)S(1)} %bitcast.93) | data formatting | bytes 4194304 | tf_op jit(solution)/shard_map/transpose | solution.py:504
  (94 shorter events, 32.8 us)
Async XLA Ops:
  1.4 9.4 %collective-permute-start.2 = (bf16[3,2,8,1024]{3,2,1,0:T(8,128)(2,1)S(1)}, bf16[3,2,8,1024]{3,2,1,0:T(8,128)(2,1)S(1)}, u32[]{:S(2)}, u32[]{:S(2)}) collective-permute-start(bf16[3,2,8,1024]{3,2,1,0:T(8,128)(2,1)S(1)} %fusion.7), channel_id=1, source_target_pairs={{0,1},{1,0},{2,3},{3,2},{4,5},{5,4},{6,7},{7,6},{8,9},{9,8},{10,11... | collective-permute-start | bytes 294920 | tf_op jit(solution)/shard_map/ppermute | solution.py:447
  5.0 5.7 %copy-start.15 = (f32[4096]{0:T(1024)S(1)}, f32[4096]{0:T(1024)}, u32[]{:S(2)}) copy-start(f32[4096]{0:T(1024)} %param.11) | copy-start | bytes 49156
  5.1 12.2 %copy-start.12 = (f32[3,32,2,1024]{3,2,1,0:T(2,128)S(1)}, f32[3,32,2,1024]{3,2,1,0:T(2,128)}, u32[]{:S(2)}) copy-start(f32[3,32,2,1024]{3,2,1,0:T(2,128)} %param.9) | copy-start | bytes 2359300
  5.1 8.9 %collective-permute-start = (bf16[8,16,1024]{2,1,0:T(8,128)(2,1)S(1)}, bf16[8,16,1024]{2,1,0:T(8,128)(2,1)S(1)}, u32[]{:S(2)}, u32[]{:S(2)}) collective-permute-start(bf16[8,16,1024]{2,1,0:T(8,128)(2,1)S(1)} %bitcast.105), channel_id=1, source_target_pairs={{0,1},{1,0},{2,3},{3,2},{4,5},{5,4},{6,7},{7,6},{8,9},{9,8},{10,11... | collective-permute-start | bytes 786440 | tf_op jit(solution)/shard_map/ppermute | solution.py:466
  9.4 14.2 %collective-permute-start.4 = (bf16[16,16,1024]{2,1,0:T(8,128)(2,1)S(1)}, bf16[16,16,1024]{2,1,0:T(8,128)(2,1)}, u32[]{:S(2)}, u32[]{:S(2)}) collective-permute-start(bf16[16,16,1024]{2,1,0:T(8,128)(2,1)S(1)} %bitcast.99), channel_id=1, source_target_pairs={{0,1},{1,0},{2,3},{3,2},{4,5},{5,4},{6,7},{7,6},{8,9},{9,8},{10,11... | collective-permute-start | bytes 1572872 | tf_op jit(solution)/shard_map/ppermute | solution.py:466
  10.8 10.2 %collective-permute-start.3 = (bf16[3,2,8,1024]{3,2,1,0:T(8,128)(2,1)S(1)}, bf16[3,2,8,1024]{3,2,1,0:T(8,128)(2,1)}, u32[]{:S(2)}, u32[]{:S(2)}) collective-permute-start(bf16[3,2,8,1024]{3,2,1,0:T(8,128)(2,1)S(1)} %collective-permute-done.2), channel_id=1, source_target_pairs={{0,2},{2,4},{4,6},{3,1},{5,3},{7,5},{8,10},{10,12},{12,14},{11,9},... | collective-permute-start | bytes 294920 | tf_op jit(solution)/shard_map/ppermute | solution.py:448
  14.0 7.0 %copy-start.8 = (bf16[8,16,1024]{2,1,0:T(8,128)(2,1)}, bf16[8,16,1024]{2,1,0:T(8,128)(2,1)S(1)}, u32[]{:S(2)}) copy-start(bf16[8,16,1024]{2,1,0:T(8,128)(2,1)S(1)} %collective-permute-done.beside_ref) | copy-start | bytes 786436
  14.0 8.0 %collective-permute-start.1 = (bf16[8,16,1024]{2,1,0:T(8,128)(2,1)S(1)}, bf16[8,16,1024]{2,1,0:T(8,128)(2,1)S(1)}, u32[]{:S(2)}, u32[]{:S(2)}) collective-permute-start(bf16[8,16,1024]{2,1,0:T(8,128)(2,1)S(1)} %collective-permute-done.beside_ref), channel_id=1, source_target_pairs={{0,2},{2,4},{4,6},{3,1},{5,3},{7,5},{8,10},{10,12},{12,14},{11,9},... | collective-permute-start | bytes 786440 | tf_op jit(solution)/shard_map/ppermute | solution.py:468
  20.7 17.7 %copy-start.5 = (bf16[4,2,16,1024]{3,2,1,0:T(8,128)(2,1)S(1)}, bf16[4,2,16,1024]{3,2,1,0:T(8,128)(2,1)}, u32[]{:S(2)}) copy-start(bf16[4,2,16,1024]{3,2,1,0:T(8,128)(2,1)} %copy-done.4) | copy-start | bytes 786436
  21.0 17.3 %copy-start.9 = (bf16[8,16,1024]{2,1,0:T(8,128)(2,1)S(1)}, bf16[8,16,1024]{2,1,0:T(8,128)(2,1)}, u32[]{:S(2)}) copy-start(bf16[8,16,1024]{2,1,0:T(8,128)(2,1)} %copy-done.8) | copy-start | bytes 786436
  21.0 19.6 %collective-permute-start.6 = (bf16[16,16,1024]{2,1,0:T(8,128)(2,1)S(1)}, bf16[16,16,1024]{2,1,0:T(8,128)(2,1)}, u32[]{:S(2)}, u32[]{:S(2)}) collective-permute-start(bf16[16,16,1024]{2,1,0:T(8,128)(2,1)S(1)} %bitcast.103), channel_id=1, source_target_pairs={{0,1},{1,0},{2,3},{3,2},{4,5},{5,4},{6,7},{7,6},{8,9},{9,8},{10,11... | collective-permute-start | bytes 1572872 | tf_op jit(solution)/shard_map/ppermute | solution.py:466
  22.0 16.2 %copy-start.10 = (bf16[8,16,1024]{2,1,0:T(8,128)(2,1)}, bf16[8,16,1024]{2,1,0:T(8,128)(2,1)S(1)}, u32[]{:S(2)}) copy-start(bf16[8,16,1024]{2,1,0:T(8,128)(2,1)S(1)} %collective-permute-done.1.beyond_ref) | copy-start | bytes 786436
  22.1 23.5 %collective-permute-start.8 = (bf16[16,16,1024]{2,1,0:T(8,128)(2,1)S(1)}, bf16[16,16,1024]{2,1,0:T(8,128)(2,1)}, u32[]{:S(2)}, u32[]{:S(2)}) collective-permute-start(bf16[16,16,1024]{2,1,0:T(8,128)(2,1)S(1)} %bitcast.101), channel_id=1, source_target_pairs={{0,1},{1,0},{2,3},{3,2},{4,5},{5,4},{6,7},{7,6},{8,9},{9,8},{10,11... | collective-permute-start | bytes 1572872 | tf_op jit(solution)/shard_map/ppermute | solution.py:466
  23.6 20.2 %collective-permute-start.5 = (bf16[16,16,1024]{2,1,0:T(8,128)(2,1)}, bf16[16,16,1024]{2,1,0:T(8,128)(2,1)S(1)}, u32[]{:S(2)}, u32[]{:S(2)}) collective-permute-start(bf16[16,16,1024]{2,1,0:T(8,128)(2,1)} %collective-permute-done.4.beside_ref), channel_id=1, source_target_pairs={{0,2},{2,4},{4,6},{3,1},{5,3},{7,5},{8,10},{10,12},{12,14},{11,9},... | collective-permute-start | bytes 1572872 | tf_op jit(solution)/shard_map/ppermute | solution.py:468
  38.3 17.0 %copy-start.17 = (s32[4096]{0:T(1024)S(1)}, s32[4096]{0:T(1024)}, u32[]{:S(2)}) copy-start(s32[4096]{0:T(1024)} %param.12) | copy-start | bytes 49156
  40.6 19.4 %collective-permute-start.7 = (bf16[16,16,1024]{2,1,0:T(8,128)(2,1)}, bf16[16,16,1024]{2,1,0:T(8,128)(2,1)}, u32[]{:S(2)}, u32[]{:S(2)}) collective-permute-start(bf16[16,16,1024]{2,1,0:T(8,128)(2,1)} %collective-permute-done.6.beside_ref), channel_id=1, source_target_pairs={{0,2},{2,4},{4,6},{3,1},{5,3},{7,5},{8,10},{10,12},{12,14},{11,9},... | collective-permute-start | bytes 1572872 | tf_op jit(solution)/shard_map/ppermute | solution.py:468
  44.6 7.8 %collective-permute-start.10 = (bf16[8,16,1024]{2,1,0:T(8,128)(2,1)}, bf16[8,16,1024]{2,1,0:T(8,128)(2,1)}, u32[]{:S(2)}, u32[]{:S(2)}) collective-permute-start(bf16[8,16,1024]{2,1,0:T(8,128)(2,1)} %bitcast.15.own_ref), channel_id=1, source_target_pairs={{0,1},{1,0},{2,3},{3,2},{4,5},{5,4},{6,7},{7,6},{8,9},{9,8},{10,11... | collective-permute-start | bytes 786440 | tf_op jit(solution)/shard_map/ppermute | solution.py:466
  45.6 21.9 %collective-permute-start.9 = (bf16[16,16,1024]{2,1,0:T(8,128)(2,1)}, bf16[16,16,1024]{2,1,0:T(8,128)(2,1)}, u32[]{:S(2)}, u32[]{:S(2)}) collective-permute-start(bf16[16,16,1024]{2,1,0:T(8,128)(2,1)} %collective-permute-done.8.beside_ref), channel_id=1, source_target_pairs={{0,2},{2,4},{4,6},{3,1},{5,3},{7,5},{8,10},{10,12},{12,14},{11,9},... | collective-permute-start | bytes 1572872 | tf_op jit(solution)/shard_map/ppermute | solution.py:469
  52.4 20.6 %collective-permute-start.11 = (bf16[8,16,1024]{2,1,0:T(8,128)(2,1)}, bf16[8,16,1024]{2,1,0:T(8,128)(2,1)S(1)}, u32[]{:S(2)}, u32[]{:S(2)}) collective-permute-start(bf16[8,16,1024]{2,1,0:T(8,128)(2,1)} %collective-permute-done.10.beside_ref), channel_id=1, source_target_pairs={{0,2},{2,4},{4,6},{3,1},{5,3},{7,5},{8,10},{10,12},{12,14},{11,9},... | collective-permute-start | bytes 786440 | tf_op jit(solution)/shard_map/ppermute | solution.py:469
  81.9 6.6 %collective-permute-start.13 = (bf16[40,16,128]{2,1,0:T(8,128)(2,1)S(1)}, bf16[40,16,128]{2,1,0:T(8,128)(2,1)S(1)}, u32[]{:S(2)}, u32[]{:S(2)}) collective-permute-start(bf16[40,16,128]{2,1,0:T(8,128)(2,1)S(1)} %get-tuple-element.31), channel_id=1, source_target_pairs={{1,0},{2,1},{3,2},{4,3},{5,4},{6,5},{7,6},{9,8},{10,9},{11,10},{12... | collective-permute-start | bytes 491528 | tf_op jit(solution)/shard_map/ppermute | solution.py:481
  83.9 7.9 %collective-permute-start.12 = (bf16[40,16,128]{2,1,0:T(8,128)(2,1)S(1)}, bf16[40,16,128]{2,1,0:T(8,128)(2,1)S(1)}, u32[]{:S(2)}, u32[]{:S(2)}) collective-permute-start(bf16[40,16,128]{2,1,0:T(8,128)(2,1)S(1)} %get-tuple-element.31), channel_id=1, source_target_pairs={{0,1},{1,2},{2,3},{3,4},{4,5},{5,6},{6,7},{8,9},{9,10},{10,11},{11... | collective-permute-start | bytes 491528 | tf_op jit(solution)/shard_map/ppermute | solution.py:481
  91.9 8.5 %collective-permute-start.14 = (bf16[1,3,32,16,128]{4,3,2,1,0:T(8,128)(2,1)S(1)}, bf16[1,3,32,16,128]{4,3,2,1,0:T(8,128)(2,1)S(1)}, u32[]{:S(2)}, u32[]{:S(2)}) collective-permute-start(bf16[1,3,32,16,128]{4,3,2,1,0:T(8,128)(2,1)S(1)} %slice_bitcast_fusion), channel_id=1, source_target_pairs={{0,16},{8,24},{16,0},{24,8},{1,17},{9,25},{17,1},{25,9},{2,18},{10... | collective-permute-start | bytes 1179656 | tf_op jit(solution)/shard_map/ppermute | solution.py:491
  100.4 5.1 %collective-permute-start.15 = (bf16[2,3,32,16,128]{4,3,2,1,0:T(8,128)(2,1)S(1)}, bf16[2,3,32,16,128]{4,3,2,1,0:T(8,128)(2,1)S(1)}, u32[]{:S(2)}, u32[]{:S(2)}) collective-permute-start(bf16[2,3,32,16,128]{4,3,2,1,0:T(8,128)(2,1)S(1)} %pad_maximum_fusion), channel_id=1, source_target_pairs={{0,8},{8,0},{16,24},{24,16},{1,9},{9,1},{17,25},{25,17},{2,10},{10... | collective-permute-start | bytes 2359304 | tf_op jit(solution)/shard_map/ppermute | solution.py:491
  106.9 47.9 %all-to-all-start = ((bf16[4,32,2,2,16,128]{5,4,3,2,1,0:T(8,128)(2,1)}), bf16[4,32,2,2,16,128]{5,4,3,2,1,0:T(8,128)(2,1)S(1)}, u32[]{:S(2)}, u32[]{:S(2)}) async-start(bf16[4,32,2,2,16,128]{5,4,3,2,1,0:T(8,128)(2,1)} %bitcast.109), calls=%async_computation | async-start | bytes 4194304 | tf_op jit(solution)/shard_map/all_to_all | solution.py:502
  (12 other events, 32.2 us)

commit v6 on v5

--- a/solution.py
+++ b/solution.py
@@ -23,19 +23,33 @@
     return pltpu.CompilerParams(vmem_limit_bytes=mib * 1024 * 1024)
 
 
-def advance(upper, lower, center, c):
+def advance(upper, lower, center, w):
     width = center.shape[1]
     east = pltpu.roll(center, width - 1, 1)
     west = pltpu.roll(center, 1, 1)
-    advect = c[0] * (upper - lower) + c[1] * (east - west)
-    laplace = upper + lower + east + west - 4.0 * center
-    return center - 0.5 * advect + c[2] * laplace
-
-
-def forecast_kernel(first, odd_ref, own_ref, beside_ref, beyond_ref, coef_ref, cprev_ref, cnext_ref, field_ref):
+    return w[0] * center + w[1] * upper + w[2] * lower + w[3] * east + w[4] * west
+
+
+def weights(c):
+    across, along = 0.5 * c[0], 0.5 * c[1]
+    return [1.0 - 4.0 * c[2], c[2] - across, c[2] + across, c[2] - along, c[2] + along]
+
+
+def forecast_kernel(first, odd_ref, own_ref, beside_ref, beyond_ref, coef_ref, cprev_ref, cnext_ref, field_ref, weight_ref):
     levels, width = field_ref.shape[0], own_ref.shape[2]
     odd = odd_ref[0] == 1
     share = cprev_ref.shape[2]
+    for block in range(first // share, (first + levels - 1) // share + 1):
+        low, high = max(block * share, first), min(block * share + share, first + levels)
+        inner = slice(low - block * share, high - block * share)
+        for row in range(4):
+            if row in (1, 2):
+                c = [coef_ref[k, row - 1, low:high, :] for k in range(3)]
+            else:
+                side_ref = cprev_ref if row == 0 else cnext_ref
+                c = [side_ref[block, k, inner, :] for k in range(3)]
+            for i, w in enumerate(weights(c)):
+                weight_ref[row * 5 + i, low - first : high - first, :] = w
 
     def level(z, carry):
         beside = [beside_ref[2 * z + r].astype(F32) for r in range(2)]
@@ -43,16 +57,11 @@
         rows = [jnp.where(odd, beside[r], beyond[r]) for r in range(2)]
         rows += [own_ref[2 * z + r].astype(F32) for r in range(2)]
         rows += [jnp.where(odd, beyond[r], beside[r]) for r in range(2)]
-        at = pl.ds(first + z, 1)
-        coeffs = [
-            [cprev_ref[(first + z) // share, k, pl.ds((first + z) % share, 1), :] for k in range(3)],
-            [coef_ref[k, 0, at, :] for k in range(3)],
-            [coef_ref[k, 1, at, :] for k in range(3)],
-            [cnext_ref[(first + z) // share, k, pl.ds((first + z) % share, 1), :] for k in range(3)],
-        ]
-        once = [advance(rows[i + 2], rows[i], rows[i + 1], coeffs[i]) for i in range(4)]
+        at = pl.ds(z, 1)
+        w = [[weight_ref[row * 5 + i, at, :] for i in range(5)] for row in range(4)]
+        once = [advance(rows[i + 2], rows[i], rows[i + 1], w[i]) for i in range(4)]
         for r in range(2):
-            twice = advance(once[r + 2], once[r], once[r + 1], coeffs[r + 1]).astype(BF16)
+            twice = advance(once[r + 2], once[r], once[r + 1], w[r + 1]).astype(BF16)
             for t in range(width // LANES):
                 field_ref[z, r, t] = twice[:, t * LANES : (t + 1) * LANES]
         return carry
@@ -68,6 +77,7 @@
         out_shape=jax.ShapeDtypeStruct((levels, rows, width // LANES, members, LANES), BF16),
         in_specs=[SMEM] + [VMEM] * 6,
         out_specs=VMEM,
+        scratch_shapes=[pltpu.VMEM((20, levels, width), F32)],
         compiler_params=params(32),
         name="forecast",
     )(odd, own, beside, beyond, coef, cprev, cnext)
@@ -186,7 +196,7 @@
     scale_ref[q // 2, :, sl] = jnp.broadcast_to(inv, (8, 128))
 
 
-def solve_stage(u, stage, held, work, consts, out_ref, first, members):
+def solve_stage(u, stage, held, work, consts, out_ref, diag_ref, first, members):
     state_ref, factor_ref = held
     sq_ref, force_ref, scale_ref = work
     ident, _, low, _ = consts
@@ -214,7 +224,10 @@
         shift = mul(state_ref[u, 64:].astype(BF16), block_diag(factor_ref[u], low))
         yield
         scale = scale_ref[u, :1]
-        out_ref[first + u] = (math.sqrt(members - 1.0) * jnp.sqrt(scale)) * state_ref[u, 64:] + scale * shift
+        transform = (math.sqrt(members - 1.0) * jnp.sqrt(scale)) * state_ref[u, 64:] + scale * shift
+        on = transform * ident
+        out_ref[first + u] = (transform - on).astype(BF16)
+        diag_ref[first + u] = jnp.broadcast_to(jnp.sum(on, axis=0, keepdims=True), (8, 256))
 
 
 def run(steps, filler, share):
@@ -237,7 +250,7 @@
         pass
 
 
-def transform_kernel(slot_ref, ens_ref, obs_ref, wgt_ref, lists_ref, out_ref, cat_ref, rows_ref, *scratch):
+def transform_kernel(slot_ref, ens_ref, obs_ref, wgt_ref, lists_ref, out_ref, diag_ref, cat_ref, rows_ref, *scratch):
     work, (lists_a, lists_b, sems), held = (scratch[:3], scratch[3:6]), scratch[6:9], scratch[9:]
     smem = (lists_a, lists_b)
     groups = slot_ref.shape[0]
@@ -273,7 +286,7 @@
 
     def solve(stage, block, half):
         at = jnp.maximum(block, 0) * GROUPS
-        return [solve_stage(u, stage, held, work[half], consts, out_ref, at, members) for u in range(GROUPS)]
+        return [solve_stage(u, stage, held, work[half], consts, out_ref, diag_ref, at, members) for u in range(GROUPS)]
 
     def gram(q, block, half):
         return gram_pair(q, rows_ref, wgt_ref, jnp.maximum(block, 0) * pairs, work[half], consts)
@@ -326,9 +339,12 @@
     ]
     return pl.pallas_call(
         transform_kernel,
-        out_shape=jax.ShapeDtypeStruct((pairs, 64, 256), F32),
+        out_shape=[
+            jax.ShapeDtypeStruct((pairs, 64, 256), BF16),
+            jax.ShapeDtypeStruct((pairs, 8, 256), F32),
+        ],
         in_specs=[SMEM] + [VMEM] * 4,
-        out_specs=VMEM,
+        out_specs=[VMEM] * 2,
         scratch_shapes=[
             pltpu.VMEM((windows * blocks * LANES, LANES), F32),
             pltpu.VMEM((2 * WIDE, 2, LANES, LANES), F32),
@@ -345,7 +361,7 @@
     )(slots, ens, obs, wgt, lists)
 
 
-def update_kernel(state_ref, transform_ref, out_ref, cells_ref, moved_ref, center_ref):
+def update_kernel(state_ref, transform_ref, diag_ref, out_ref, cells_ref, moved_ref, center_ref):
     groups, levels, _, tiles, per, _ = state_ref.shape
     width = tiles * LANES
     members = groups * per
@@ -364,7 +380,6 @@
 
     lax.fori_loop(0, levels, enter, 0, unroll=4)
 
-    ident = eye4()
     lane = lax.broadcasted_iota(jnp.int32, (64, 128), 1)
     low = jnp.where(lane < 64, 1.0, 0.0).astype(BF16)
 
@@ -374,10 +389,7 @@
             q = g * 2 + half
             halves.append(jnp.concatenate([cells_ref[pl.ds(2 * q + c, levels, stride=width), :] for c in range(2)], 0))
         x = jnp.concatenate(halves, 1)
-        t = transform_ref[g]
-        on = t * ident
-        diag = jnp.sum(on, axis=0, keepdims=True)
-        y = x * diag + mul(x.astype(BF16), block_diag((t - on).astype(BF16), low))
+        y = x * diag_ref[g, :1] + mul(x.astype(BF16), block_diag(transform_ref[g], low))
         for half in range(2):
             q = g * 2 + half
             for c in range(2):
@@ -395,13 +407,13 @@
     lax.fori_loop(0, levels, leave, 0, unroll=4)
 
 
-def update(state, transform):
+def update(state, transform, diag):
     groups, levels, rows, tiles, per, _ = state.shape
     width = tiles * LANES
     return pl.pallas_call(
         update_kernel,
         out_shape=jax.ShapeDtypeStruct((levels, rows, groups * per, width), BF16),
-        in_specs=[VMEM, VMEM],
+        in_specs=[VMEM] * 3,
         out_specs=VMEM,
         scratch_shapes=[
             pltpu.VMEM((levels * width, LANES), F32),
@@ -410,7 +422,7 @@
         ],
         compiler_params=params(24),
         name="update",
-    )(state, transform)
+    )(state, transform, diag)
 
 
 def cuts(levels):
@@ -488,19 +500,18 @@
     ens = window[None]
     distance = groups // 2
     while distance:
-        ens = jnp.concatenate([ens, lax.ppermute(ens, "mem", [(i, i ^ distance) for i in range(groups)])], 0)
-        if distance == groups // 2:
-            ens, ship = lax.optimization_barrier((ens, ship))
+        arrived = lax.ppermute(ens, "mem", [(i, i ^ distance) for i in range(groups)])
+        arrived, ship = lax.optimization_barrier((arrived, ship))
+        ens = jnp.concatenate([ens, arrived], 0)
         distance //= 2
     slots = bit_reversed(jnp.arange(groups, dtype=jnp.int32) ^ me, bits)
 
     position = lax.broadcasted_iota(jnp.int32, loc_weight.shape, 2)
     wgt = jnp.where(position < counts[..., None], loc_weight, 0.0)
-    transform = transforms(slots, lists, ens, obs, wgt)
-
-    ship, _ = lax.optimization_barrier((ship, ens))
+    transform, diag = transforms(slots, lists, ens, obs, wgt)
+
     state = lax.all_to_all(ship, "mem", 0, 0, tiled=False)
-    result = update(state, transform)
+    result = update(state, transform, diag)
     return jnp.transpose(result, (2, 0, 1, 3))
 
 

time: 172 us -> 171 us (level); the launches traced: 170 us -> 170 us
  waiting for transfers between devices: 21.7 us -> 26.8 us
  local copies, waits for them, and re-layouts: 26.9 us -> 23 us
    ppermute x1, waiting for transfers between devices: 1.31 us -> 4.89 us  [on_device(): lax.ppermute(sent, 'slab', down)]
    ppermute x1, starting transfers between devices: 1.92 us -> 4.26 us  [on_device(): lax.ppermute(sent, 'slab', down)]
    slice x7, local copies, waits for them, and re-layouts: 9.83 us -> 7.7 us  [on_device(): own[first:last].reshape(-1, members, columns)]
    ppermute x2, waiting for transfers between devices: 7.67 us -> 9.59 us  [on_device(): lax.ppermute(ens, 'mem', [(i, i ^ distance) for i in range(groups)])]
    ppermute x1, waiting for transfers between devices: 3.2 us -> 1.31 us  [on_device(): lax.ppermute(sent, 'slab', up)]
    ppermute x2, starting transfers between devices: 3.5 us -> 1.72 us  [on_device(): lax.ppermute(ens, 'mem', [(i, i ^ distance) for i in range(groups)])]
    unnamed x45 -> x40, local copies, waits for them, and re-layouts: 11.2 us -> 9.65 us
where the time goes in v6:
time: 171 us; the launch traced here: 170 us
  Pallas kernels  70.2 us (41%)
  starting transfers between devices  35.2 us (21%)
  waiting for transfers between devices  26.8 us (16%)
  local copies, waits for them, and re-layouts  23 us (13%)
  blocking collectives  12 us (7%)
  other arithmetic  2.59 us (2%)
    pallas_call x1, Pallas kernels, transforms(): pl.pallas_call(transform_kernel, out_shape=[jax.ShapeDtypeStruct((pairs,...  40.7 us
    pallas_call x5, Pallas kernels, forecast(): pl.pallas_call(functools.partial(forecast_kernel, first), out_shape=jax.S...  13.9 us
    all_gather x1, blocking collectives, on_device(): sides = lax.all_gather(jnp.stack([near, far]), 'mem', axis=0, tiled=False)  12 us
    unnamed x40, local copies, waits for them, and re-layouts  9.65 us
    ppermute x3, starting transfers between devices, on_device(): beyonds.append(lax.ppermute(besides[i - 2], 'slab', skip))  9.6 us
    ppermute x2, waiting for transfers between devices, on_device(): lax.ppermute(ens, 'mem', [(i, i ^ distance) for i in range(groups)])  9.59 us
    pallas_call x1, Pallas kernels, update(): pl.pallas_call(update_kernel, out_shape=jax.ShapeDtypeStruct((levels, row...  8.92 us
    slice x7, local copies, waits for them, and re-layouts, on_device(): own[first:last].reshape(-1, members, columns)  7.7 us
  transfers between devices with their start and end apart: 17, of which 9 were waited for; matrix products, arithmetic and copies ran while one was open for 8% of the time, Pallas kernels for 31%

profile of v6, /device:TPU:9, one launch (start us, length us, event | category | flops | bytes accessed | tf_op | source)
XLA Modules:
  0.0 170.4 jit_solution(355023784644072928)
XLA Ops:
  2.7 2.2 %fusion.19 = (bf16[4,2,16,1024]{3,1,0,2:T(2,128)(2,1)}, bf16[4,2,16,1024]{3,1,0,2:T(2,128)(2,1)S(1)}) fusion(bf16[32,2,16,1024]{3,1,0,2:T(2,128)(2,1)} %bitcast.112), kind=kLoop, calls=%fused_computation.60 | loop fusion | bytes 1048576 | tf_op jit(solution)/shard_map/slice | solution.py:455
  5.3 2.7 %fusion.18 = (bf16[8,2,16,1024]{3,1,0,2:T(2,128)(2,1)S(1)}, bf16[8,2,16,1024]{3,1,0,2:T(2,128)(2,1)S(1)}, bf16[8,2,16,1024]{3,1,0,2:T(2,128)(2,1)S(1)}) fusion(bf16[32,2,16,1024]{3,1,0,2:T(2,128)(2,1)} %bitcast.113), kind=kLoop, calls=%fused_computation.59 | loop fusion | bytes 3145728 | tf_op jit(solution)/shard_map/slice | solution.py:455
  9.7 3.2 %collective-permute-start.3 = (bf16[3,2,8,1024]{3,2,1,0:T(8,128)(2,1)S(1)}, bf16[3,2,8,1024]{3,2,1,0:T(8,128)(2,1)}, u32[]{:S(2)}, u32[]{:S(2)}) collective-permute-start(bf16[3,2,8,1024]{3,2,1,0:T(8,128)(2,1)S(1)} %collective-permute-done.2), channel_id=1, source_target_pairs={{0,2},{2,4},{4,6},{3,1},{5,3},{7,5},{8,10},{10,12},{12,14},{11,9},... | collective-permute-start | bytes 294920 | tf_op jit(solution)/shard_map/ppermute | solution.py:460
  12.9 3.2 %collective-permute-start.1 = (bf16[8,16,1024]{2,1,0:T(8,128)(2,1)S(1)}, bf16[8,16,1024]{2,1,0:T(8,128)(2,1)S(1)}, u32[]{:S(2)}, u32[]{:S(2)}) collective-permute-start(bf16[8,16,1024]{2,1,0:T(8,128)(2,1)S(1)} %collective-permute-done.beside_ref), channel_id=1, source_target_pairs={{0,2},{2,4},{4,6},{3,1},{5,3},{7,5},{8,10},{10,12},{12,14},{11,9},... | collective-permute-start | bytes 786440 | tf_op jit(solution)/shard_map/ppermute | solution.py:480
  23.3 3.2 %collective-permute-start.5 = (bf16[16,16,1024]{2,1,0:T(8,128)(2,1)}, bf16[16,16,1024]{2,1,0:T(8,128)(2,1)S(1)}, u32[]{:S(2)}, u32[]{:S(2)}) collective-permute-start(bf16[16,16,1024]{2,1,0:T(8,128)(2,1)} %collective-permute-done.4.beside_ref), channel_id=1, source_target_pairs={{0,2},{2,4},{4,6},{3,1},{5,3},{7,5},{8,10},{10,12},{12,14},{11,9},... | collective-permute-start | bytes 1572872 | tf_op jit(solution)/shard_map/ppermute | solution.py:480
  26.5 12.0 %all-gather = bf16[8,3,2,8,1024]{4,3,2,1,0:T(8,128)(2,1)S(1)} all-gather(bf16[2,3,2,8,1024]{4,3,2,1,0:T(8,128)(2,1)S(1)} %pad_maximum_fusion.3), channel_id=2, replica_groups=mesh['mem'=4,'slab'=8] {'mem'}, dimensions={0}, use_global_device_ids=true | all-gather | bytes 983040 | tf_op jit(solution)/shard_map/all_gather | solution.py:461
  40.7 3.2 %collective-permute-start.7 = (bf16[16,16,1024]{2,1,0:T(8,128)(2,1)}, bf16[16,16,1024]{2,1,0:T(8,128)(2,1)}, u32[]{:S(2)}, u32[]{:S(2)}) collective-permute-start(bf16[16,16,1024]{2,1,0:T(8,128)(2,1)} %collective-permute-done.6.beside_ref), channel_id=1, source_target_pairs={{0,2},{2,4},{4,6},{3,1},{5,3},{7,5},{8,10},{10,12},{12,14},{11,9},... | collective-permute-start | bytes 1572872 | tf_op jit(solution)/shard_map/ppermute | solution.py:480
  45.8 3.2 %collective-permute-start.9 = (bf16[16,16,1024]{2,1,0:T(8,128)(2,1)}, bf16[16,16,1024]{2,1,0:T(8,128)(2,1)}, u32[]{:S(2)}, u32[]{:S(2)}) collective-permute-start(bf16[16,16,1024]{2,1,0:T(8,128)(2,1)} %collective-permute-done.8.beside_ref), channel_id=1, source_target_pairs={{0,2},{2,4},{4,6},{3,1},{5,3},{7,5},{8,10},{10,12},{12,14},{11,9},... | collective-permute-start | bytes 1572872 | tf_op jit(solution)/shard_map/ppermute | solution.py:481
  49.1 3.4 %collective-permute-done.10.beside_ref = bf16[8,16,1024]{2,1,0:T(8,128)(2,1)} collective-permute-done((bf16[8,16,1024]{2,1,0:T(8,128)(2,1)}, bf16[8,16,1024]{2,1,0:T(8,128)(2,1)}, u32[]{:S(2)}, u32[]{:S(2)}) %collective-permute-start.10) | collective-permute-done | bytes 262176 | tf_op jit(solution)/shard_map/ppermute | solution.py:478
  52.5 2.9 %collective-permute-start.11 = (bf16[8,16,1024]{2,1,0:T(8,128)(2,1)}, bf16[8,16,1024]{2,1,0:T(8,128)(2,1)S(1)}, u32[]{:S(2)}, u32[]{:S(2)}) collective-permute-start(bf16[8,16,1024]{2,1,0:T(8,128)(2,1)} %collective-permute-done.10.beside_ref), channel_id=1, source_target_pairs={{0,2},{2,4},{4,6},{3,1},{5,3},{7,5},{8,10},{10,12},{12,14},{11,9},... | collective-permute-start | bytes 786440 | tf_op jit(solution)/shard_map/ppermute | solution.py:481
  56.5 3.5 %forecast.6 = bf16[8,2,8,16,128]{4,3,2,1,0:T(8,128)(2,1)S(1)} custom-call(s32[1]{0:T(128)} %bitcast.3.odd_ref, bf16[16,16,1024]{2,1,0:T(8,128)(2,1)S(1)} %bitcast.100, bf16[16,16,1024]{2,1,0:T(8,128)(2,1)} %collective-permute-done.4.beside_ref, bf16[16,16,1024]{2,1,0:T(8,128)(2,1)S(1)} %copy-done.5, f32[3,2,32,1024]{3,2,1,0:T(8,128)S(1)} %bitcast.89, ...), custom_call_target="tpu_custom_call" | custom-call | tf_op jit(solution)/shard_map/forecast/pallas_call | solution.py:75
  60.0 3.6 %forecast.7 = bf16[8,2,8,16,128]{4,3,2,1,0:T(8,128)(2,1)S(1)} custom-call(s32[1]{0:T(128)} %bitcast.3.odd_ref, bf16[16,16,1024]{2,1,0:T(8,128)(2,1)S(1)} %bitcast.104, bf16[16,16,1024]{2,1,0:T(8,128)(2,1)} %collective-permute-done.6.beside_ref, bf16[16,16,1024]{2,1,0:T(8,128)(2,1)} %collective-permute-done.7.beyond_ref, f32[3,2,32,1024]{3,2,1,0:T(8,128)S(1)} %bitcast.90, ...), custom_call_target="tpu_custom_call" | custom-call | tf_op jit(solution)/shard_map/forecast/pallas_call | solution.py:75
  63.6 3.9 %collective-permute-done.9.beyond_ref = bf16[16,16,1024]{2,1,0:T(8,128)(2,1)} collective-permute-done((bf16[16,16,1024]{2,1,0:T(8,128)(2,1)}, bf16[16,16,1024]{2,1,0:T(8,128)(2,1)}, u32[]{:S(2)}, u32[]{:S(2)}) %collective-permute-start.9) | collective-permute-done | bytes 524320 | tf_op jit(solution)/shard_map/ppermute | solution.py:481
  67.5 3.6 %forecast.8 = bf16[8,2,8,16,128]{4,3,2,1,0:T(8,128)(2,1)S(1)} custom-call(s32[1]{0:T(128)} %bitcast.3.odd_ref, bf16[16,16,1024]{2,1,0:T(8,128)(2,1)S(1)} %bitcast.102, bf16[16,16,1024]{2,1,0:T(8,128)(2,1)} %collective-permute-done.8.beside_ref, bf16[16,16,1024]{2,1,0:T(8,128)(2,1)} %collective-permute-done.9.beyond_ref, f32[3,2,32,1024]{3,2,1,0:T(8,128)S(1)} %bitcast.91, ...), custom_call_target="tpu_custom_call" | custom-call | tf_op jit(solution)/shard_map/forecast/pallas_call | solution.py:75
  73.0 2.1 %forecast.9 = bf16[4,2,8,16,128]{4,3,2,1,0:T(8,128)(2,1)S(1)} custom-call(s32[1]{0:T(128)} %bitcast.3.odd_ref, bf16[8,16,1024]{2,1,0:T(8,128)(2,1)} %bitcast.15.own_ref, bf16[8,16,1024]{2,1,0:T(8,128)(2,1)} %collective-permute-done.10.beside_ref, bf16[8,16,1024]{2,1,0:T(8,128)(2,1)S(1)} %collective-permute-done.11.beyond_ref, ...), custom_call_target="tpu_custom_call" | custom-call | tf_op jit(solution)/shard_map/forecast/pallas_call | solution.py:75
  75.1 6.7 %observe.1 = bf16[32,16,128]{2,1,0:T(8,128)(2,1)S(1)} custom-call(s32[8,8,128]{2,1,0:T(8,128)S(1)} %bitcast.108, bf16[64,16,128]{2,1,0:T(8,128)(2,1)S(1)} %bitcast.97, bf16[128,16,128]{2,1,0:T(8,128)(2,1)S(1)} %bitcast.94, bf16[128,16,128]{2,1,0:T(8,128)(2,1)S(1)} %bitcast.95, bf16[128,16,128]{2,1,0:T(8,128)(2,1)S(1)} %bitcast.96, ...), custom_call_target="tpu_custom_call" | custom-call | tf_op jit(solution)/shard_map/observe/pallas_call | solution.py:130
  83.8 4.3 %collective-permute-start.13 = (bf16[40,16,128]{2,1,0:T(8,128)(2,1)S(1)}, bf16[40,16,128]{2,1,0:T(8,128)(2,1)S(1)}, u32[]{:S(2)}, u32[]{:S(2)}) collective-permute-start(bf16[40,16,128]{2,1,0:T(8,128)(2,1)S(1)} %get-tuple-element.37), channel_id=1, source_target_pairs={{1,0},{2,1},{3,2},{4,3},{5,4},{6,5},{7,6},{9,8},{10,9},{11,10},{12... | collective-permute-start | bytes 491528 | tf_op jit(solution)/shard_map/ppermute | solution.py:493
  89.4 4.9 %collective-permute-done.13 = bf16[40,16,128]{2,1,0:T(8,128)(2,1)S(1)} collective-permute-done((bf16[40,16,128]{2,1,0:T(8,128)(2,1)S(1)}, bf16[40,16,128]{2,1,0:T(8,128)(2,1)S(1)}, u32[]{:S(2)}, u32[]{:S(2)}) %collective-permute-start.13) | collective-permute-done | bytes 163872 | tf_op jit(solution)/shard_map/ppermute | solution.py:493
  95.0 2.0 %copy.57 = bf16[32,2,4,2,16,128]{5,4,3,1,0,2:T(8,128)(2,1)} copy(bf16[32,2,4,2,16,128]{5,4,3,2,1,0:T(8,128)(2,1)S(1)} %bitcast.111) | data formatting | bytes 4194304 | tf_op jit(solution)/shard_map/reshape | solution.py:499
  96.9 7.7 %collective-permute-done.14 = bf16[1,3,32,16,128]{4,3,2,1,0:T(8,128)(2,1)S(1)} collective-permute-done((bf16[1,3,32,16,128]{4,3,2,1,0:T(8,128)(2,1)S(1)}, bf16[1,3,32,16,128]{4,3,2,1,0:T(8,128)(2,1)S(1)}, u32[]{:S(2)}, u32[]{:S(2)}) %collective-permute-start.14) | collective-permute-done | bytes 393248 | tf_op jit(solution)/shard_map/ppermute | solution.py:503
  108.9 4.0 %all-to-all-start = ((bf16[4,32,2,2,16,128]{5,4,3,2,1,0:T(8,128)(2,1)}), bf16[4,32,2,2,16,128]{5,4,3,2,1,0:T(8,128)(2,1)S(1)}, u32[]{:S(2)}, u32[]{:S(2)}) async-start(bf16[4,32,2,2,16,128]{5,4,3,2,1,0:T(8,128)(2,1)} %bitcast.109), calls=%async_computation | async-start | bytes 4194304 | tf_op jit(solution)/shard_map/all_to_all | solution.py:513
  114.3 40.7 %transforms.1 = (bf16[64,64,256]{2,1,0:T(8,128)(2,1)S(1)}, f32[64,8,256]{2,1,0:T(8,128)S(1)}) custom-call(s32[4]{0:T(128)S(1)} %shift-left_add_fusion.slot_ref, bf16[4,3,32,16,128]{4,3,2,1,0:T(8,128)(2,1)S(1)} %pad_maximum_fusion.ens_ref, f32[3,2,32,128]{3,2,1,0:T(8,128)S(1)} %fusion.9.obs_ref, f32[2,128,128]{2,1,0:T(8,128)S(1)} %fusion.6.wgt_ref, ...), custom_call_target="tpu_custom_call" | custom-call | tf_op jit(solution)/shard_map/transforms/pallas_call | solution.py:340
  158.0 8.9 %update.1 = bf16[32,2,64,256]{3,2,1,0:T(8,128)(2,1)S(1)} custom-call(bf16[4,32,2,2,16,128]{5,4,3,2,1,0:T(8,128)(2,1)S(1)} %all-to-all-done.state_ref, bf16[64,64,256]{2,1,0:T(8,128)(2,1)S(1)} %copy-done.1, f32[64,8,256]{2,1,0:T(8,128)S(1)} %get-tuple-element.28.diag_ref), custom_call_target="tpu_custom_call" | custom-call | tf_op jit(solution)/shard_map/update/pallas_call | solution.py:413
  166.9 3.5 %copy.48 = bf16[64,32,2,256]{3,2,1,0:T(2,128)(2,1)} copy(bf16[64,32,2,256]{3,0,2,1:T(8,128)(2,1)S(1)} %bitcast.93) | data formatting | bytes 4194304 | tf_op jit(solution)/shard_map/transpose | solution.py:515
  (89 shorter events, 31.4 us)
Async XLA Ops:
  1.4 8.3 %collective-permute-start.2 = (bf16[3,2,8,1024]{3,2,1,0:T(8,128)(2,1)S(1)}, bf16[3,2,8,1024]{3,2,1,0:T(8,128)(2,1)S(1)}, u32[]{:S(2)}, u32[]{:S(2)}) collective-permute-start(bf16[3,2,8,1024]{3,2,1,0:T(8,128)(2,1)S(1)} %fusion.7), channel_id=1, source_target_pairs={{0,1},{1,0},{2,3},{3,2},{4,5},{5,4},{6,7},{7,6},{8,9},{9,8},{10,11... | collective-permute-start | bytes 294920 | tf_op jit(solution)/shard_map/ppermute | solution.py:459
  5.1 7.9 %collective-permute-start = (bf16[8,16,1024]{2,1,0:T(8,128)(2,1)S(1)}, bf16[8,16,1024]{2,1,0:T(8,128)(2,1)S(1)}, u32[]{:S(2)}, u32[]{:S(2)}) collective-permute-start(bf16[8,16,1024]{2,1,0:T(8,128)(2,1)S(1)} %bitcast.105), channel_id=1, source_target_pairs={{0,1},{1,0},{2,3},{3,2},{4,5},{5,4},{6,7},{7,6},{8,9},{9,8},{10,11... | collective-permute-start | bytes 786440 | tf_op jit(solution)/shard_map/ppermute | solution.py:478
  8.3 15.0 %collective-permute-start.4 = (bf16[16,16,1024]{2,1,0:T(8,128)(2,1)S(1)}, bf16[16,16,1024]{2,1,0:T(8,128)(2,1)}, u32[]{:S(2)}, u32[]{:S(2)}) collective-permute-start(bf16[16,16,1024]{2,1,0:T(8,128)(2,1)S(1)} %bitcast.99), channel_id=1, source_target_pairs={{0,1},{1,0},{2,3},{3,2},{4,5},{5,4},{6,7},{7,6},{8,9},{9,8},{10,11... | collective-permute-start | bytes 1572872 | tf_op jit(solution)/shard_map/ppermute | solution.py:478
  9.7 10.3 %collective-permute-start.3 = (bf16[3,2,8,1024]{3,2,1,0:T(8,128)(2,1)S(1)}, bf16[3,2,8,1024]{3,2,1,0:T(8,128)(2,1)}, u32[]{:S(2)}, u32[]{:S(2)}) collective-permute-start(bf16[3,2,8,1024]{3,2,1,0:T(8,128)(2,1)S(1)} %collective-permute-done.2), channel_id=1, source_target_pairs={{0,2},{2,4},{4,6},{3,1},{5,3},{7,5},{8,10},{10,12},{12,14},{11,9},... | collective-permute-start | bytes 294920 | tf_op jit(solution)/shard_map/ppermute | solution.py:460
  12.9 7.1 %copy-start.6 = (bf16[8,16,1024]{2,1,0:T(8,128)(2,1)}, bf16[8,16,1024]{2,1,0:T(8,128)(2,1)S(1)}, u32[]{:S(2)}) copy-start(bf16[8,16,1024]{2,1,0:T(8,128)(2,1)S(1)} %collective-permute-done.beside_ref) | copy-start | bytes 786436
  12.9 8.1 %collective-permute-start.1 = (bf16[8,16,1024]{2,1,0:T(8,128)(2,1)S(1)}, bf16[8,16,1024]{2,1,0:T(8,128)(2,1)S(1)}, u32[]{:S(2)}, u32[]{:S(2)}) collective-permute-start(bf16[8,16,1024]{2,1,0:T(8,128)(2,1)S(1)} %collective-permute-done.beside_ref), channel_id=1, source_target_pairs={{0,2},{2,4},{4,6},{3,1},{5,3},{7,5},{8,10},{10,12},{12,14},{11,9},... | collective-permute-start | bytes 786440 | tf_op jit(solution)/shard_map/ppermute | solution.py:480
  19.7 18.9 %copy-start.3 = (bf16[4,2,16,1024]{3,2,1,0:T(8,128)(2,1)S(1)}, bf16[4,2,16,1024]{3,2,1,0:T(8,128)(2,1)}, u32[]{:S(2)}) copy-start(bf16[4,2,16,1024]{3,2,1,0:T(8,128)(2,1)} %copy-done.2) | copy-start | bytes 786436
  20.0 18.6 %copy-start.7 = (bf16[8,16,1024]{2,1,0:T(8,128)(2,1)S(1)}, bf16[8,16,1024]{2,1,0:T(8,128)(2,1)}, u32[]{:S(2)}) copy-start(bf16[8,16,1024]{2,1,0:T(8,128)(2,1)} %copy-done.6) | copy-start | bytes 786436
  20.0 20.6 %collective-permute-start.6 = (bf16[16,16,1024]{2,1,0:T(8,128)(2,1)S(1)}, bf16[16,16,1024]{2,1,0:T(8,128)(2,1)}, u32[]{:S(2)}, u32[]{:S(2)}) collective-permute-start(bf16[16,16,1024]{2,1,0:T(8,128)(2,1)S(1)} %bitcast.103), channel_id=1, source_target_pairs={{0,1},{1,0},{2,3},{3,2},{4,5},{5,4},{6,7},{7,6},{8,9},{9,8},{10,11... | collective-permute-start | bytes 1572872 | tf_op jit(solution)/shard_map/ppermute | solution.py:478
  21.1 17.5 %copy-start.8 = (bf16[8,16,1024]{2,1,0:T(8,128)(2,1)}, bf16[8,16,1024]{2,1,0:T(8,128)(2,1)S(1)}, u32[]{:S(2)}) copy-start(bf16[8,16,1024]{2,1,0:T(8,128)(2,1)S(1)} %collective-permute-done.1.beyond_ref) | copy-start | bytes 786436
  21.1 24.7 %collective-permute-start.8 = (bf16[16,16,1024]{2,1,0:T(8,128)(2,1)S(1)}, bf16[16,16,1024]{2,1,0:T(8,128)(2,1)}, u32[]{:S(2)}, u32[]{:S(2)}) collective-permute-start(bf16[16,16,1024]{2,1,0:T(8,128)(2,1)S(1)} %bitcast.101), channel_id=1, source_target_pairs={{0,1},{1,0},{2,3},{3,2},{4,5},{5,4},{6,7},{7,6},{8,9},{9,8},{10,11... | collective-permute-start | bytes 1572872 | tf_op jit(solution)/shard_map/ppermute | solution.py:478
  23.3 20.6 %collective-permute-start.5 = (bf16[16,16,1024]{2,1,0:T(8,128)(2,1)}, bf16[16,16,1024]{2,1,0:T(8,128)(2,1)S(1)}, u32[]{:S(2)}, u32[]{:S(2)}) collective-permute-start(bf16[16,16,1024]{2,1,0:T(8,128)(2,1)} %collective-permute-done.4.beside_ref), channel_id=1, source_target_pairs={{0,2},{2,4},{4,6},{3,1},{5,3},{7,5},{8,10},{10,12},{12,14},{11,9},... | collective-permute-start | bytes 1572872 | tf_op jit(solution)/shard_map/ppermute | solution.py:480
  38.6 16.8 %copy-start.15 = (s32[4096]{0:T(1024)S(1)}, s32[4096]{0:T(1024)}, u32[]{:S(2)}) copy-start(s32[4096]{0:T(1024)} %param.12) | copy-start | bytes 49156
  40.7 19.3 %collective-permute-start.7 = (bf16[16,16,1024]{2,1,0:T(8,128)(2,1)}, bf16[16,16,1024]{2,1,0:T(8,128)(2,1)}, u32[]{:S(2)}, u32[]{:S(2)}) collective-permute-start(bf16[16,16,1024]{2,1,0:T(8,128)(2,1)} %collective-permute-done.6.beside_ref), channel_id=1, source_target_pairs={{0,2},{2,4},{4,6},{3,1},{5,3},{7,5},{8,10},{10,12},{12,14},{11,9},... | collective-permute-start | bytes 1572872 | tf_op jit(solution)/shard_map/ppermute | solution.py:480
  44.7 7.8 %collective-permute-start.10 = (bf16[8,16,1024]{2,1,0:T(8,128)(2,1)}, bf16[8,16,1024]{2,1,0:T(8,128)(2,1)}, u32[]{:S(2)}, u32[]{:S(2)}) collective-permute-start(bf16[8,16,1024]{2,1,0:T(8,128)(2,1)} %bitcast.15.own_ref), channel_id=1, source_target_pairs={{0,1},{1,0},{2,3},{3,2},{4,5},{5,4},{6,7},{7,6},{8,9},{9,8},{10,11... | collective-permute-start | bytes 786440 | tf_op jit(solution)/shard_map/ppermute | solution.py:478
  45.8 21.7 %collective-permute-start.9 = (bf16[16,16,1024]{2,1,0:T(8,128)(2,1)}, bf16[16,16,1024]{2,1,0:T(8,128)(2,1)}, u32[]{:S(2)}, u32[]{:S(2)}) collective-permute-start(bf16[16,16,1024]{2,1,0:T(8,128)(2,1)} %collective-permute-done.8.beside_ref), channel_id=1, source_target_pairs={{0,2},{2,4},{4,6},{3,1},{5,3},{7,5},{8,10},{10,12},{12,14},{11,9},... | collective-permute-start | bytes 1572872 | tf_op jit(solution)/shard_map/ppermute | solution.py:481
  52.5 20.6 %collective-permute-start.11 = (bf16[8,16,1024]{2,1,0:T(8,128)(2,1)}, bf16[8,16,1024]{2,1,0:T(8,128)(2,1)S(1)}, u32[]{:S(2)}, u32[]{:S(2)}) collective-permute-start(bf16[8,16,1024]{2,1,0:T(8,128)(2,1)} %collective-permute-done.10.beside_ref), channel_id=1, source_target_pairs={{0,2},{2,4},{4,6},{3,1},{5,3},{7,5},{8,10},{10,12},{12,14},{11,9},... | collective-permute-start | bytes 786440 | tf_op jit(solution)/shard_map/ppermute | solution.py:481
  81.8 7.5 %collective-permute-start.12 = (bf16[40,16,128]{2,1,0:T(8,128)(2,1)S(1)}, bf16[40,16,128]{2,1,0:T(8,128)(2,1)S(1)}, u32[]{:S(2)}, u32[]{:S(2)}) collective-permute-start(bf16[40,16,128]{2,1,0:T(8,128)(2,1)S(1)} %get-tuple-element.37), channel_id=1, source_target_pairs={{0,1},{1,2},{2,3},{3,4},{4,5},{5,6},{6,7},{8,9},{9,10},{10,11},{11... | collective-permute-start | bytes 491528 | tf_op jit(solution)/shard_map/ppermute | solution.py:493
  83.8 10.5 %collective-permute-start.13 = (bf16[40,16,128]{2,1,0:T(8,128)(2,1)S(1)}, bf16[40,16,128]{2,1,0:T(8,128)(2,1)S(1)}, u32[]{:S(2)}, u32[]{:S(2)}) collective-permute-start(bf16[40,16,128]{2,1,0:T(8,128)(2,1)S(1)} %get-tuple-element.37), channel_id=1, source_target_pairs={{1,0},{2,1},{3,2},{4,3},{5,4},{6,5},{7,6},{9,8},{10,9},{11,10},{12... | collective-permute-start | bytes 491528 | tf_op jit(solution)/shard_map/ppermute | solution.py:493
  94.4 10.3 %collective-permute-start.14 = (bf16[1,3,32,16,128]{4,3,2,1,0:T(8,128)(2,1)S(1)}, bf16[1,3,32,16,128]{4,3,2,1,0:T(8,128)(2,1)S(1)}, u32[]{:S(2)}, u32[]{:S(2)}) collective-permute-start(bf16[1,3,32,16,128]{4,3,2,1,0:T(8,128)(2,1)S(1)} %slice_bitcast_fusion), channel_id=1, source_target_pairs={{0,16},{8,24},{16,0},{24,8},{1,17},{9,25},{17,1},{25,9},{2,18},{10... | collective-permute-start | bytes 1179656 | tf_op jit(solution)/shard_map/ppermute | solution.py:503
  104.7 8.2 %copy-start.12 = (s32[2,128,128]{2,1,0:T(8,128)S(1)}, s32[2,128,128]{2,1,0:T(8,128)}, u32[]{:S(2)}) copy-start(s32[2,128,128]{2,1,0:T(8,128)} %param.13) | copy-start | bytes 393220
  104.7 8.3 %copy-start.16 = (s32[2,128]{1,0:T(2,128)S(1)}, s32[2,128]{1,0:T(2,128)}, u32[]{:S(2)}) copy-start(s32[2,128]{1,0:T(2,128)} %param.14) | copy-start | bytes 3076
  104.7 3.3 %collective-permute-start.15 = (bf16[2,3,32,16,128]{4,3,2,1,0:T(8,128)(2,1)S(1)}, bf16[2,3,32,16,128]{4,3,2,1,0:T(8,128)(2,1)S(1)}, u32[]{:S(2)}, u32[]{:S(2)}) collective-permute-start(bf16[2,3,32,16,128]{4,3,2,1,0:T(8,128)(2,1)S(1)} %pad_maximum_fusion.1), channel_id=1, source_target_pairs={{0,8},{8,0},{16,24},{24,16},{1,9},{9,1},{17,25},{25,17},{2,10},{10... | collective-permute-start | bytes 2359304 | tf_op jit(solution)/shard_map/ppermute | solution.py:503
  108.9 47.5 %all-to-all-start = ((bf16[4,32,2,2,16,128]{5,4,3,2,1,0:T(8,128)(2,1)}), bf16[4,32,2,2,16,128]{5,4,3,2,1,0:T(8,128)(2,1)S(1)}, u32[]{:S(2)}, u32[]{:S(2)}) async-start(bf16[4,32,2,2,16,128]{5,4,3,2,1,0:T(8,128)(2,1)} %bitcast.109), calls=%async_computation | async-start | bytes 4194304 | tf_op jit(solution)/shard_map/all_to_all | solution.py:513
  (10 other events, 20.5 us)
